TPU v7x, 32 devices: a whole 2x2x4 slice. The times are simulated.
32 devices in a mesh: dp: 8 (over y, x, core), tensor: 4 (over z).
Axes of the slice: x: 2, y: 2, z: 4, core: 2. Of those that a mesh axis runs over, the one named last changes fastest.
Arguments:
- tokens: bfloat16 [8192, 1024], P(('dp', 'tensor')), may hold values from -6 to 6
- query_proj: bfloat16 [1024, 512], P('dp', 'tensor'), may hold values from -0.1875 to 0.1875
- attend_out: bfloat16 [512, 1024], P('tensor', 'dp'), may hold values from -3 to 3
- inner_proj: bfloat16 [2, 1024, 1536], P(None, 'dp', 'tensor'), may hold values from -0.1875 to 0.1875
- step_proj: bfloat16 [1024, 24], P('dp', 'tensor'), may hold values from -0.1875 to 0.1875
- mamba_out: bfloat16 [1536, 1024], P('tensor', 'dp'), may hold values from -0.15625 to 0.15625
- hidden_proj: bfloat16 [2, 1024, 2048], P(None, 'dp', 'tensor'), may hold values from -0.1875 to 0.1875
- down_proj: bfloat16 [2048, 1024], P('tensor', 'dp'), may hold values from -0.125 to 0.125
- channel_taps: bfloat16 [5, 24, 64], P(None, 'tensor', 'dp'), may hold values from -3 to 3
- mixer_gain: bfloat16 [24, 64], P('tensor', 'dp'), may hold values from 0.25 to 1.75
- decay_log: bfloat16 [24], P('tensor'), may hold values from -4 to 0
- step_bias: bfloat16 [24], P('tensor'), may hold values from -6 to -2
- skip_weight: bfloat16 [24], P('tensor'), may hold values from 0.5 to 2
- shared_proj: bfloat16 [1024, 512], P(('dp', 'tensor')), may hold values from -0.1875 to 0.1875
- norm_gains: bfloat16 [2, 1024], P(None, ('dp', 'tensor')), may hold values from 0.25 to 1.75
- shared_taps: bfloat16 [5, 256], P(None, ('dp', 'tensor')), may hold values from -3 to 3
- cotangent: bfloat16 [8192, 1024], P(('dp', 'tensor')), may hold values from -6 to 6
Outputs:
- layer_out: bfloat16 [8192, 1024], P(('dp', 'tensor'))
- gradient_tokens: bfloat16 [8192, 1024], P(('dp', 'tensor'))
- gradient_query: float32 [1024, 512], P('dp', 'tensor')
- gradient_attend: float32 [512, 1024], P('tensor', 'dp')
- gradient_inner: float32 [2, 1024, 1536], P(None, 'dp', 'tensor')
- gradient_step: float32 [1024, 24], P('dp', 'tensor')
- gradient_mamba: float32 [1536, 1024], P('tensor', 'dp')
- gradient_hidden: float32 [2, 1024, 2048], P(None, 'dp', 'tensor')
- gradient_down: float32 [2048, 1024], P('tensor', 'dp')
- gradient_channel: float32 [5, 24, 64], P(None, 'tensor', 'dp')
- gradient_mixer: float32 [24, 64], P('tensor', 'dp')
- gradient_decay: float32 [24], P('tensor')
- gradient_bias: float32 [24], P('tensor')
- gradient_skip: float32 [24], P('tensor')
- gradient_shared: float32 [1024, 512], P(('dp', 'tensor'))
- gradient_norms: float32 [2, 1024], P(None, ('dp', 'tensor'))
- gradient_taps: float32 [5, 256], P(None, ('dp', 'tensor'))
All inputs are finite; a program needn't handle non-finite values.
Results may differ from a plain program's by a relative error of at most 0.024.
Values may be sent and summed in bfloat16 or wider, within the bound.
A program may use at most 192 MiB of HBM per device.

v0:
```python
from functools import partial

import jax
import jax.numpy as jnp
from jax import lax
from jax.sharding import PartitionSpec as P

QHEADS = 8
KVHEADS = 2
HEAD_SIZE = 64
SSM_DIM = 64
CONV = 4
SEQS_DEV = 1
INNER = 1536


epsilon = 1e-05
rope_base = 100000000000.0
highest_precision = lax.Precision.HIGHEST
neg_large = -1e30
block_len = 128


def norm_apply(values, gain):
    factor = lax.rsqrt(jnp.mean(values * values, axis=-1, keepdims=True) + epsilon)
    return values * factor * gain


def rope_tables(length, width):
    halfway = width // 2
    inverse = rope_base ** (-jnp.arange(halfway, dtype=jnp.float32) * (2.0 / width))
    angles = jnp.arange(length, dtype=jnp.float32)[:, None] * inverse[None, :]
    return (jnp.cos(angles), jnp.sin(angles))


def rotate(values, cosine, sine):
    halfway = values.shape[-1] // 2
    first = values[..., :halfway]
    second = values[..., halfway:]
    cos_wide = cosine[:, None, :]
    sin_wide = sine[:, None, :]
    return jnp.concatenate(
        [first * cos_wide - second * sin_wide, second * cos_wide + first * sin_wide], axis=-1
    )


def causal_conv(sequences, table):
    taps = table.shape[0] - 1
    length = sequences.shape[1]
    padded = jnp.pad(sequences, ((0, 0), (taps - 1, 0), (0, 0)))
    total = table[taps] + jnp.zeros_like(sequences)
    for offset in range(taps):
        total = total + table[offset] * padded[:, offset : offset + length]
    return total


def duality_scan(inputs, step_size, decay, in_mat, out_mat):
    length, num_heads, head_width = inputs.shape
    state_width = in_mat.shape[-1]
    window = min(block_len, length)
    blocks = length // window
    x_blocks = inputs.reshape(blocks, window, num_heads, head_width)
    s_blocks = step_size.reshape(blocks, window, num_heads)
    b_blocks = in_mat.reshape(blocks, window, state_width)
    c_blocks = out_mat.reshape(blocks, window, state_width)
    cumul = jnp.cumsum(s_blocks * decay, axis=1)
    lower_mask = jnp.arange(window)[:, None] >= jnp.arange(window)[None, :]
    gap_logs = cumul[:, :, None, :] - cumul[:, None, :, :]
    fading = jnp.exp(jnp.where(lower_mask[None, :, :, None], gap_logs, -jnp.inf))
    cross_terms = jnp.einsum("cin,cjn->cij", c_blocks, b_blocks, precision=highest_precision)
    mixing = cross_terms[..., None] * fading * s_blocks[:, None, :, :]
    within = jnp.einsum("cijh,cjhp->cihp", mixing, x_blocks, precision=highest_precision)
    ending = cumul[:, -1:, :]
    carried = x_blocks * (jnp.exp(ending - cumul) * s_blocks)[..., None]
    contrib = jnp.einsum("cjn,cjhp->chnp", b_blocks, carried, precision=highest_precision)
    block_fade = jnp.exp(ending[:, 0, :])

    def advance(carry, pieces):
        fade_now, added = pieces
        return (fade_now[:, None, None] * carry + added, carry)

    start = jnp.zeros((num_heads, state_width, head_width), inputs.dtype)
    finished, entering = lax.scan(advance, start, (block_fade, contrib))
    across = (
        jnp.einsum("cin,chnp->cihp", c_blocks, entering, precision=highest_precision)
        * jnp.exp(cumul)[..., None]
    )
    return (within + across).reshape(length, num_heads, head_width)


def mixer_local(
    gate_raw,
    signal_raw,
    step_raw,
    pair_raw,
    inner_taps,
    outer_taps,
    decay_log,
    step_bias,
    skip_weight,
    num_seq,
):
    total_rows = gate_raw.shape[0]
    seq_len = total_rows // num_seq
    num_heads = step_raw.shape[1]
    head_width = signal_raw.shape[1] // num_heads
    signal = jax.nn.silu(causal_conv(signal_raw.reshape(num_seq, seq_len, -1), inner_taps))
    paired = jax.nn.silu(causal_conv(pair_raw.reshape(num_seq, seq_len, -1), outer_taps))
    state_width = paired.shape[-1] // 2
    in_mat = paired[..., :state_width]
    out_mat = paired[..., state_width:]
    step_size = jax.nn.softplus(step_raw.reshape(num_seq, seq_len, num_heads) + step_bias)
    decay = -jnp.exp(decay_log)
    signal_heads = signal.reshape(num_seq, seq_len, num_heads, head_width)
    scanned = jax.vmap(duality_scan, in_axes=(0, 0, None, 0, 0))(
        signal_heads, step_size, decay, in_mat, out_mat
    )
    scanned = scanned + skip_weight[:, None] * signal_heads
    return scanned.reshape(total_rows, num_heads * head_width) * jax.nn.silu(gate_raw)


def causal_scores(query_low, key_low):
    length = query_low.shape[0]
    attention_scores = jnp.einsum(
        "lhd,md->hlm", query_low, key_low, preferred_element_type=jnp.float32
    ) * HEAD_SIZE ** (-0.5)
    causal = jnp.arange(length)[:, None] >= jnp.arange(length)[None, :]
    return jnp.where(causal[None], attention_scores, neg_large)


def attend_forward(pieces):
    query_low, key_low, value_low = pieces
    attention_scores = causal_scores(query_low, key_low)
    top_score = jnp.max(attention_scores, axis=-1, keepdims=True)
    expd = jnp.exp(attention_scores - top_score)
    total = jnp.sum(expd, axis=-1, keepdims=True)
    attention_probabilities = (expd / total).astype(jnp.bfloat16)
    result = jnp.einsum(
        "hlm,md->lhd", attention_probabilities, value_low, preferred_element_type=jnp.float32
    )
    return (result.astype(jnp.bfloat16), top_score[..., 0] + jnp.log(total[..., 0]))


def attend_backward(pieces):
    query_low, key_low, value_low, log_sums, grad_low = pieces
    attention_scores = causal_scores(query_low, key_low)
    attention_probabilities = jnp.exp(attention_scores - log_sums[..., None])
    probs_low = attention_probabilities.astype(jnp.bfloat16)
    grad_probs = jnp.einsum("lhd,md->hlm", grad_low, value_low, preferred_element_type=jnp.float32)
    centre = jnp.sum(attention_probabilities * grad_probs, axis=-1, keepdims=True)
    grad_scores = (attention_probabilities * (grad_probs - centre)).astype(jnp.bfloat16)
    query_back = jnp.einsum(
        "hlm,md->lhd", grad_scores, key_low, preferred_element_type=jnp.float32
    ) * HEAD_SIZE ** (-0.5)
    key_back = jnp.einsum(
        "hlm,lhd->md", grad_scores, query_low, preferred_element_type=jnp.float32
    ) * HEAD_SIZE ** (-0.5)
    value_back = jnp.einsum("hlm,lhd->md", probs_low, grad_low, preferred_element_type=jnp.float32)
    return (query_back, key_back, value_back)


def collect_rows(values):
    return lax.all_gather(values, "tensor", axis=0, tiled=True)


def spread_rows(values):
    return lax.psum_scatter(
        values.astype(jnp.bfloat16), "tensor", scatter_dimension=0, tiled=True
    ).astype(jnp.float32)


def ffn_collect(values):
    return lax.all_gather(values, "tensor", axis=0, tiled=True)


def ffn_spread(values):
    return lax.psum_scatter(
        values.astype(jnp.bfloat16), "tensor", scatter_dimension=0, tiled=True
    ).astype(jnp.float32)


def tensor_total(values):
    return lax.psum(values, "tensor")


def matmul(left, right):
    return jnp.dot(left, right, preferred_element_type=jnp.float32)


def left_contract(left, right):
    return jnp.einsum("md,mk->dk", left, right, preferred_element_type=jnp.float32)


def right_contract(left, right):
    return jnp.einsum("mk,dk->md", left, right, preferred_element_type=jnp.float32)


def per_device(
    tokens,
    query_proj,
    attend_out,
    inner_proj,
    step_proj,
    mamba_out,
    hidden_proj,
    down_proj,
    channel_taps,
    mixer_gain,
    decay_log,
    step_bias,
    skip_weight,
    shared_proj,
    norm_gains,
    shared_taps,
    cotangent,
):
    tensor_size = lax.axis_size("tensor")
    tensor_index = lax.axis_index("tensor")
    local_rows = tokens.shape[0]
    group_rows = local_rows * tensor_size
    seq_count = SEQS_DEV
    seq_len = group_rows // seq_count
    kv_cols = KVHEADS * HEAD_SIZE
    split_full = (
        lax.all_gather(query_proj, "dp", axis=0, tiled=True),
        lax.all_gather(attend_out, "dp", axis=1, tiled=True),
        lax.all_gather(inner_proj, "dp", axis=1, tiled=True),
        lax.all_gather(step_proj, "dp", axis=0, tiled=True),
        lax.all_gather(mamba_out, "dp", axis=1, tiled=True),
        lax.all_gather(hidden_proj, "dp", axis=1, tiled=True),
        lax.all_gather(down_proj, "dp", axis=1, tiled=True),
        lax.all_gather(channel_taps, "dp", axis=2, tiled=True),
        lax.all_gather(mixer_gain, "dp", axis=1, tiled=True),
    )
    shared_full = (
        lax.all_gather(shared_proj, ("dp", "tensor"), axis=0, tiled=True),
        lax.all_gather(norm_gains, ("dp", "tensor"), axis=1, tiled=True),
        lax.all_gather(shared_taps, ("dp", "tensor"), axis=1, tiled=True),
    )
    (
        full_query,
        full_attend,
        full_inner,
        full_step,
        full_mamba,
        full_hidden,
        full_down,
        full_taps,
        full_gain,
    ) = split_full
    full_shared, full_norms, full_stap = shared_full
    local_heads = full_step.shape[1]
    taps_inner = full_taps.astype(jnp.float32).reshape(CONV + 1, local_heads * SSM_DIM)
    taps_shared = full_stap.astype(jnp.float32)
    gain_mix = full_gain.astype(jnp.float32).reshape(local_heads * SSM_DIM)
    gain_first = full_norms[0].astype(jnp.float32)
    gain_second = full_norms[1].astype(jnp.float32)
    token_f32 = tokens.astype(jnp.float32)
    normed_one, norm_one_back = jax.vjp(norm_apply, token_f32, gain_first)
    local_one = normed_one.astype(jnp.bfloat16)
    group_one = collect_rows(local_one)
    query_raw = matmul(group_one, full_query)
    shared_raw = matmul(group_one, full_shared)
    gate_raw = matmul(group_one, full_inner[0])
    signal_raw = matmul(group_one, full_inner[1])
    step_raw = matmul(group_one, full_step)
    q_heads = query_raw.shape[1] // HEAD_SIZE
    kv_head = tensor_index * q_heads // (QHEADS // KVHEADS)
    cosine, sine = rope_tables(seq_len, HEAD_SIZE)
    query_rot = rotate(
        query_raw.reshape(seq_count, seq_len, q_heads, HEAD_SIZE), cosine, sine
    ).astype(jnp.bfloat16)
    key_raw = lax.dynamic_slice_in_dim(shared_raw, kv_head * HEAD_SIZE, HEAD_SIZE, 1)
    value_raw = lax.dynamic_slice_in_dim(shared_raw, kv_cols + kv_head * HEAD_SIZE, HEAD_SIZE, 1)
    key_rot = rotate(key_raw.reshape(seq_count, seq_len, 1, HEAD_SIZE), cosine, sine)[
        :, :, 0
    ].astype(jnp.bfloat16)
    value_low = value_raw.reshape(seq_count, seq_len, HEAD_SIZE).astype(jnp.bfloat16)
    attended, log_sums = lax.map(attend_forward, (query_rot, key_rot, value_low))
    attended_flat = attended.reshape(group_rows, q_heads * HEAD_SIZE)
    mix_part = matmul(attended_flat, full_attend)
    mixed_in, mixer_back = jax.vjp(
        partial(mixer_local, num_seq=seq_count),
        gate_raw,
        signal_raw,
        step_raw,
        shared_raw[:, 2 * kv_cols :],
        taps_inner,
        taps_shared,
        decay_log.astype(jnp.float32),
        step_bias.astype(jnp.float32),
        skip_weight.astype(jnp.float32),
    )
    square_sum = tensor_total(jnp.sum(mixed_in * mixed_in, axis=1))
    inv_rms = lax.rsqrt(square_sum / INNER + epsilon)[:, None]
    mamba_low = (mixed_in * inv_rms * gain_mix).astype(jnp.bfloat16)
    mix_part = mix_part + matmul(mamba_low, full_mamba)
    hidden = token_f32 + spread_rows(mix_part)
    normed_two, norm_two_back = jax.vjp(norm_apply, hidden, gain_second)
    local_two = normed_two.astype(jnp.bfloat16)
    ffn_rows = ffn_collect(local_two)
    gate_val = matmul(ffn_rows, full_hidden[0])
    up_val = matmul(ffn_rows, full_hidden[1])
    sigmoid_gate = jax.nn.sigmoid(gate_val)
    inner_low = (gate_val * sigmoid_gate * up_val).astype(jnp.bfloat16)
    down_term = matmul(inner_low, full_down)
    down_term = ffn_spread(down_term)
    hidden_out = hidden + down_term
    layer_out = hidden_out.astype(jnp.bfloat16)
    back_split = (
        lax.all_gather(query_proj, "dp", axis=0, tiled=True),
        lax.all_gather(attend_out, "dp", axis=1, tiled=True),
        lax.all_gather(inner_proj, "dp", axis=1, tiled=True),
        lax.all_gather(step_proj, "dp", axis=0, tiled=True),
        lax.all_gather(mamba_out, "dp", axis=1, tiled=True),
        lax.all_gather(hidden_proj, "dp", axis=1, tiled=True),
        lax.all_gather(down_proj, "dp", axis=1, tiled=True),
        lax.all_gather(channel_taps, "dp", axis=2, tiled=True),
        lax.all_gather(mixer_gain, "dp", axis=1, tiled=True),
    )
    back_common = (
        lax.all_gather(shared_proj, ("dp", "tensor"), axis=0, tiled=True),
        lax.all_gather(norm_gains, ("dp", "tensor"), axis=1, tiled=True),
        lax.all_gather(shared_taps, ("dp", "tensor"), axis=1, tiled=True),
    )
    (
        back_query,
        back_attend,
        back_inner,
        back_step,
        back_mamba,
        back_hidden,
        back_down,
        unused_taps,
        unused_gain,
    ) = back_split
    back_shared = back_common[0]
    grad_out = ffn_collect(cotangent)
    grad_down = left_contract(inner_low, grad_out)
    grad_inner_units = right_contract(grad_out, back_down)
    grad_up = (grad_inner_units * gate_val * sigmoid_gate).astype(jnp.bfloat16)
    grad_gate = (
        grad_inner_units * up_val * sigmoid_gate * (1.0 + gate_val * (1.0 - sigmoid_gate))
    ).astype(jnp.bfloat16)
    grad_hidden = jnp.stack([left_contract(ffn_rows, grad_gate), left_contract(ffn_rows, grad_up)])
    part_two = right_contract(grad_gate, back_hidden[0]) + right_contract(grad_up, back_hidden[1])
    grad_normed_two = ffn_spread(part_two)
    grad_from_two, grad_gain_two = norm_two_back(grad_normed_two)
    grad_resid = cotangent.astype(jnp.float32) + grad_from_two
    grad_mix = collect_rows(grad_resid.astype(jnp.bfloat16))
    grad_attend = left_contract(attended_flat, grad_mix)
    grad_attended = right_contract(grad_mix, back_attend).astype(jnp.bfloat16)
    grad_attended = grad_attended.reshape(seq_count, seq_len, q_heads, HEAD_SIZE)
    query_back, key_back, value_back = lax.map(
        attend_backward, (query_rot, key_rot, value_low, log_sums, grad_attended)
    )
    grad_query_raw = (
        rotate(query_back, cosine, -sine)
        .reshape(group_rows, q_heads * HEAD_SIZE)
        .astype(jnp.bfloat16)
    )
    grad_key_raw = rotate(key_back[:, :, None], cosine, -sine).reshape(group_rows, HEAD_SIZE)
    grad_value_raw = value_back.reshape(group_rows, HEAD_SIZE)
    grad_query = left_contract(group_one, grad_query_raw)
    part_one = right_contract(grad_query_raw, back_query)
    grad_mamba = left_contract(mamba_low, grad_mix)
    grad_normed_mix = right_contract(grad_mix, back_mamba)
    scaled_grad = grad_normed_mix * gain_mix
    grad_gain_mix = jnp.sum(grad_normed_mix * mixed_in * inv_rms, axis=0)
    inner_dot = tensor_total(jnp.sum(scaled_grad * mixed_in, axis=1))
    grad_mixed = inv_rms * scaled_grad - mixed_in * inv_rms**3 * (inner_dot / INNER)[:, None]
    (
        grad_gate_raw,
        grad_signal_raw,
        grad_step_raw,
        grad_pair_raw,
        grad_taps_inner,
        grad_taps_shared,
        grad_decay,
        grad_bias,
        grad_skip,
    ) = mixer_back(grad_mixed)
    gate_low = grad_gate_raw.astype(jnp.bfloat16)
    signal_low = grad_signal_raw.astype(jnp.bfloat16)
    step_low = grad_step_raw.astype(jnp.bfloat16)
    grad_inner = jnp.stack(
        [left_contract(group_one, gate_low), left_contract(group_one, signal_low)]
    )
    grad_step = left_contract(group_one, step_low)
    part_one = (
        part_one
        + right_contract(gate_low, back_inner[0])
        + right_contract(signal_low, back_inner[1])
    )
    part_one = part_one + right_contract(step_low, back_step)
    kv_grad = jnp.zeros((group_rows, 2 * kv_cols), jnp.float32)
    kv_grad = lax.dynamic_update_slice_in_dim(kv_grad, grad_key_raw, kv_head * HEAD_SIZE, 1)
    kv_grad = lax.dynamic_update_slice_in_dim(
        kv_grad, grad_value_raw, kv_cols + kv_head * HEAD_SIZE, 1
    )
    shared_part = jnp.concatenate([kv_grad, grad_pair_raw], axis=1)
    part_rows, shared_rows = (
        lax.psum_scatter(
            part_one.astype(jnp.bfloat16), "tensor", scatter_dimension=0, tiled=True
        ).astype(jnp.float32),
        lax.psum_scatter(
            shared_part.astype(jnp.bfloat16), "tensor", scatter_dimension=0, tiled=True
        ).astype(jnp.float32),
    )
    shared_low = shared_rows.astype(jnp.bfloat16)
    grad_shared = left_contract(local_one, shared_low)
    grad_normed_one = part_rows + right_contract(shared_low, back_shared)
    grad_from_one, grad_gain_one = norm_one_back(grad_normed_one)
    gradient_tokens = (grad_resid + grad_from_one).astype(jnp.bfloat16)
    split_grads = (
        lax.psum_scatter(grad_query, "dp", scatter_dimension=0, tiled=True),
        lax.psum_scatter(grad_attend, "dp", scatter_dimension=1, tiled=True),
        lax.psum_scatter(grad_inner, "dp", scatter_dimension=1, tiled=True),
        lax.psum_scatter(grad_step, "dp", scatter_dimension=0, tiled=True),
        lax.psum_scatter(grad_mamba, "dp", scatter_dimension=1, tiled=True),
        lax.psum_scatter(grad_hidden, "dp", scatter_dimension=1, tiled=True),
        lax.psum_scatter(grad_down, "dp", scatter_dimension=1, tiled=True),
        lax.psum_scatter(
            grad_taps_inner.reshape(CONV + 1, local_heads, SSM_DIM),
            "dp",
            scatter_dimension=2,
            tiled=True,
        ),
        lax.psum_scatter(
            grad_gain_mix.reshape(local_heads, SSM_DIM), "dp", scatter_dimension=1, tiled=True
        ),
    )
    shared_grads = (
        lax.psum_scatter(grad_shared, ("dp", "tensor"), scatter_dimension=0, tiled=True),
        lax.psum_scatter(
            jnp.stack([grad_gain_one, grad_gain_two]),
            ("dp", "tensor"),
            scatter_dimension=1,
            tiled=True,
        ),
        lax.psum_scatter(grad_taps_shared, ("dp", "tensor"), scatter_dimension=1, tiled=True),
    )
    head_grads = lax.psum((grad_decay, grad_bias, grad_skip), "dp")
    (
        gradient_query,
        gradient_attend,
        gradient_inner,
        gradient_step,
        gradient_mamba,
        gradient_hidden,
        gradient_down,
        gradient_channel,
        gradient_mixer,
    ) = split_grads
    gradient_shared, gradient_norms, gradient_taps = shared_grads
    gradient_decay, gradient_bias, gradient_skip = head_grads
    return (
        layer_out,
        gradient_tokens,
        gradient_query,
        gradient_attend,
        gradient_inner,
        gradient_step,
        gradient_mamba,
        gradient_hidden,
        gradient_down,
        gradient_channel,
        gradient_mixer,
        gradient_decay,
        gradient_bias,
        gradient_skip,
        gradient_shared,
        gradient_norms,
        gradient_taps,
    )


def solution(mesh):
    placed = (
        P(("dp", "tensor"), None),
        P("dp", "tensor"),
        P("tensor", "dp"),
        P(None, "dp", "tensor"),
        P("dp", "tensor"),
        P("tensor", "dp"),
        P(None, "dp", "tensor"),
        P("tensor", "dp"),
        P(None, "tensor", "dp"),
        P("tensor", "dp"),
        P("tensor"),
        P("tensor"),
        P("tensor"),
        P(("dp", "tensor"), None),
        P(None, ("dp", "tensor")),
        P(None, ("dp", "tensor")),
        P(("dp", "tensor"), None),
    )
    return jax.shard_map(
        per_device,
        mesh=mesh,
        in_specs=placed,
        out_specs=(
            P(("dp", "tensor"), None),
            P(("dp", "tensor"), None),
            P("dp", "tensor"),
            P("tensor", "dp"),
            P(None, "dp", "tensor"),
            P("dp", "tensor"),
            P("tensor", "dp"),
            P(None, "dp", "tensor"),
            P("tensor", "dp"),
            P(None, "tensor", "dp"),
            P("tensor", "dp"),
            P("tensor"),
            P("tensor"),
            P("tensor"),
            P(("dp", "tensor"), None),
            P(None, ("dp", "tensor")),
            P(None, ("dp", "tensor")),
        ),
        check_vma=False,
    )
```

profile of v0, /device:TPU:0, one launch (start us, length us, event | category | flops | bytes accessed | tf_op | source)
XLA Modules:
  0.0 1476.7 jit_solution(16667399744116317751)
XLA Ops:
  9.0 69.5 %all-gather = bf16[32,32,2]{1,2,0:T(2,128)(2,1)S(1)} all-gather(bf16[1,32,2]{1,2,0:T(2,128)(2,1)} %bitcast.536), channel_id=1, replica_groups=mesh['dp'=8,'tensor'=4] {'dp','tensor'}, dimensions={0}, use_global_device_ids=true | all-gather | bytes 4224 | tf_op jit(solution)/shard_map/all_gather | solution.py:237
  84.3 64.9 %all_gather.63 = bf16[5,256]{0,1:T(8,128)(2,1)S(1)} all-gather(bf16[5,8]{0,1:T(8,128)(2,1)S(1)} %copy.414), channel_id=1, replica_groups=mesh['dp'=8,'tensor'=4] {'dp','tensor'}, dimensions={1}, use_global_device_ids=true | all-gather | bytes 2640 | tf_op jit(solution)/shard_map/all_gather | solution.py:238
  150.4 8.3 all_gather.61
  158.8 12.9 all_gather.66
  171.7 10.3 all_gather.59
  186.0 8.0 all_gather.65
  194.1 8.8 all_gather.64
  203.0 9.8 all_gather.60
  231.3 3.0 copy.413
  234.3 2.9 copy.501
  239.5 2.8 convolution_bitcast_fusion.5
  244.4 31.3 %while.11 = (s32[]{:T(128)}, f32[1,6,128,64]{3,2,1,0:T(8,128)S(1)}, f32[8,1,6,128,64]{4,3,2,1,0:T(8,128)}, f32[8,1,6,1,1]{2,4,3,1,0:T(1,128)}, f32[8,1,6]{2,1,0:...) while((s32[]{:T(128)}, f32[1,6,128,64]{3,2,1,0:T(8,128)S(1)}, ...), condition=%wide.region_5.6_spmd.clone, body=%wide.region_4.5_spmd.clone.sunk | while | flops 196611 | bytes 1967296 | solution.py:83
  275.7 3.3 copy.426
  281.9 6.4 bitcast_add_fusion.3
  290.7 3.0 copy.429
  293.7 5.5 multiply_reduce_fusion.8
  299.2 11.0 psum.35
  328.5 40.6 %reduce-scatter.20.cloned.1.call-done = bf16[256,1024]{1,0:T(8,128)(2,1)} async-done(((bf16[1024,1024]{1,0:T(8,128)(2,1)}), bf16[256,1024]{1,0:T(8,128)(2,1)}) %reduce-scatter.20.cloned.1.call-update) | async-done | bytes 524304 | tf_op jit(solution)/shard_map/reduce_scatter | solution.py:167
  374.2 24.0 %all-gather.18.cloned.1.call-done = bf16[2,1024,512]{2,1,0:T(8,128)(2,1)} async-done(((bf16[2,128,512]{2,1,0:T(8,128)(2,1)}), bf16[2,1024,512]{2,1,0:T(8,128)(2,1)}) %all-gather.18.cloned.1.call-update) | async-done | bytes 2097168 | tf_op jit(solution)/shard_map/all_gather | solution.py:230
  398.3 47.5 %all-gather.16.cloned.1.call-done = bf16[1024,1024]{1,0:T(8,128)(2,1)} async-done(((bf16[256,1024]{1,0:T(8,128)(2,1)}), bf16[1024,1024]{1,0:T(8,128)(2,1)}) %all-gather.16.cloned.1.call-update) | async-done | bytes 2097168 | tf_op jit(solution)/shard_map/all_gather | solution.py:173
  445.7 4.6 fusion.88
  450.4 2.7 fusion.89
  453.0 17.1 %all-gather.20.cloned.1.call-done = bf16[512,1024]{1,0:T(8,128)(2,1)} async-done(((bf16[512,128]{1,0:T(8,128)(2,1)}), bf16[512,1024]{1,0:T(8,128)(2,1)}) %all-gather.20.cloned.1.call-update) | async-done | bytes 1048592 | tf_op jit(solution)/shard_map/all_gather | solution.py:231
  470.1 47.6 %all-gather.22.cloned.1.call-done = bf16[1024,1024]{1,0:T(8,128)(2,1)} async-done(((bf16[256,1024]{1,0:T(8,128)(2,1)}), bf16[1024,1024]{1,0:T(8,128)(2,1)}) %all-gather.22.cloned.1.call-update) | async-done | bytes 2097168 | tf_op jit(solution)/shard_map/all_gather | solution.py:173
  517.7 6.4 multiply_convert_fusion
  528.1 42.7 %reduce-scatter.24.cloned.1.call-done = bf16[256,1024]{1,0:T(8,128)(2,1)} async-done(((bf16[1024,1024]{1,0:T(8,128)(2,1)}), bf16[256,1024]{1,0:T(8,128)(2,1)}) %reduce-scatter.24.cloned.1.call-update) | async-done | bytes 524304 | tf_op jit(solution)/shard_map/reduce_scatter | solution.py:177
  574.7 4.9 copy.443
  580.2 39.5 %all-gather.24.cloned.1.call-done = bf16[1024,1024]{1,0:T(8,128)(2,1)} async-done(((bf16[256,1024]{1,0:T(8,128)(2,1)}), bf16[1024,1024]{1,0:T(8,128)(2,1)}) %all-gather.24.cloned.1.call-update) | async-done | bytes 2097168 | tf_op jit(solution)/shard_map/all_gather | solution.py:163
  622.3 5.2 fusion.3
  636.6 3.0 multiply_reduce_fusion.1
  639.7 9.9 psum.36
  649.6 5.6 fusion.29
  655.3 3.0 copy.433
  660.6 6.1 fusion.56
  667.8 2.8 convolution_bitcast_fusion.4
  672.7 47.1 %while.46 = (s32[]{:T(128)}, f32[1,6,128,64]{3,2,1,0:T(8,128)S(1)}, f32[8,1,6]{2,1,0:T(1,128)S(1)}, f32[8,1,6,128,64]{4,3,2,1,0:T(8,128)}, f32[8,1,6,128,64]{3,4...) while((s32[]{:T(128)}, f32[1,6,128,64]{3,2,1,0:T(8,128)S(1)}, ...), condition=%wide.region_18.19_spmd.clone, body=%wide.region_16.18_spmd.clone.sunk | while | flops 294910 | bytes 2163960 | solution.py:83
  720.4 8.8 fusion.27
  731.0 9.8 fusion.20
  742.4 5.2 fusion.65
  761.7 5.7 bitcast_add_fusion.2
  769.8 3.0 copy.441
  772.9 6.2 multiply_reduce_fusion.5
  779.1 2.8 broadcast_multiply_fusion
  787.6 3.8 fusion.100
  792.8 3.4 fusion.90
  802.8 4.2 convolution_convert_fusion
  807.1 39.6 %reduce-scatter.26.cloned.1.call-done = bf16[256,1024]{1,0:T(8,128)(2,1)} async-done(((bf16[1024,1024]{1,0:T(8,128)(2,1)}), bf16[256,1024]{1,0:T(8,128)(2,1)}) %reduce-scatter.26.cloned.1.call-update) | async-done | bytes 524304 | tf_op jit(solution)/shard_map/reduce_scatter | solution.py:403
  846.6 3.0 fusion.75
  850.8 4.6 fusion.173
  855.6 3.3 convolution_bitcast_fusion
  866.4 3.0 fusion.172
  869.4 4.3 fusion.155
  884.8 39.8 %all-reduce.25 = f32[5,256]{1,0:T(8,128)S(1)} all-reduce(f32[5,256]{1,0:T(8,128)S(1)} %pad_add_fusion.7), channel_id=18, replica_groups=mesh['dp'=8,'tensor'=4] {'dp','tensor'}, use_global_device_ids=true, to_apply=%region_61.62.clone | all-reduce | flops 1280 | bytes 10240
  924.6 23.9 %all-reduce.26 = (f32[5,6,64]{2,1,0:T(8,128)S(1)}, f32[6,64]{1,0:T(8,128)S(1)}, f32[6]{0:T(128)}, f32[6]{0:T(128)}, f32[6]{0:T(128)}) all-reduce(f32[5,6,64]{2,1,0:T(8,128)S(1)} %reshape.835, f32[6,64]{1,0:T(8,128)S(1)} %reshape.836, f32[6]{0:T(128)S(1)} %negate_multiply_fusion, ...), channel_id=14, replica_groups=mesh['dp'=8,'tensor'=4] {'dp'}, use_global_device_ids=true, to_apply=%region_42.43.clone | all-reduce | flops 2322 | bytes 18576
  950.6 2.8 fusion.82
  953.3 74.5 %reduce-scatter.46.cloned.1.call-done = f32[32,2]{1,0:T(8,128)} async-done(((f32[1024,2]{1,0:T(8,128)}), f32[32,2]{1,0:T(8,128)}) %reduce-scatter.46.cloned.1.call-update) | async-done | bytes 272
  1029.2 40.3 %reduce-scatter.42.cloned.1.call-done = f32[512,128]{1,0:T(8,128)} async-done(((f32[512,1024]{1,0:T(8,128)}), f32[512,128]{1,0:T(8,128)}) %reduce-scatter.42.cloned.1.call-update) | async-done | bytes 262160 | tf_op jit(solution)/shard_map/reduce_scatter | solution.py:422
  1069.5 55.5 %reduce-scatter.40.cloned.1.call-done = f32[2,128,512]{2,1,0:T(8,128)} async-done(((f32[2,1024,512]{2,1,0:T(8,128)}), f32[2,128,512]{2,1,0:T(8,128)}) %reduce-scatter.40.cloned.1.call-update) | async-done | bytes 524304 | tf_op jit(solution)/shard_map/reduce_scatter | solution.py:421
  1125.0 34.7 %reduce-scatter.36.cloned.1.call-done = f32[128,6]{0,1:T(8,128)} async-done(((f32[1024,6]{0,1:T(8,128)}), f32[128,6]{0,1:T(8,128)}) %reduce-scatter.36.cloned.1.call-update) | async-done | bytes 3088 | tf_op jit(solution)/shard_map/reduce_scatter | solution.py:419
  1159.7 38.0 %reduce-scatter.30.cloned.1.call-done = f32[128,128]{1,0:T(8,128)} async-done(((f32[1024,128]{1,0:T(8,128)}), f32[128,128]{1,0:T(8,128)}) %reduce-scatter.30.cloned.1.call-update) | async-done | bytes 65552 | tf_op jit(solution)/shard_map/reduce_scatter | solution.py:416
  1197.7 37.8 %reduce-scatter.32.cloned.1.call-done = f32[128,128]{1,0:T(8,128)} async-done(((f32[128,1024]{1,0:T(8,128)}), f32[128,128]{1,0:T(8,128)}) %reduce-scatter.32.cloned.1.call-update) | async-done | bytes 65552 | tf_op jit(solution)/shard_map/reduce_scatter | solution.py:417
  1235.5 42.6 %reduce-scatter.38.cloned.1.call-done = f32[384,128]{1,0:T(8,128)} async-done(((f32[384,1024]{1,0:T(8,128)}), f32[384,128]{1,0:T(8,128)}) %reduce-scatter.38.cloned.1.call-update) | async-done | bytes 196624 | tf_op jit(solution)/shard_map/reduce_scatter | solution.py:420
  1278.1 50.6 %reduce-scatter.34.cloned.1.call-done = f32[2,128,384]{2,1,0:T(8,128)} async-done(((f32[2,1024,384]{2,1,0:T(8,128)}), f32[2,128,384]{2,1,0:T(8,128)}) %reduce-scatter.34.cloned.1.call-update) | async-done | bytes 393232 | tf_op jit(solution)/shard_map/reduce_scatter | solution.py:418
  1328.7 141.0 %reduce-scatter.44.cloned.1.call-done = f32[32,512]{1,0:T(8,128)} async-done(((f32[1024,512]{1,0:T(8,128)}), f32[32,512]{1,0:T(8,128)}) %reduce-scatter.44.cloned.1.call-update) | async-done | bytes 65552 | tf_op jit(solution)/shard_map/reduce_scatter | solution.py:434
  (652 shorter events, 222.8 us)
Async XLA Ops:
  7.2 206.8 %all-gather.10.cloned.1.call-start = ((), (), s32[]{:S(2)}) async-start(), calls=%async_computation.14 | async-start | bytes 2621440 | tf_op jit(solution)/shard_map/all_gather | solution.py:163
  8.5 75.8 %copy-start.166 = (bf16[5,8]{1,0:T(8,128)(2,1)S(1)}, bf16[5,8]{1,0:T(8,128)(2,1)}, u32[]{:S(2)}) copy-start(bf16[5,8]{1,0:T(8,128)(2,1)} %param.36) | copy-start | bytes 244
  8.5 72.2 %copy-start.144 = (f32[256]{0:T(256)}, f32[256]{0:T(256)S(1)}, u32[]{:S(2)}) copy-start(f32[256]{0:T(256)S(1)} %fusion.144) | copy-start | bytes 3076
  80.7 69.6 %copy-start.131 = (bf16[5,6,8]{2,1,0:T(8,128)(2,1)S(1)}, bf16[5,6,8]{2,1,0:T(8,128)(2,1)}, u32[]{:S(2)}) copy-start(bf16[5,6,8]{2,1,0:T(8,128)(2,1)} %param.29) | copy-start | bytes 1444
  80.7 78.2 %copy-start.87 = (bf16[384,128]{1,0:T(8,128)(2,1)S(1)}, bf16[384,128]{1,0:T(8,128)(2,1)}, u32[]{:S(2)}) copy-start(bf16[384,128]{1,0:T(8,128)(2,1)} %param.26) | copy-start | bytes 294916
  80.7 139.5 %all-gather.12.cloned.1.call-start = ((), (), s32[]{:S(2)}) async-start(), calls=%async_computation.15 | async-start | bytes 1081344 | tf_op jit(solution)/shard_map/all_gather | solution.py:236
  81.4 144.6 %all-gather.14.cloned.1.call-start = ((), (), s32[]{:S(2)}) async-start(), calls=%async_computation.16 | async-start | bytes 1769472 | tf_op jit(solution)/shard_map/all_gather | solution.py:227
  82.2 286.9 %reduce-scatter.20.cloned.1.call-start = ((), (), s32[]{:S(2)}) async-start(), calls=%async_computation.17 | async-start | bytes 2621440 | tf_op jit(solution)/shard_map/reduce_scatter | solution.py:167
  82.9 129.9 %copy-start.153 = (f32[32]{0:T(128)}, f32[32]{0:T(128)S(1)}, u32[]{:S(2)}) copy-start(f32[32]{0:T(128)S(1)} %multiply_power_fusion) | copy-start | bytes 388
  82.9 88.9 %copy-start.97 = (bf16[128,128]{1,0:T(8,128)(2,1)S(1)}, bf16[128,128]{1,0:T(8,128)(2,1)}, u32[]{:S(2)}) copy-start(bf16[128,128]{1,0:T(8,128)(2,1)} %param.22) | copy-start | bytes 98308
  82.9 99.1 %copy-start.171 = (bf16[6]{0:T(256)(128)(2,1)S(1)}, bf16[6]{0:T(256)(128)(2,1)}, u32[]{:S(2)}) copy-start(bf16[6]{0:T(256)(128)(2,1)} %param.32) | copy-start | bytes 40
  84.2 100.9 %copy-start.168 = (bf16[6]{0:T(256)(128)(2,1)S(1)}, bf16[6]{0:T(256)(128)(2,1)}, u32[]{:S(2)}) copy-start(bf16[6]{0:T(256)(128)(2,1)} %param.33) | copy-start | bytes 40
  84.2 101.7 %copy-start.167 = (bf16[6,8]{1,0:T(8,128)(2,1)S(1)}, bf16[6,8]{1,0:T(8,128)(2,1)}, u32[]{:S(2)}) copy-start(bf16[6,8]{1,0:T(8,128)(2,1)} %param.30) | copy-start | bytes 292
  84.2 109.9 %copy-start.164 = (bf16[128,6]{0,1:T(8,128)(2,1)S(1)}, bf16[128,6]{0,1:T(8,128)(2,1)}, u32[]{:S(2)}) copy-start(bf16[128,6]{0,1:T(8,128)(2,1)} %param.25) | copy-start | bytes 4612
  84.2 118.7 %copy-start.98 = (bf16[128,128]{1,0:T(8,128)(2,1)S(1)}, bf16[128,128]{1,0:T(8,128)(2,1)}, u32[]{:S(2)}) copy-start(bf16[128,128]{1,0:T(8,128)(2,1)} %param.23) | copy-start | bytes 98308
  149.3 63.4 %copy-start.172 = (bf16[6]{0:T(256)(128)(2,1)S(1)}, bf16[6]{0:T(256)(128)(2,1)}, u32[]{:S(2)}) copy-start(bf16[6]{0:T(256)(128)(2,1)} %param.31) | copy-start | bytes 40
  182.2 46.4 %copy-start.113 = (f32[384]{0:T(512)}, f32[384]{0:T(512)S(1)}, u32[]{:S(2)}) copy-start(f32[384]{0:T(512)S(1)} %mul.1046) | copy-start | bytes 4612
  194.1 130.1 %copy-start.89 = (f32[384]{0:T(512)}, f32[384]{0:T(512)S(1)}, u32[]{:S(2)}) copy-start(f32[384]{0:T(512)S(1)} %reshape.840) | copy-start | bytes 4612
  203.0 11.1 copy-start.84
  220.2 17.0 %copy-start.91 = (f32[8,6]{1,0:T(8,128)}, f32[8,6]{1,0:T(8,128)S(1)}, u32[]{:S(2)}) copy-start(f32[8,6]{1,0:T(8,128)S(1)} %get-tuple-element.473) | copy-start | bytes 580
  226.0 13.5 copy-start.15
  299.2 13.0 copy-start.154
  299.2 16.2 %copy-start.43 = (bf16[1024,128]{1,0:T(8,128)(2,1)S(1)}, bf16[1024,128]{1,0:T(8,128)(2,1)}, u32[]{:S(2)}) copy-start(bf16[1024,128]{1,0:T(8,128)(2,1)} %all_gather.59) | copy-start | bytes 786436
  327.8 41.3 %copy-start.4 = (bf16[256,1024]{1,0:T(8,128)(2,1)S(1)}, bf16[256,1024]{1,0:T(8,128)(2,1)}, u32[]{:S(2)}) copy-start(bf16[256,1024]{1,0:T(8,128)(2,1)} %param.21) | copy-start | bytes 1572868
  327.8 70.4 %all-gather.18.cloned.1.call-start = ((), (), s32[]{:S(2)}) async-start(), calls=%async_computation.19 | async-start | bytes 2359296 | tf_op jit(solution)/shard_map/all_gather | solution.py:230
  328.4 117.3 %all-gather.16.cloned.1.call-start = ((), (), s32[]{:S(2)}) async-start(), calls=%async_computation.18 | async-start | bytes 2621440 | tf_op jit(solution)/shard_map/all_gather | solution.py:173
  370.4 202.7 %copy-start.111 = (f32[256]{0:T(256)}, f32[256]{0:T(256)S(1)}, u32[]{:S(2)}) copy-start(f32[256]{0:T(256)S(1)} %fusion.145) | copy-start | bytes 3076
  372.5 97.6 %all-gather.20.cloned.1.call-start = ((), (), s32[]{:S(2)}) async-start(), calls=%async_computation.20 | async-start | bytes 1179648 | tf_op jit(solution)/shard_map/all_gather | solution.py:231
  373.2 144.5 %all-gather.22.cloned.1.call-start = ((), (), s32[]{:S(2)}) async-start(), calls=%async_computation.22 | async-start | bytes 2621440 | tf_op jit(solution)/shard_map/all_gather | solution.py:173
  374.0 196.9 %reduce-scatter.24.cloned.1.call-start = ((), (), s32[]{:S(2)}) async-start(), calls=%async_computation.23 | async-start | bytes 2621440 | tf_op jit(solution)/shard_map/reduce_scatter | solution.py:177
  528.1 42.8 %copy-start.18 = (bf16[256,1024]{1,0:T(8,128)(2,1)S(1)}, bf16[256,1024]{1,0:T(8,128)(2,1)}, u32[]{:S(2)}) copy-start(bf16[256,1024]{1,0:T(8,128)(2,1)} %reduce-scatter.20.cloned.1.call-done) | copy-start | bytes 1572868
  528.1 91.6 %all-gather.24.cloned.1.call-start = ((), (), s32[]{:S(2)}) async-start(), calls=%async_computation.24 | async-start | bytes 2621440 | tf_op jit(solution)/shard_map/all_gather | solution.py:163
  574.4 232.7 %reduce-scatter.28.cloned.1.call-start = ((), (), s32[]{:S(2)}) async-start(), calls=%async_computation.26 | async-start | bytes 1310720 | tf_op jit(solution)/shard_map/reduce_scatter | solution.py:406
  636.6 13.0 copy-start.122
  636.6 13.0 copy-start.124
  720.4 9.9 copy-start.94
  720.4 10.6 copy-start.58
  720.4 10.6 copy-start.100
  720.4 10.6 copy-start.103
  720.4 10.6 copy-start.128
  729.2 11.7 copy-start.55
  731.0 11.3 copy-start.3
  761.5 85.1 %reduce-scatter.26.cloned.1.call-start = ((), (), s32[]{:S(2)}) async-start(), calls=%async_computation.25 | async-start | bytes 2621440 | tf_op jit(solution)/shard_map/reduce_scatter | solution.py:403
  802.7 147.8 %reduce-scatter.22.cloned.1.call-start = ((), (), s32[]{:S(2)}) async-start(), calls=%async_computation.21 | async-start | bytes 2621440 | tf_op jit(solution)/shard_map/reduce_scatter | solution.py:177
  807.0 39.7 %copy-start.96 = (f32[1,1024]{1,0:T(1,128)S(1)}, f32[1,1024]{1,0:T(1,128)}, u32[]{:S(2)}) copy-start(f32[1,1024]{1,0:T(1,128)} %copy-done.95) | copy-start | bytes 12292
  807.0 39.7 %copy-start.145 = (f32[256]{0:T(256)S(1)}, f32[256]{0:T(256)}, u32[]{:S(2)}) copy-start(f32[256]{0:T(256)} %copy-done.144) | copy-start | bytes 3076
  807.0 42.7 %copy-start.125 = (f32[1024]{0:T(1024)S(1)}, f32[1024]{0:T(1024)}, u32[]{:S(2)}) copy-start(f32[1024]{0:T(1024)} %get-tuple-element.391) | copy-start | bytes 12292
  807.0 220.9 %reduce-scatter.46.cloned.1.call-start = ((), (), s32[]{:S(2)}) async-start(), calls=%async_computation.35 | async-start | bytes 540672
  850.7 218.8 %reduce-scatter.42.cloned.1.call-start = ((), (), s32[]{:S(2)}) async-start(), calls=%async_computation.33 | async-start | bytes 2359296 | tf_op jit(solution)/shard_map/reduce_scatter | solution.py:422
  855.3 269.7 %reduce-scatter.40.cloned.1.call-start = ((), (), s32[]{:S(2)}) async-start(), calls=%async_computation.32 | async-start | bytes 4718592 | tf_op jit(solution)/shard_map/reduce_scatter | solution.py:421
  862.7 297.0 %reduce-scatter.36.cloned.1.call-start = ((), (), s32[]{:S(2)}) async-start(), calls=%async_computation.30 | async-start | bytes 36864 | tf_op jit(solution)/shard_map/reduce_scatter | solution.py:419
  863.8 334.0 %reduce-scatter.30.cloned.1.call-start = ((), (), s32[]{:S(2)}) async-start(), calls=%async_computation.27 | async-start | bytes 589824 | tf_op jit(solution)/shard_map/reduce_scatter | solution.py:416
  866.3 369.2 %reduce-scatter.32.cloned.1.call-start = ((), (), s32[]{:S(2)}) async-start(), calls=%async_computation.28 | async-start | bytes 589824 | tf_op jit(solution)/shard_map/reduce_scatter | solution.py:417
  869.4 408.7 %reduce-scatter.38.cloned.1.call-start = ((), (), s32[]{:S(2)}) async-start(), calls=%async_computation.31 | async-start | bytes 1769472 | tf_op jit(solution)/shard_map/reduce_scatter | solution.py:420
  873.8 454.9 %reduce-scatter.34.cloned.1.call-start = ((), (), s32[]{:S(2)}) async-start(), calls=%async_computation.29 | async-start | bytes 3538944 | tf_op jit(solution)/shard_map/reduce_scatter | solution.py:418
  879.5 590.2 %reduce-scatter.44.cloned.1.call-start = ((), (), s32[]{:S(2)}) async-start(), calls=%async_computation.34 | async-start | bytes 2162688 | tf_op jit(solution)/shard_map/reduce_scatter | solution.py:434
  880.6 70.0 %copy-start.51 = (f32[256,1024]{1,0:T(8,128)S(1)}, f32[256,1024]{1,0:T(8,128)}, u32[]{:S(2)}) copy-start(f32[256,1024]{1,0:T(8,128)} %get-tuple-element.505) | copy-start | bytes 3145732
  882.4 42.1 %copy-start.173 = (bf16[6]{0:T(256)(128)(2,1)S(1)}, bf16[6]{0:T(256)(128)(2,1)}, u32[]{:S(2)}) copy-start(bf16[6]{0:T(256)(128)(2,1)} %param.31) | copy-start | bytes 40
  882.5 68.0 %copy-start.133 = (f32[256]{0:T(256)S(1)}, f32[256]{0:T(256)}, u32[]{:S(2)}) copy-start(f32[256]{0:T(256)} %copy-done.132) | copy-start | bytes 3076
  882.5 68.1 %copy-start.19 = (bf16[256,1024]{1,0:T(8,128)(2,1)S(1)}, bf16[256,1024]{1,0:T(8,128)(2,1)}, u32[]{:S(2)}) copy-start(bf16[256,1024]{1,0:T(8,128)(2,1)} %reduce-scatter.20.cloned.1.call-done) | copy-start | bytes 1572868
  882.5 68.1 %copy-start.35 = (bf16[256,1024]{1,0:T(8,128)(2,1)S(1)}, bf16[256,1024]{1,0:T(8,128)(2,1)}, u32[]{:S(2)}) copy-start(bf16[256,1024]{1,0:T(8,128)(2,1)} %param.37) | copy-start | bytes 1572868
  882.5 68.1 %copy-start.37 = (bf16[256,1024]{1,0:T(8,128)(2,1)S(1)}, bf16[256,1024]{1,0:T(8,128)(2,1)}, u32[]{:S(2)}) copy-start(bf16[256,1024]{1,0:T(8,128)(2,1)} %reduce-scatter.24.cloned.1.call-done) | copy-start | bytes 1572868
  882.5 68.1 %copy-start.112 = (f32[256]{0:T(256)S(1)}, f32[256]{0:T(256)}, u32[]{:S(2)}) copy-start(f32[256]{0:T(256)} %copy-done.111) | copy-start | bytes 3076
  882.5 68.1 %copy-start.143 = (f32[256]{0:T(256)S(1)}, f32[256]{0:T(256)}, u32[]{:S(2)}) copy-start(f32[256]{0:T(256)} %copy-done.142) | copy-start | bytes 3076
  (137 other events, 404.4 us)
Sparse Core Ops, SparseCore 0:
  80.8 42.9 all-gather.9
  126.7 52.6 all-gather.11
  181.4 24.7 all-gather.13
  328.0 41.0 reduce-scatter.19
  371.0 27.2 all-gather.17
  399.8 45.9 all-gather.15
  447.8 22.2 all-gather.19
  471.7 45.9 all-gather.21
  528.2 42.5 reduce-scatter.23
  574.5 45.2 all-gather.23
  761.6 27.0 reduce-scatter.27
  802.9 43.7 reduce-scatter.25
  848.9 43.0 reduce-scatter.21
  894.2 133.6 reduce-scatter.45
  1031.6 37.8 reduce-scatter.41
  1073.7 51.3 reduce-scatter.39
  1128.5 31.1 reduce-scatter.35
  1163.5 34.1 reduce-scatter.29
  1201.4 34.0 reduce-scatter.31
  1239.6 38.4 reduce-scatter.37
  1282.4 46.2 reduce-scatter.33
  1331.5 138.1 reduce-scatter.43
where the time goes:
time: 1480 us
  waiting for transfers between devices  817 us (55%)
  blocking collectives  277 us (19%)
  matrix products  145 us (10%)
  local copies, waits for them, and re-layouts  128 us (9%)
  other arithmetic  89.4 us (6%)
  between operations  17.2 us (1%)
    reduce_scatter x1, waiting for transfers between devices, per_device(): lax.psum_scatter(grad_shared, ('dp', 'tensor'), scatter_dimension=0, tile...  141 us
    all_gather x2, waiting for transfers between devices, ffn_collect(): return lax.all_gather(values, 'tensor', axis=0, tiled=True)  95.1 us
    unnamed x23, waiting for transfers between devices  78.1 us
    all_gather x1, blocking collectives, per_device(): lax.all_gather(norm_gains, ('dp', 'tensor'), axis=1, tiled=True)  69.5 us
    all_gather x1, blocking collectives, per_device(): lax.all_gather(shared_taps, ('dp', 'tensor'), axis=1, tiled=True)  64.9 us
    unnamed x2, blocking collectives  63.7 us
    reduce_scatter x1, waiting for transfers between devices, per_device(): lax.psum_scatter(grad_hidden, 'dp', scatter_dimension=1, tiled=True)  55.5 us
    reduce_scatter x1, waiting for transfers between devices, per_device(): lax.psum_scatter(grad_inner, 'dp', scatter_dimension=1, tiled=True)  50.6 us
  transfers between devices with their start and end apart: 22, of which 17 were waited for; matrix products, arithmetic and copies ran while one was open for 8% of the time, Pallas kernels for 0%

commit v1 on v0

v1 whole, which is shorter than its diff:
```python
from functools import partial

import jax
import jax.numpy as jnp
from jax import lax
from jax.experimental import pallas as pl
from jax.experimental.pallas import tpu as pltpu
from jax.sharding import PartitionSpec as P

MESH = pl.DeviceIdType.MESH

QHEADS = 8
KVHEADS = 2
HEAD_SIZE = 64
SSM_DIM = 64
CONV = 4
SEQS_DEV = 1
INNER = 1536


epsilon = 1e-05
rope_base = 100000000000.0
highest_precision = lax.Precision.HIGHEST
neg_large = -1e30
block_len = 128


def norm_apply(values, gain):
    factor = lax.rsqrt(jnp.mean(values * values, axis=-1, keepdims=True) + epsilon)
    return values * factor * gain


def rope_tables(length, width):
    halfway = width // 2
    inverse = rope_base ** (-jnp.arange(halfway, dtype=jnp.float32) * (2.0 / width))
    angles = jnp.arange(length, dtype=jnp.float32)[:, None] * inverse[None, :]
    return (jnp.cos(angles), jnp.sin(angles))


def rotate(values, cosine, sine):
    halfway = values.shape[-1] // 2
    first = values[..., :halfway]
    second = values[..., halfway:]
    cos_wide = cosine[:, None, :]
    sin_wide = sine[:, None, :]
    return jnp.concatenate(
        [first * cos_wide - second * sin_wide, second * cos_wide + first * sin_wide], axis=-1
    )


def causal_conv(sequences, table):
    taps = table.shape[0] - 1
    length = sequences.shape[1]
    padded = jnp.pad(sequences, ((0, 0), (taps - 1, 0), (0, 0)))
    total = table[taps] + jnp.zeros_like(sequences)
    for offset in range(taps):
        total = total + table[offset] * padded[:, offset : offset + length]
    return total


def duality_scan(inputs, step_size, decay, in_mat, out_mat):
    length, num_heads, head_width = inputs.shape
    state_width = in_mat.shape[-1]
    window = min(block_len, length)
    blocks = length // window
    x_blocks = inputs.reshape(blocks, window, num_heads, head_width)
    s_blocks = step_size.reshape(blocks, window, num_heads)
    b_blocks = in_mat.reshape(blocks, window, state_width)
    c_blocks = out_mat.reshape(blocks, window, state_width)
    cumul = jnp.cumsum(s_blocks * decay, axis=1)
    lower_mask = jnp.arange(window)[:, None] >= jnp.arange(window)[None, :]
    gap_logs = cumul[:, :, None, :] - cumul[:, None, :, :]
    fading = jnp.exp(jnp.where(lower_mask[None, :, :, None], gap_logs, -jnp.inf))
    cross_terms = jnp.einsum("cin,cjn->cij", c_blocks, b_blocks, precision=highest_precision)
    mixing = cross_terms[..., None] * fading * s_blocks[:, None, :, :]
    within = jnp.einsum("cijh,cjhp->cihp", mixing, x_blocks, precision=highest_precision)
    ending = cumul[:, -1:, :]
    carried = x_blocks * (jnp.exp(ending - cumul) * s_blocks)[..., None]
    contrib = jnp.einsum("cjn,cjhp->chnp", b_blocks, carried, precision=highest_precision)
    block_fade = jnp.exp(ending[:, 0, :])

    def advance(carry, pieces):
        fade_now, added = pieces
        return (fade_now[:, None, None] * carry + added, carry)

    start = jnp.zeros((num_heads, state_width, head_width), inputs.dtype)
    finished, entering = lax.scan(advance, start, (block_fade, contrib))
    across = (
        jnp.einsum("cin,chnp->cihp", c_blocks, entering, precision=highest_precision)
        * jnp.exp(cumul)[..., None]
    )
    return (within + across).reshape(length, num_heads, head_width)


def mixer_local(
    gate_raw,
    signal_raw,
    step_raw,
    pair_raw,
    inner_taps,
    outer_taps,
    decay_log,
    step_bias,
    skip_weight,
    num_seq,
):
    total_rows = gate_raw.shape[0]
    seq_len = total_rows // num_seq
    num_heads = step_raw.shape[1]
    head_width = signal_raw.shape[1] // num_heads
    signal = jax.nn.silu(causal_conv(signal_raw.reshape(num_seq, seq_len, -1), inner_taps))
    paired = jax.nn.silu(causal_conv(pair_raw.reshape(num_seq, seq_len, -1), outer_taps))
    state_width = paired.shape[-1] // 2
    in_mat = paired[..., :state_width]
    out_mat = paired[..., state_width:]
    step_size = jax.nn.softplus(step_raw.reshape(num_seq, seq_len, num_heads) + step_bias)
    decay = -jnp.exp(decay_log)
    signal_heads = signal.reshape(num_seq, seq_len, num_heads, head_width)
    scanned = jax.vmap(duality_scan, in_axes=(0, 0, None, 0, 0))(
        signal_heads, step_size, decay, in_mat, out_mat
    )
    scanned = scanned + skip_weight[:, None] * signal_heads
    return scanned.reshape(total_rows, num_heads * head_width) * jax.nn.silu(gate_raw)


def causal_scores(query_low, key_low):
    length = query_low.shape[0]
    attention_scores = jnp.einsum(
        "lhd,md->hlm", query_low, key_low, preferred_element_type=jnp.float32
    ) * HEAD_SIZE ** (-0.5)
    causal = jnp.arange(length)[:, None] >= jnp.arange(length)[None, :]
    return jnp.where(causal[None], attention_scores, neg_large)


def attend_forward(pieces):
    query_low, key_low, value_low = pieces
    attention_scores = causal_scores(query_low, key_low)
    top_score = jnp.max(attention_scores, axis=-1, keepdims=True)
    expd = jnp.exp(attention_scores - top_score)
    total = jnp.sum(expd, axis=-1, keepdims=True)
    attention_probabilities = (expd / total).astype(jnp.bfloat16)
    result = jnp.einsum(
        "hlm,md->lhd", attention_probabilities, value_low, preferred_element_type=jnp.float32
    )
    return (result.astype(jnp.bfloat16), top_score[..., 0] + jnp.log(total[..., 0]))


def attend_backward(pieces):
    query_low, key_low, value_low, log_sums, grad_low = pieces
    attention_scores = causal_scores(query_low, key_low)
    attention_probabilities = jnp.exp(attention_scores - log_sums[..., None])
    probs_low = attention_probabilities.astype(jnp.bfloat16)
    grad_probs = jnp.einsum("lhd,md->hlm", grad_low, value_low, preferred_element_type=jnp.float32)
    centre = jnp.sum(attention_probabilities * grad_probs, axis=-1, keepdims=True)
    grad_scores = (attention_probabilities * (grad_probs - centre)).astype(jnp.bfloat16)
    query_back = jnp.einsum(
        "hlm,md->lhd", grad_scores, key_low, preferred_element_type=jnp.float32
    ) * HEAD_SIZE ** (-0.5)
    key_back = jnp.einsum(
        "hlm,lhd->md", grad_scores, query_low, preferred_element_type=jnp.float32
    ) * HEAD_SIZE ** (-0.5)
    value_back = jnp.einsum("hlm,lhd->md", probs_low, grad_low, preferred_element_type=jnp.float32)
    return (query_back, key_back, value_back)


def dp_bits(index):
    core = lax.rem(index, 2)
    xbit = lax.rem(index // 2, 2)
    ybit = lax.rem(index // 4, 2)
    return core, xbit, ybit


def gather_kernel(nt, *refs):
    (tok, que, att, inn, stp, mam, sha, sma) = refs[:8]
    (tok_f, que_f, att_f, inn_f, stp_f, mam_f, sha_f, sma_f) = refs[8:16]
    (lsem, zs_send, zs_recv, t_send, t_recv, d_send, d_recv) = refs[16:]
    d = lax.axis_index("dp")
    z = lax.axis_index("tensor")
    core, xbit, ybit = dp_bits(d)
    d_core = d + 1 - 2 * core
    d_x = d + 2 - 4 * xbit
    d_y = d + 4 - 8 * ybit
    d_xy = d_x + 4 - 8 * ybit

    barrier = pltpu.get_barrier_semaphore()
    for peer in (d_core, d_x, d_y):
        pl.semaphore_signal(barrier, inc=1, device_id=(peer, z), device_id_type=MESH)
    for k in range(1, nt):
        pl.semaphore_signal(
            barrier, inc=1, device_id=(d, lax.rem(z + k, nt)), device_id_type=MESH
        )
    pl.semaphore_wait(barrier, 3 + nt - 1)

    def remote(src, dst, send, recv, dev):
        return pltpu.make_async_remote_copy(
            src_ref=src, dst_ref=dst, send_sem=send, recv_sem=recv,
            device_id=dev, device_id_type=MESH,
        )

    small = []
    for i, (src, dst) in enumerate(((sha, sha_f), (sma, sma_f))):
        for k in range(1, nt):
            copy = remote(
                src, dst.at[d, z], zs_send.at[i, k], zs_recv.at[i, k],
                (d, lax.rem(z + k, nt)),
            )
            copy.start()
            small.append(copy)
    q_rows = que.shape[0]
    cols = att.shape[1]
    i_rows = inn.shape[1]
    s_rows = stp.shape[0]
    items = (
        (inn, lambda s: inn_f.at[:, pl.ds(s * i_rows, i_rows)]),
        (que, lambda s: que_f.at[pl.ds(s * q_rows, q_rows)]),
        (att, lambda s: att_f.at[:, pl.ds(pl.multiple_of(s * cols, cols), cols)]),
        (stp, lambda s: stp_f.at[pl.ds(s * s_rows, s_rows)]),
        (mam, lambda s: mam_f.at[:, pl.ds(pl.multiple_of(s * cols, cols), cols)]),
    )
    locals_ = []
    for i, (src, dst) in enumerate(
        [(tok, tok_f.at[z]), (sha, sha_f.at[d, z]), (sma, sma_f.at[d, z])]
        + [(src, at(d)) for src, at in items]
    ):
        copy = pltpu.make_async_copy(src, dst, lsem.at[i])
        copy.start()
        locals_.append(copy)
    sent = []

    def stage_one(i, src, at):
        for j, peer in enumerate((d_x, d_y, d_core)):
            copy = remote(src, at(d), d_send.at[i, j], d_recv.at[i, j], (peer, z))
            copy.start()
            sent.append(copy)

    for i, (src, at) in enumerate(items):
        stage_one(i, src, at)

    def tok_copy(slot, dirn, hop):
        dev = z + 1 if dirn == 0 else z - 1
        return remote(
            tok_f.at[slot], tok_f.at[slot], t_send.at[dirn, hop], t_recv.at[dirn, hop], (d, dev)
        )

    def own_copy(dirn):
        dev = z + 1 if dirn == 0 else z - 1
        return remote(tok, tok_f.at[z], t_send.at[dirn, 0], t_recv.at[dirn, 0], (d, dev))

    pl.when(z < nt - 1)(lambda: own_copy(0).start())
    pl.when(z > 0)(lambda: own_copy(1).start())

    locals_[1].wait()
    locals_[2].wait()
    for copy in small:
        copy.wait()
    n = len(items)
    shared_items = (
        (sha_f.at[d], lambda s: sha_f.at[s]),
        (sma_f.at[d], lambda s: sma_f.at[s]),
    )
    for i, (src, at) in enumerate(shared_items):
        stage_one(n + i, src, at)

    def wait_recv(i, j, at, slot):
        remote(at(slot), at(slot), d_send.at[i, j], d_recv.at[i, j], (d_core, z)).wait_recv()

    def forward(i, j, at, slot, peer):
        copy = remote(at(slot), at(slot), d_send.at[i, j], d_recv.at[i, j], (peer, z))
        copy.start()
        sent.append(copy)

    everything = [at for _, at in items] + [at for _, at in shared_items]
    via_y = (0, n + 1)

    def diagonal(i, at):
        wait_recv(i, 0, at, d_x)
        if i in via_y:
            forward(i, 3, at, d_x, d_y)
        forward(i, 4, at, d_x, d_core)
        wait_recv(i, 1, at, d_y)
        if i not in via_y:
            forward(i, 3, at, d_y, d_x)
        forward(i, 5, at, d_y, d_core)

    for i in range(n):
        diagonal(i, everything[i])

    def hop(dist):
        def from_left():
            tok_copy(z - dist, 0, dist - 1).wait_recv()

        def from_right():
            tok_copy(z + dist, 1, dist - 1).wait_recv()

        pl.when(z >= dist)(from_left)
        if dist < nt - 1:
            pl.when((z >= dist) & (z < nt - 1))(lambda: tok_copy(z - dist, 0, dist).start())
        pl.when(z + dist < nt)(from_right)
        if dist < nt - 1:
            pl.when((z + dist < nt) & (z > 0))(lambda: tok_copy(z + dist, 1, dist).start())

    hop(1)
    for i in range(n, n + 2):
        diagonal(i, everything[i])
    for i, at in enumerate(everything):
        wait_recv(i, 3, at, d_xy)
        forward(i, 6, at, d_xy, d_core)
    for dist in range(2, nt):
        hop(dist)
    for i, at in enumerate(everything):
        wait_recv(i, 2, at, d_core)
        for j in (4, 5, 6):
            wait_recv(i, j, at, d_core)
    for i, copy in enumerate(locals_):
        if i not in (1, 2):
            copy.wait()
    for copy in sent:
        copy.wait_send()
    pl.when(z < nt - 1)(lambda: own_copy(0).wait_send())
    pl.when(z > 0)(lambda: own_copy(1).wait_send())
    for dist in range(1, nt - 1):
        pl.when((z >= dist) & (z < nt - 1))(lambda: tok_copy(z - dist, 0, dist).wait_send())
        pl.when((z + dist < nt) & (z > 0))(lambda: tok_copy(z + dist, 1, dist).wait_send())


def gather_start(tok, que, att, inn, stp, mam, sha, sma, nd, nt):
    if nd != 8:
        shared = lax.all_gather(sha, ("dp", "tensor"), axis=0)
        small = lax.all_gather(sma, ("dp", "tensor"), axis=0)
        return (
            lax.all_gather(tok, "tensor", axis=0),
            lax.all_gather(que, "dp", axis=0, tiled=True),
            lax.all_gather(att, "dp", axis=1, tiled=True),
            lax.all_gather(inn, "dp", axis=1, tiled=True),
            lax.all_gather(stp, "dp", axis=0, tiled=True),
            lax.all_gather(mam, "dp", axis=1, tiled=True),
            shared.reshape((nd, nt) + sha.shape),
            small.reshape((nd, nt) + sma.shape),
        )
    bf = jnp.bfloat16
    outs = (
        (nt,) + tok.shape,
        (nd * que.shape[0], que.shape[1]),
        (att.shape[0], nd * att.shape[1]),
        (2, nd * inn.shape[1], inn.shape[2]),
        (nd * stp.shape[0], stp.shape[1]),
        (mam.shape[0], nd * mam.shape[1]),
        (nd, nt) + sha.shape,
        (nd, nt) + sma.shape,
    )
    anywhere = pl.BlockSpec(memory_space=pl.ANY)
    dma = pltpu.SemaphoreType.DMA
    return pl.pallas_call(
        partial(gather_kernel, nt),
        out_shape=[jax.ShapeDtypeStruct(s, bf) for s in outs],
        in_specs=[anywhere] * 8,
        out_specs=[anywhere] * 8,
        scratch_shapes=[
            dma((8,)), dma((2, nt)), dma((2, nt)), dma((2, nt)), dma((2, nt)),
            dma((7, 7)), dma((7, 7)),
        ],
        compiler_params=pltpu.CompilerParams(collective_id=0, has_side_effects=True),
        name="gather_start",
    )(tok, que, att, inn, stp, mam, sha, sma)


def pick(values, index, axis=0):
    return lax.dynamic_index_in_dim(values, index, axis, keepdims=False)


def add_low(left, right):
    return (left.astype(jnp.float32) + right.astype(jnp.float32)).astype(jnp.bfloat16)


def chain_gather(values, nt):
    z = lax.axis_index("tensor")
    out = jnp.zeros((nt,) + values.shape, values.dtype)
    out = lax.dynamic_update_index_in_dim(out, values, z, 0)
    right = left = values
    for dist in range(1, nt):
        right = lax.ppermute(right, "tensor", [(i, i + 1) for i in range(dist - 1, nt - 1)])
        left = lax.ppermute(left, "tensor", [(i, i - 1) for i in range(1, nt - dist + 1)])
        pieces = out
        pieces = jnp.where(
            z >= dist,
            lax.dynamic_update_index_in_dim(pieces, right, jnp.maximum(z - dist, 0), 0),
            pieces,
        )
        out = jnp.where(
            z + dist < nt,
            lax.dynamic_update_index_in_dim(pieces, left, jnp.minimum(z + dist, nt - 1), 0),
            pieces,
        )
    return out


def chain_scatter(parts, nt):
    z = lax.axis_index("tensor")
    right = left = None
    for t in range(nt - 1):
        to_right = pick(parts, jnp.clip(nt - 1 - t + z, 0, nt - 1))
        to_left = pick(parts, jnp.clip(t - (nt - 1) + z, 0, nt - 1))
        if t > 0:
            to_right = add_low(to_right, right)
            to_left = add_low(to_left, left)
        right = lax.ppermute(to_right, "tensor", [(i, i + 1) for i in range(t + 1)])
        left = lax.ppermute(
            to_left, "tensor", [(nt - 1 - i, nt - 2 - i) for i in range(t + 1)]
        )
    f32 = jnp.float32
    return pick(parts, z).astype(f32) + right.astype(f32) + left.astype(f32)


def cube_scatter(parts, nd, last=jnp.float32):
    if nd != 8:
        return lax.psum_scatter(parts, "dp", scatter_dimension=0, tiled=False).astype(last)
    d = lax.axis_index("dp")
    core, xbit, ybit = dp_bits(d)

    def swap(values, bit):
        return lax.ppermute(values, "dp", [(i, i ^ bit) for i in range(8)])

    tail = parts.shape[1:]
    cut = parts.reshape((4, 2) + tail)
    held = add_low(pick(cut, core, 1), swap(pick(cut, 1 - core, 1), 1))
    held = held.reshape((2, 2) + tail)
    half = tail[0] // 2
    one, two = held[:, :, :half], held[:, :, half:]
    one_b = add_low(pick(one, xbit, 1), swap(pick(one, 1 - xbit, 1), 2))
    two_b = add_low(pick(two, ybit, 0), swap(pick(two, 1 - ybit, 0), 4))
    f32 = jnp.float32
    one_c = pick(one_b, ybit).astype(f32) + swap(pick(one_b, 1 - ybit), 4).astype(f32)
    two_c = pick(two_b, xbit).astype(f32) + swap(pick(two_b, 1 - xbit), 2).astype(f32)
    return jnp.concatenate([one_c, two_c], axis=0).astype(last)


def tensor_total(values):
    return lax.psum(values, "tensor")


def matmul(left, right):
    return jnp.dot(left, right, preferred_element_type=jnp.float32)


def left_contract(left, right):
    return jnp.einsum("md,mk->dk", left, right, preferred_element_type=jnp.float32)


def right_contract(left, right):
    return jnp.einsum("mk,dk->md", left, right, preferred_element_type=jnp.float32)


def per_device(
    nd,
    nt,
    tokens,
    query_proj,
    attend_out,
    inner_proj,
    step_proj,
    mamba_out,
    hidden_proj,
    down_proj,
    channel_taps,
    mixer_gain,
    decay_log,
    step_bias,
    skip_weight,
    shared_proj,
    norm_gains,
    shared_taps,
    cotangent,
):
    f32, bf16 = jnp.float32, jnp.bfloat16
    tensor_index = lax.axis_index("tensor")
    local_rows, width = tokens.shape
    group_rows = local_rows * nt
    seq_count = SEQS_DEV
    seq_len = group_rows // seq_count
    kv_cols = KVHEADS * HEAD_SIZE
    local_heads = step_proj.shape[1]
    lanes = width // nd
    units = down_proj.shape[0]
    small_parts = [channel_taps, mixer_gain, norm_gains, shared_taps]
    flat = jnp.concatenate([p.reshape(-1) for p in small_parts])
    small_len = -(-flat.shape[0] // 2048) * 2048
    small = jnp.pad(flat, (0, small_len - flat.shape[0])).reshape(-1, 128)
    (tok_full, full_query, full_attend, full_inner, full_step, full_mamba, sha, sma) = gather_start(
        tokens, query_proj, attend_out, inner_proj, step_proj, mamba_out, shared_proj, small, nd, nt
    )
    hid_in, down_in, tok_full = lax.optimization_barrier((hidden_proj, down_proj, tok_full))
    full_hidden = lax.all_gather(hid_in, "tensor", axis=2, tiled=True)
    full_hidden = lax.all_gather(full_hidden, "dp", axis=1, tiled=True)
    full_down = lax.all_gather(down_in, "tensor", axis=0, tiled=True)
    full_down = lax.all_gather(full_down, "dp", axis=1, tiled=True)

    full_shared = sha.reshape(width, -1)
    sma = sma.reshape(nd, nt, small_len)

    def small_piece(index):
        start = sum(p.size for p in small_parts[:index])
        part = small_parts[index]
        return sma[:, :, start : start + part.size].reshape((nd, nt) + part.shape)

    mine_taps = pick(small_piece(0), tensor_index, 1)
    full_taps = mine_taps.transpose(1, 2, 0, 3)
    full_gain = pick(small_piece(1), tensor_index, 1).transpose(1, 0, 2)
    full_norms = small_piece(2).transpose(2, 0, 1, 3).reshape(2, width)
    full_stap = small_piece(3).transpose(2, 0, 1, 3).reshape(CONV + 1, -1)
    taps_inner = full_taps.astype(f32).reshape(CONV + 1, local_heads * SSM_DIM)
    taps_shared = full_stap.astype(f32)
    gain_mix = full_gain.astype(f32).reshape(local_heads * SSM_DIM)
    gain_first = full_norms[0].astype(f32)
    gain_second = full_norms[1].astype(f32)

    token_f32 = tokens.astype(f32)
    group_one = norm_apply(tok_full.reshape(group_rows, width).astype(f32), gain_first).astype(bf16)
    query_raw = matmul(group_one, full_query)
    shared_raw = matmul(group_one, full_shared)
    gate_raw = matmul(group_one, full_inner[0])
    signal_raw = matmul(group_one, full_inner[1])
    step_raw = matmul(group_one, full_step)
    q_heads = query_raw.shape[1] // HEAD_SIZE
    kv_head = tensor_index * q_heads // (QHEADS // KVHEADS)
    cosine, sine = rope_tables(seq_len, HEAD_SIZE)
    query_rot = rotate(
        query_raw.reshape(seq_count, seq_len, q_heads, HEAD_SIZE), cosine, sine
    ).astype(bf16)
    key_raw = lax.dynamic_slice_in_dim(shared_raw, kv_head * HEAD_SIZE, HEAD_SIZE, 1)
    value_raw = lax.dynamic_slice_in_dim(shared_raw, kv_cols + kv_head * HEAD_SIZE, HEAD_SIZE, 1)
    key_rot = rotate(key_raw.reshape(seq_count, seq_len, 1, HEAD_SIZE), cosine, sine)[
        :, :, 0
    ].astype(bf16)
    value_low = value_raw.reshape(seq_count, seq_len, HEAD_SIZE).astype(bf16)
    attended, log_sums = lax.map(attend_forward, (query_rot, key_rot, value_low))
    attended_flat = attended.reshape(group_rows, q_heads * HEAD_SIZE)
    mix_part = matmul(attended_flat, full_attend)
    mixed_in, mixer_back = jax.vjp(
        partial(mixer_local, num_seq=seq_count),
        gate_raw,
        signal_raw,
        step_raw,
        shared_raw[:, 2 * kv_cols :],
        taps_inner,
        taps_shared,
        decay_log.astype(f32),
        step_bias.astype(f32),
        skip_weight.astype(f32),
    )
    square_sum = tensor_total(jnp.sum(mixed_in * mixed_in, axis=1))
    inv_rms = lax.rsqrt(square_sum / INNER + epsilon)[:, None]
    mamba_low = (mixed_in * inv_rms * gain_mix).astype(bf16)
    mix_part = mix_part + matmul(mamba_low, full_mamba)
    hidden = token_f32 + chain_scatter(mix_part.astype(bf16).reshape(nt, local_rows, width), nt)
    normed_two, norm_two_back = jax.vjp(norm_apply, hidden, gain_second)
    local_two = normed_two.astype(bf16)
    gate_val = matmul(local_two, full_hidden[0])
    up_val = matmul(local_two, full_hidden[1])
    sigmoid_gate = jax.nn.sigmoid(gate_val)
    inner_low = (gate_val * sigmoid_gate * up_val).astype(bf16)
    hidden_out = hidden + matmul(inner_low, full_down)
    layer_out = hidden_out.astype(bf16)
    grad_inner_units = right_contract(cotangent, full_down)
    grad_up = (grad_inner_units * gate_val * sigmoid_gate).astype(bf16)
    grad_gate = (
        grad_inner_units * up_val * sigmoid_gate * (1.0 + gate_val * (1.0 - sigmoid_gate))
    ).astype(bf16)
    grad_normed_two = right_contract(grad_gate, full_hidden[0]) + right_contract(
        grad_up, full_hidden[1]
    )
    grad_from_two, grad_gain_two = norm_two_back(grad_normed_two)
    grad_resid = cotangent.astype(f32) + grad_from_two
    grad_mix = chain_gather(grad_resid.astype(bf16), nt).reshape(group_rows, width)
    grad_down = left_contract(inner_low, cotangent)
    grad_hidden = jnp.stack([left_contract(local_two, grad_gate), left_contract(local_two, grad_up)])
    hidden_rows = width // nd
    hid_pieces = (
        grad_hidden.astype(bf16)
        .reshape(2, nd, hidden_rows, nt, units)
        .transpose(1, 3, 0, 2, 4)
        .reshape(nd, nt, 2 * hidden_rows, units)
    )
    down_pieces = (
        grad_down.astype(bf16).reshape(nt, units, nd, lanes).transpose(2, 0, 1, 3)
    )
    hid_sum = cube_scatter(hid_pieces, nd, bf16)
    down_sum = cube_scatter(down_pieces, nd, bf16)
    gradient_hidden = chain_scatter(hid_sum, nt).reshape(2, hidden_rows, units)
    gradient_down = chain_scatter(down_sum, nt)

    grad_attend = left_contract(attended_flat, grad_mix)
    grad_attended = right_contract(grad_mix, full_attend).astype(bf16)
    grad_attended = grad_attended.reshape(seq_count, seq_len, q_heads, HEAD_SIZE)
    query_back, key_back, value_back = lax.map(
        attend_backward, (query_rot, key_rot, value_low, log_sums, grad_attended)
    )
    grad_query_raw = (
        rotate(query_back, cosine, -sine).reshape(group_rows, q_heads * HEAD_SIZE).astype(bf16)
    )
    grad_key_raw = rotate(key_back[:, :, None], cosine, -sine).reshape(group_rows, HEAD_SIZE)
    grad_value_raw = value_back.reshape(group_rows, HEAD_SIZE)
    grad_query = left_contract(group_one, grad_query_raw)
    part_one = right_contract(grad_query_raw, full_query)
    grad_mamba = left_contract(mamba_low, grad_mix)
    grad_normed_mix = right_contract(grad_mix, full_mamba)
    scaled_grad = grad_normed_mix * gain_mix
    grad_gain_mix = jnp.sum(grad_normed_mix * mixed_in * inv_rms, axis=0)
    inner_dot = tensor_total(jnp.sum(scaled_grad * mixed_in, axis=1))
    grad_mixed = inv_rms * scaled_grad - mixed_in * inv_rms**3 * (inner_dot / INNER)[:, None]
    (
        grad_gate_raw,
        grad_signal_raw,
        grad_step_raw,
        grad_pair_raw,
        grad_taps_inner,
        grad_taps_shared,
        grad_decay,
        grad_bias,
        grad_skip,
    ) = mixer_back(grad_mixed)
    gate_low = grad_gate_raw.astype(bf16)
    signal_low = grad_signal_raw.astype(bf16)
    step_low = grad_step_raw.astype(bf16)
    grad_gate_w = left_contract(group_one, gate_low)
    grad_signal_w = left_contract(group_one, signal_low)
    grad_step = left_contract(group_one, step_low)
    kv_grad = jnp.zeros((group_rows, 2 * kv_cols), f32)
    kv_grad = lax.dynamic_update_slice_in_dim(kv_grad, grad_key_raw, kv_head * HEAD_SIZE, 1)
    kv_grad = lax.dynamic_update_slice_in_dim(
        kv_grad, grad_value_raw, kv_cols + kv_head * HEAD_SIZE, 1
    )
    shared_low = jnp.concatenate([kv_grad, grad_pair_raw], axis=1).astype(bf16)
    grad_shared = left_contract(group_one, shared_low)
    part_one = (
        part_one
        + right_contract(gate_low, full_inner[0])
        + right_contract(signal_low, full_inner[1])
        + right_contract(step_low, full_step)
        + right_contract(shared_low, full_shared)
    )
    grad_normed_one = chain_scatter(part_one.astype(bf16).reshape(nt, local_rows, width), nt)
    _, norm_one_back = jax.vjp(norm_apply, token_f32, gain_first)
    grad_from_one, grad_gain_one = norm_one_back(grad_normed_one)
    gradient_tokens = (grad_resid + grad_from_one).astype(bf16)

    block = width // nd

    def by_rows(values):
        c = values.shape[1]
        values = values.astype(bf16).reshape(nd, block, c // 128, 128)
        return values.transpose(0, 2, 1, 3).reshape(nd, -1, 128)

    def by_lanes(values):
        r = values.shape[0]
        values = values.astype(bf16).reshape(r, nd, block).transpose(1, 0, 2)
        return values.reshape(nd, r * block // 128, 128)

    step_wide = jnp.pad(grad_step, ((0, 0), (0, 128 - local_heads)))
    pieces = [
        by_rows(grad_query),
        by_lanes(grad_attend),
        by_rows(grad_gate_w),
        by_rows(grad_signal_w),
        by_rows(step_wide),
        by_lanes(grad_mamba),
    ]
    sizes = [p.shape[1] for p in pieces]
    mixer_sum = cube_scatter(jnp.concatenate(pieces, axis=1), nd)
    cuts = [sum(sizes[:i]) for i in range(len(sizes) + 1)]
    got = [mixer_sum[cuts[i] : cuts[i + 1]] for i in range(len(sizes))]

    def back_rows(values):
        return values.reshape(-1, block, 128).transpose(1, 0, 2).reshape(block, -1)

    gradient_query = back_rows(got[0])
    gradient_attend = got[1].reshape(-1, block)
    gradient_inner = jnp.stack([back_rows(got[2]), back_rows(got[3])])
    gradient_step = back_rows(got[4])[:, :local_heads]
    gradient_mamba = got[5].reshape(-1, block)
    shared_cut = grad_shared.astype(bf16).reshape(nd, nt, -1, grad_shared.shape[1])
    gradient_shared = chain_scatter(cube_scatter(shared_cut, nd, bf16), nt)

    over_all = jnp.concatenate([grad_gain_one, grad_gain_two, grad_taps_shared.reshape(-1)])
    over_dp = jnp.concatenate(
        [grad_taps_inner.reshape(-1), grad_gain_mix, grad_decay, grad_bias, grad_skip]
    )
    n_all = over_all.shape[0]
    over_dp = lax.psum(jnp.concatenate([over_all, over_dp]), "dp")
    over_all = lax.psum(over_dp[:n_all], "tensor")
    over_dp = over_dp[n_all:]
    d = lax.axis_index("dp")
    place = d * nt + tensor_index
    norm_w = width // (nd * nt)
    gradient_norms = lax.dynamic_slice_in_dim(
        over_all[: 2 * width].reshape(2, width), place * norm_w, norm_w, 1
    )
    tap_all = over_all[2 * width :].reshape(CONV + 1, -1)
    tap_w = shared_taps.shape[1]
    gradient_taps = lax.dynamic_slice_in_dim(tap_all, place * tap_w, tap_w, 1)
    n_taps = (CONV + 1) * local_heads * SSM_DIM
    n_gain = local_heads * SSM_DIM
    chan = over_dp[:n_taps].reshape(CONV + 1, local_heads, SSM_DIM)
    gain = over_dp[n_taps : n_taps + n_gain].reshape(local_heads, SSM_DIM)
    part = mixer_gain.shape[1]
    gradient_channel = lax.dynamic_slice_in_dim(chan, d * part, part, 2)
    gradient_mixer = lax.dynamic_slice_in_dim(gain, d * part, part, 1)
    rest = over_dp[n_taps + n_gain :]
    gradient_decay = rest[:local_heads]
    gradient_bias = rest[local_heads : 2 * local_heads]
    gradient_skip = rest[2 * local_heads :]
    return (
        layer_out,
        gradient_tokens,
        gradient_query,
        gradient_attend,
        gradient_inner,
        gradient_step,
        gradient_mamba,
        gradient_hidden,
        gradient_down,
        gradient_channel,
        gradient_mixer,
        gradient_decay,
        gradient_bias,
        gradient_skip,
        gradient_shared,
        gradient_norms,
        gradient_taps,
    )


def solution(mesh):
    placed = (
        P(("dp", "tensor"), None),
        P("dp", "tensor"),
        P("tensor", "dp"),
        P(None, "dp", "tensor"),
        P("dp", "tensor"),
        P("tensor", "dp"),
        P(None, "dp", "tensor"),
        P("tensor", "dp"),
        P(None, "tensor", "dp"),
        P("tensor", "dp"),
        P("tensor"),
        P("tensor"),
        P("tensor"),
        P(("dp", "tensor"), None),
        P(None, ("dp", "tensor")),
        P(None, ("dp", "tensor")),
        P(("dp", "tensor"), None),
    )
    return jax.shard_map(
        partial(per_device, mesh.shape["dp"], mesh.shape["tensor"]),
        mesh=mesh,
        in_specs=placed,
        out_specs=(
            P(("dp", "tensor"), None),
            P(("dp", "tensor"), None),
            P("dp", "tensor"),
            P("tensor", "dp"),
            P(None, "dp", "tensor"),
            P("dp", "tensor"),
            P("tensor", "dp"),
            P(None, "dp", "tensor"),
            P("tensor", "dp"),
            P(None, "tensor", "dp"),
            P("tensor", "dp"),
            P("tensor"),
            P("tensor"),
            P("tensor"),
            P(("dp", "tensor"), None),
            P(None, ("dp", "tensor")),
            P(None, ("dp", "tensor")),
        ),
        check_vma=False,
    )
```

time: 1480 us -> 886 us (0.60)
  waiting for transfers between devices: 817 us -> 118 us
  blocking collectives: 277 us -> 97.6 us
  starting transfers between devices: 1.75 us -> 101 us
  local copies, waits for them, and re-layouts: 128 us -> 226 us
  Pallas kernels: 0 us -> 49.2 us
  other arithmetic: 89.4 us -> 117 us
    reduce_scatter x13 -> x0, waiting for transfers between devices: 563 us -> none  [the longest x1 141 us: per_device(): lax.psum_scatter(grad_shared, ('dp', 'tensor'), scatter_dimension=0, tile...]
    all_gather x8 -> x3, waiting for transfers between devices: 176 us -> 0.02 us  [the longest x1 0.02 us: per_device(): full_down = lax.all_gather(full_down, 'dp', axis=1, tiled=True)]
    all_gather x8 -> x1, blocking collectives: 192 us -> 20.6 us  [per_device(): full_down = lax.all_gather(down_in, 'tensor', axis=0, tiled=True)]
    ppermute x0 -> x56, waiting for transfers between devices: none -> 118 us  [the longest x20 55.3 us: swap(): return lax.ppermute(values, 'dp', [(i, i ^ bit) for i in range(8)])]
    ppermute x0 -> x56, starting transfers between devices: none -> 101 us  [the longest x15 58.4 us: chain_scatter(): right = lax.ppermute(to_right, 'tensor', [(i, i + 1) for i in range(t + 1)])]
    unnamed x23 -> x3, waiting for transfers between devices: 78.1 us -> 0.05 us
    unnamed x2 -> x0, blocking collectives: 63.7 us -> none
    psum x0 -> x2, blocking collectives: none -> 58.1 us  [the longest x1 35.7 us: per_device(): over_dp = lax.psum(jnp.concatenate([over_all, over_dp]), 'dp')]
  transfers between devices with their start and end apart: 22 -> 59, of which waited for: 17 -> 23; matrix products, arithmetic and copies ran while one was open for 8% -> 51% of each run, Pallas kernels for 0% -> 0%
where the time goes in v1:
time: 886 us; the launch traced here: 871 us
  local copies, waits for them, and re-layouts  226 us (26%)
  matrix products  144 us (16%)
  waiting for transfers between devices  118 us (13%)
  other arithmetic  117 us (13%)
  starting transfers between devices  101 us (11%)
  blocking collectives  97.6 us (11%)
  Pallas kernels  49.2 us (6%)
  between operations  17.2 us (2%)
    ppermute x15, starting transfers between devices, chain_scatter(): right = lax.ppermute(to_right, 'tensor', [(i, i + 1) for i in range(t + 1)])  58.4 us
    ppermute x20, waiting for transfers between devices, swap(): return lax.ppermute(values, 'dp', [(i, i ^ bit) for i in range(8)])  55.3 us
    pallas_call x1, Pallas kernels, gather_start(): pl.pallas_call(partial(gather_kernel, nt), out_shape=[jax.ShapeDtypeStruc...  49.2 us
    dynamic_slice x32, local copies, waits for them, and re-layouts, duality_scan(): finished, entering = lax.scan(advance, start, (block_fade, contrib))  36.6 us
    psum x1, blocking collectives, per_device(): over_dp = lax.psum(jnp.concatenate([over_all, over_dp]), 'dp')  35.7 us
    unnamed x427, local copies, waits for them, and re-layouts  34.7 us
    dot_general x10, matrix products, right_contract(): jnp.einsum('mk,dk->md', left, right, preferred_element_type=jnp.float32)  31.2 us
    another operation x4, local copies, waits for them, and re-layouts, per_device(): jnp.stack([left_contract(local_two, grad_gate), left_contract(local_two,...  26.3 us
  transfers between devices with their start and end apart: 59, of which 23 were waited for; matrix products, arithmetic and copies ran while one was open for 51% of the time, Pallas kernels for 0%

profile of v1, /device:TPU:0, one launch (start us, length us, event | category | flops | bytes accessed | tf_op | source)
XLA Modules:
  0.0 870.8 jit_solution(17782263414816607018)
XLA Ops:
  12.4 49.2 %gather_start.1 = (bf16[4,256,1024]{2,1,0:T(8,128)(2,1)}, bf16[1024,128]{1,0:T(8,128)(2,1)}, bf16[128,1024]{1,0:T(8,128)(2,1)}, bf16[2,1024,384]{2,1,0:T(8,128)(...) custom-call(bf16[256,1024]{1,0:T(8,128)(2,1)} %refs_0_.1, ...), custom_call_target="tpu_custom_call" | custom-call | tf_op jit(solution)/shard_map/gather_start/pallas_call | solution.py:353
  61.7 20.6 %all_gather.14 = bf16[2048,128]{1,0:T(8,128)(2,1)} all-gather(bf16[512,128]{1,0:T(8,128)(2,1)} %param.28), channel_id=1, replica_groups=mesh['dp'=8,'tensor'=4] {'tensor'}, dimensions={0}, use_global_device_ids=true | all-gather | bytes 655360 | tf_op jit(solution)/shard_map/all_gather | solution.py:494
  123.7 52.2 %while.11 = (s32[]{:T(128)}, f32[1,6,128,64]{3,2,1,0:T(8,128)S(1)}, f32[8,1,6,128,64]{4,3,2,1,0:T(8,128)S(1)}, f32[8,1,6,1,1]{2,4,3,1,0:T(1,128)}, f32[8,1,6]{2,...) while((s32[]{:T(128)}, f32[1,6,128,64]{3,2,1,0:T(8,128)S(1)}, ...), condition=%wide.region_5.6_spmd.clone, body=%wide.region_4.5_spmd.clone.sunk | while | flops 196611 | bytes 2163904 | solution.py:87
  184.2 6.4 bitcast_add_fusion.3
  193.0 3.2 copy.571
  196.6 5.5 multiply_reduce_fusion.9
  202.2 10.3 %psum.28 = f32[1024]{0:T(1024)S(1)} all-reduce(f32[1024]{0:T(1024)S(1)} %get-tuple-element.582), channel_id=1, replica_groups=mesh['dp'=8,'tensor'=4] {'tensor'}, use_global_device_ids=true, to_apply=%region_7.8 | all-reduce | flops 1024 | bytes 8192 | tf_op jit(solution)/shard_map/psum | solution.py:438
  232.1 8.3 collective-permute-done
  240.6 4.4 collective-permute-start.1
  245.0 7.3 collective-permute-done.1
  255.3 5.8 collective-permute-start.2
  263.0 4.9 copy.586
  270.7 12.3 %collective-permute-done.5 = bf16[256,1024]{1,0:T(8,128)(2,1)} collective-permute-done((bf16[256,1024]{1,0:T(8,128)(2,1)S(1)}, bf16[256,1024]{1,0:T(8,128)(2,1)}, u32[]{:S(2)}, u32[]{:S(2)}) %collective-permute-start.5) | collective-permute-done | bytes 524320 | tf_op jit(solution)/shard_map/ppermute | solution.py:407
  285.7 5.1 convolution_bitcast_fusion
  290.8 3.6 fusion.19
  294.4 5.5 multiply_convert_fusion.2
  305.9 4.7 collective-permute-start.6
  312.4 3.4 convolution_convert_fusion
  315.8 3.3 convolution_convert_fusion.1
  319.1 7.8 stack.14
  326.9 5.3 copy.623
  332.2 7.8 stack.13
  340.0 5.4 copy.622
  345.4 7.6 pad_maximum_fusion
  353.0 4.7 dynamic-slice_bitcast_fusion
  360.1 9.7 %constant_dynamic-slice_fusion.9 = (bf16[4,1,4,512,128]{4,1,0,3,2:T(2,128)(2,1)}, bf16[4,1,4,512,128]{4,1,0,3,2:T(2,128)(2,1)S(1)}) fusion(bf16[4,2,4,512,128]{4,1,0,3,2:T(2,128)(2,1)S(1)} %bitcast.843, s32[]{:T(128)S(6)} %select_n.315, s32[]{:T(128)S(6)} %select_n.316), kind=kLoop, calls=%fused_computation.500 | loop fusion | bytes 8388616 | tf_op jit(solution)/shard_map/jit(dynamic_index_in_dim)/dynamic_slice | solution.py:368
  379.5 11.2 %collective-permute-done.9 = bf16[256,1024]{1,0:T(8,128)(2,1)S(1)} collective-permute-done((bf16[256,1024]{1,0:T(8,128)(2,1)}, bf16[256,1024]{1,0:T(8,128)(2,1)S(1)}, u32[]{:S(2)}, u32[]{:S(2)}) %collective-permute-start.9) | collective-permute-done | bytes 524320 | tf_op jit(solution)/shard_map/ppermute | solution.py:382
  392.9 12.9 %collective-permute-done.11 = bf16[256,1024]{1,0:T(8,128)(2,1)S(1)} collective-permute-done((bf16[256,1024]{1,0:T(8,128)(2,1)S(1)}, bf16[256,1024]{1,0:T(8,128)(2,1)S(1)}, u32[]{:S(2)}, u32[]{:S(2)}) %collective-permute-start.11) | collective-permute-done | bytes 524320 | tf_op jit(solution)/shard_map/ppermute | solution.py:382
  406.0 3.1 multiply_reduce_fusion.2
  409.1 8.6 psum.29
  417.7 5.6 fusion.45
  434.6 30.1 %while.46 = (s32[]{:T(128)}, f32[1,6,128,64]{3,2,1,0:T(8,128)S(1)}, f32[8,1,6]{2,1,0:T(1,128)S(1)}, f32[8,1,6,128,64]{4,3,2,1,0:T(8,128)}, f32[8,1,6,128,64]{3,4...) while((s32[]{:T(128)}, f32[1,6,128,64]{3,2,1,0:T(8,128)S(1)}, ...), condition=%wide.region_15.16_spmd.clone, body=%wide.region_13.15_spmd.clone.sunk | while | flops 294910 | bytes 2163960 | solution.py:87
  464.8 8.8 %fusion.43 = (f32[8,128,6]{1,2,0:T(8,128)S(1)}, f32[8,6,64,128]{3,2,1,0:T(8,128)}) fusion(f32[1,8,128,6,64]{2,1,0,4,3:T(8,128)} %bitcast.897, f32[8,128,128,1]{2,1,3,0:T(8,128)} %bitcast.880, f32[8,1,6,128,64]{4,3,2,1,0:T(8,128)} %get-tuple-element.261), kind=kOutput, calls=%fused_computation.120 | convolution fusion | flops 604760064 | bytes 5267456 | tf_op jit(solution)/shard_map/transpose(jvp(vmap(cjn,cjhp->chnp)))/dot_general | solution.py:79
  476.1 8.0 fusion.71
  484.1 5.6 fusion.4
  499.9 3.3 fusion.122
  505.5 8.3 fusion.36
  513.9 3.7 bitcast_add_fusion.2
  519.9 3.1 copy.584
  523.0 6.4 multiply_reduce_fusion.6
  531.2 3.2 fusion.126
  540.0 3.7 fusion.146
  556.7 5.4 fusion.83
  568.7 3.5 dynamic_update_slice.58
  577.7 6.6 add_convert_fusion
  585.4 4.8 collective-permute-start.12
  606.3 3.3 convolution_convert_fusion.2
  620.9 3.8 collective-permute-done.46
  629.2 7.8 collective-permute-done.49
  640.3 4.2 collective-permute-start.51
  645.4 7.5 collective-permute-done.37
  655.3 4.0 collective-permute-done.36
  662.2 3.9 collective-permute-start.52
  667.0 3.0 collective-permute-start.39
  680.6 4.7 collective-permute-done.13
  687.6 6.5 collective-permute-start.14
  695.6 5.8 collective-permute-start.41
  718.4 3.6 fusion.3
  728.6 35.7 %psum.30 = f32[5650]{0:T(1024)} all-reduce(f32[5650]{0:T(1024)} %concatenate.88), channel_id=1, replica_groups=mesh['dp'=8,'tensor'=4] {'dp'}, use_global_device_ids=true, to_apply=%region_43.44 | all-reduce | flops 5650 | bytes 45200 | tf_op jit(solution)/shard_map/psum | solution.py:688
  769.7 22.4 %psum.31 = f32[3328]{0:T(1024)} all-reduce(f32[3328]{0:T(1024)} %slice.331), channel_id=1, replica_groups=mesh['dp'=8,'tensor'=4] {'tensor'}, use_global_device_ids=true, to_apply=%region_44.45 | all-reduce | flops 3328 | bytes 26624 | tf_op jit(solution)/shard_map/psum | solution.py:689
  803.8 16.7 %collective-permute-done.26 = bf16[2,2,256,512]{3,2,1,0:T(8,128)(2,1)S(1)} collective-permute-done((bf16[2,2,256,512]{3,2,1,0:T(8,128)(2,1)S(1)}, bf16[2,2,256,512]{3,2,1,0:T(8,128)(2,1)S(1)}, u32[]{:S(2)}, u32[]{:S(2)}) %collective-permute-start.26) | collective-permute-done | bytes 1048608 | tf_op jit(solution)/shard_map/ppermute | solution.py:421
  827.4 3.7 collective-permute-done.27
  838.7 4.4 collective-permute-start.29
  851.9 7.4 collective-permute-start.30
  (890 shorter events, 376.3 us)
Async XLA Ops:
  7.2 116.1 %all-gather.4.cloned.1.call-start = ((), (), s32[]{:S(2)}) async-start(), calls=%async_computation | async-start | bytes 1310720 | tf_op jit(solution)/shard_map/all_gather | solution.py:492
  61.6 24.6 %copy-start.12 = (bf16[4,256,1024]{2,1,0:T(8,128)(2,1)S(1)}, bf16[4,256,1024]{2,1,0:T(8,128)(2,1)}, u32[]{:S(2)}) copy-start(bf16[4,256,1024]{2,1,0:T(8,128)(2,1)} %get-tuple-element.249) | copy-start | bytes 6291460
  61.6 224.0 %all-gather.8.cloned.1.call-start = ((), (), s32[]{:S(2)}) async-start(), calls=%async_computation.2 | async-start | bytes 4718592 | tf_op jit(solution)/shard_map/all_gather | solution.py:495
  82.3 208.5 %all-gather.6.cloned.1.call-start = ((), (), s32[]{:S(2)}) async-start(), calls=%async_computation.1 | async-start | bytes 9437184 | tf_op jit(solution)/shard_map/all_gather | solution.py:493
  86.2 129.1 %copy-start.116 = (f32[1024]{0:T(1024)}, f32[1024]{0:T(1024)S(1)}, u32[]{:S(2)}) copy-start(f32[1024]{0:T(1024)S(1)} %reshape.1302) | copy-start | bytes 12292
  228.6 11.8 %collective-permute-start = (bf16[256,1024]{1,0:T(8,128)(2,1)S(1)}, bf16[256,1024]{1,0:T(8,128)(2,1)S(1)}, u32[]{:S(2)}, u32[]{:S(2)}) collective-permute-start(bf16[256,1024]{1,0:T(8,128)(2,1)S(1)} %get-tuple-element.606), channel_id=1, source_target_pairs={{0,1},{4,5},{8,9},{12,13},{16,17},{20,21},{24,25},{28,29}} | collective-permute-start | bytes 1572872 | tf_op jit(solution)/shard_map/ppermute | solution.py:406
  230.6 14.4 %collective-permute-start.3 = (bf16[256,1024]{1,0:T(8,128)(2,1)}, bf16[256,1024]{1,0:T(8,128)(2,1)}, u32[]{:S(2)}, u32[]{:S(2)}) collective-permute-start(bf16[256,1024]{1,0:T(8,128)(2,1)} %get-tuple-element.607), channel_id=1, source_target_pairs={{3,2},{7,6},{11,10},{15,14},{19,18},{23,22},{27,26},{31,30}} | collective-permute-start | bytes 1572872 | tf_op jit(solution)/shard_map/ppermute | solution.py:407
  240.6 11.7 %collective-permute-start.1 = (bf16[256,1024]{1,0:T(8,128)(2,1)S(1)}, bf16[256,1024]{1,0:T(8,128)(2,1)S(1)}, u32[]{:S(2)}, u32[]{:S(2)}) collective-permute-start(bf16[256,1024]{1,0:T(8,128)(2,1)S(1)} %fusion.115), channel_id=1, source_target_pairs={{0,1},{1,2},{4,5},{5,6},{8,9},{9,10},{12,13},{13,14},{16,17},{17,1... | collective-permute-start | bytes 1572872 | tf_op jit(solution)/shard_map/ppermute | solution.py:406
  254.6 6.5 collective-permute-start.4
  255.3 15.4 %collective-permute-start.2 = (bf16[256,1024]{1,0:T(8,128)(2,1)}, bf16[256,1024]{1,0:T(8,128)(2,1)}, u32[]{:S(2)}, u32[]{:S(2)}) collective-permute-start(bf16[256,1024]{1,0:T(8,128)(2,1)} %get-tuple-element.604), channel_id=1, source_target_pairs={{0,1},{1,2},{2,3},{4,5},{5,6},{6,7},{8,9},{9,10},{10,11},{12,13},{... | collective-permute-start | bytes 1572872 | tf_op jit(solution)/shard_map/ppermute | solution.py:406
  261.3 21.6 %collective-permute-start.5 = (bf16[256,1024]{1,0:T(8,128)(2,1)S(1)}, bf16[256,1024]{1,0:T(8,128)(2,1)}, u32[]{:S(2)}, u32[]{:S(2)}) collective-permute-start(bf16[256,1024]{1,0:T(8,128)(2,1)S(1)} %fusion.114), channel_id=1, source_target_pairs={{3,2},{2,1},{1,0},{7,6},{6,5},{5,4},{11,10},{10,9},{9,8},{15,14},{... | collective-permute-start | bytes 1572872 | tf_op jit(solution)/shard_map/ppermute | solution.py:407
  284.8 89.5 %copy-start.13 = (f32[256,1024]{1,0:T(8,128)}, f32[256,1024]{1,0:T(8,128)S(1)}, u32[]{:S(2)}) copy-start(f32[256,1024]{1,0:T(8,128)S(1)} %get-tuple-element.581) | copy-start | bytes 3145732
  305.9 66.3 %collective-permute-start.6 = (bf16[256,1024]{1,0:T(8,128)(2,1)}, bf16[256,1024]{1,0:T(8,128)(2,1)}, u32[]{:S(2)}, u32[]{:S(2)}) collective-permute-start(bf16[256,1024]{1,0:T(8,128)(2,1)} %get-tuple-element.579), channel_id=1, source_target_pairs={{0,1},{1,2},{2,3},{4,5},{5,6},{6,7},{8,9},{9,10},{10,11},{12,13},{... | collective-permute-start | bytes 1572872 | tf_op jit(solution)/shard_map/ppermute | solution.py:381
  310.6 62.3 %collective-permute-start.7 = (bf16[256,1024]{1,0:T(8,128)(2,1)}, bf16[256,1024]{1,0:T(8,128)(2,1)}, u32[]{:S(2)}, u32[]{:S(2)}) collective-permute-start(bf16[256,1024]{1,0:T(8,128)(2,1)} %get-tuple-element.579), channel_id=1, source_target_pairs={{1,0},{2,1},{3,2},{5,4},{6,5},{7,6},{9,8},{10,9},{11,10},{13,12},{... | collective-permute-start | bytes 1572872 | tf_op jit(solution)/shard_map/ppermute | solution.py:382
  357.7 360.7 %collective-permute-start.23 = (bf16[4,4,256,512]{3,2,1,0:T(8,128)(2,1)}, bf16[4,4,256,512]{3,2,1,0:T(8,128)(2,1)}, u32[]{:S(2)}, u32[]{:S(2)}) collective-permute-start(bf16[4,4,256,512]{3,2,1,0:T(8,128)(2,1)} %dynamic-slice_bitcast_fusion), channel_id=1, source_target_pairs={{0,4},{4,0},{8,12},{12,8},{16,20},{20,16},{24,28},{28,24},{1,5},{5... | collective-permute-start | bytes 12582920 | tf_op jit(solution)/shard_map/ppermute | solution.py:421
  371.7 242.2 %collective-permute-start.34 = (bf16[4,4,512,128]{3,2,1,0:T(8,128)(2,1)}, bf16[4,4,512,128]{3,2,1,0:T(8,128)(2,1)}, u32[]{:S(2)}, u32[]{:S(2)}) collective-permute-start(bf16[4,4,512,128]{3,2,1,0:T(8,128)(2,1)} %bitcast.816), channel_id=1, source_target_pairs={{0,4},{4,0},{8,12},{12,8},{16,20},{20,16},{24,28},{28,24},{1,5},{5... | collective-permute-start | bytes 6291464 | tf_op jit(solution)/shard_map/ppermute | solution.py:421
  372.2 5.3 collective-permute-start.8
  372.9 17.8 %collective-permute-start.9 = (bf16[256,1024]{1,0:T(8,128)(2,1)}, bf16[256,1024]{1,0:T(8,128)(2,1)S(1)}, u32[]{:S(2)}, u32[]{:S(2)}) collective-permute-start(bf16[256,1024]{1,0:T(8,128)(2,1)} %collective-permute-done.7), channel_id=1, source_target_pairs={{1,0},{2,1},{5,4},{6,5},{9,8},{10,9},{13,12},{14,13},{17,16},{18,1... | collective-permute-start | bytes 1572872 | tf_op jit(solution)/shard_map/ppermute | solution.py:382
  377.6 15.1 %collective-permute-start.10 = (bf16[256,1024]{1,0:T(8,128)(2,1)S(1)}, bf16[256,1024]{1,0:T(8,128)(2,1)S(1)}, u32[]{:S(2)}, u32[]{:S(2)}) collective-permute-start(bf16[256,1024]{1,0:T(8,128)(2,1)S(1)} %collective-permute-done.8), channel_id=1, source_target_pairs={{2,3},{6,7},{10,11},{14,15},{18,19},{22,23},{26,27},{30,31}} | collective-permute-start | bytes 1572872 | tf_op jit(solution)/shard_map/ppermute | solution.py:381
  390.8 15.0 %collective-permute-start.11 = (bf16[256,1024]{1,0:T(8,128)(2,1)S(1)}, bf16[256,1024]{1,0:T(8,128)(2,1)S(1)}, u32[]{:S(2)}, u32[]{:S(2)}) collective-permute-start(bf16[256,1024]{1,0:T(8,128)(2,1)S(1)} %collective-permute-done.9), channel_id=1, source_target_pairs={{1,0},{5,4},{9,8},{13,12},{17,16},{21,20},{25,24},{29,28}} | collective-permute-start | bytes 1572872 | tf_op jit(solution)/shard_map/ppermute | solution.py:382
  585.4 81.6 %collective-permute-start.12 = (bf16[256,1024]{1,0:T(8,128)(2,1)}, bf16[256,1024]{1,0:T(8,128)(2,1)}, u32[]{:S(2)}, u32[]{:S(2)}) collective-permute-start(bf16[256,1024]{1,0:T(8,128)(2,1)} %get-tuple-element.602), channel_id=1, source_target_pairs={{0,1},{4,5},{8,9},{12,13},{16,17},{20,21},{24,25},{28,29}} | collective-permute-start | bytes 1572872 | tf_op jit(solution)/shard_map/ppermute | solution.py:406
  609.6 8.5 collective-permute-start.45
  618.4 6.4 collective-permute-start.46
  618.5 26.0 %collective-permute-start.35 = (bf16[2,2,512,128]{3,2,1,0:T(8,128)(2,1)S(1)}, bf16[2,2,512,128]{3,2,1,0:T(8,128)(2,1)S(1)}, u32[]{:S(2)}, u32[]{:S(2)}) collective-permute-start(bf16[2,2,512,128]{3,2,1,0:T(8,128)(2,1)S(1)} %dynamic-slice_bitcast_fusion.6), channel_id=1, source_target_pairs={{0,8},{4,12},{8,0},{12,4},{16,24},{20,28},{24,16},{28,20},{1,9},{5... | collective-permute-start | bytes 1572872 | tf_op jit(solution)/shard_map/ppermute | solution.py:421
  620.6 5.4 collective-permute-start.48
  624.8 4.3 collective-permute-start.47
  626.1 10.9 %collective-permute-start.49 = (bf16[2,32,512]{2,1,0:T(8,128)(2,1)S(1)}, bf16[2,32,512]{2,1,0:T(8,128)(2,1)S(1)}, u32[]{:S(2)}, u32[]{:S(2)}) collective-permute-start(bf16[2,32,512]{2,1,0:T(8,128)(2,1)S(1)} %dynamic-slice_bitcast_fusion.21), channel_id=1, source_target_pairs={{0,8},{4,12},{8,0},{12,4},{16,24},{20,28},{24,16},{28,20},{1,9},{5... | collective-permute-start | bytes 196616 | tf_op jit(solution)/shard_map/ppermute | solution.py:421
  637.1 2.9 collective-permute-start.50
  638.4 1.8 collective-permute-start.53
  639.9 13.0 %collective-permute-start.37 = (bf16[2,2,512,128]{3,2,1,0:T(8,128)(2,1)S(1)}, bf16[2,2,512,128]{3,2,1,0:T(8,128)(2,1)S(1)}, u32[]{:S(2)}, u32[]{:S(2)}) collective-permute-start(bf16[2,2,512,128]{3,2,1,0:T(8,128)(2,1)S(1)} %dynamic-slice_bitcast_fusion.5), channel_id=1, source_target_pairs={{0,16},{4,20},{8,24},{12,28},{16,0},{20,4},{24,8},{28,12},{1,17},{... | collective-permute-start | bytes 1572872 | tf_op jit(solution)/shard_map/ppermute | solution.py:421
  640.3 13.1 %collective-permute-start.51 = (bf16[32,512]{1,0:T(8,128)(2,1)S(1)}, bf16[32,512]{1,0:T(8,128)(2,1)S(1)}, u32[]{:S(2)}, u32[]{:S(2)}) collective-permute-start(bf16[32,512]{1,0:T(8,128)(2,1)S(1)} %get-tuple-element.657), channel_id=1, source_target_pairs={{0,1},{1,2},{4,5},{5,6},{8,9},{9,10},{12,13},{13,14},{16,17},{17,1... | collective-permute-start | bytes 98312 | tf_op jit(solution)/shard_map/ppermute | solution.py:406
  644.5 9.0 %collective-permute-start.54 = (bf16[32,512]{1,0:T(8,128)(2,1)S(1)}, bf16[32,512]{1,0:T(8,128)(2,1)S(1)}, u32[]{:S(2)}, u32[]{:S(2)}) collective-permute-start(bf16[32,512]{1,0:T(8,128)(2,1)S(1)} %get-tuple-element.658), channel_id=1, source_target_pairs={{3,2},{2,1},{7,6},{6,5},{11,10},{10,9},{15,14},{14,13},{19,18},{18... | collective-permute-start | bytes 98312 | tf_op jit(solution)/shard_map/ppermute | solution.py:407
  652.9 6.4 collective-permute-start.36
  653.4 42.3 %collective-permute-start.18 = (bf16[4,1536,128]{2,1,0:T(8,128)(2,1)}, bf16[4,1536,128]{2,1,0:T(8,128)(2,1)}, u32[]{:S(2)}, u32[]{:S(2)}) collective-permute-start(bf16[4,1536,128]{2,1,0:T(8,128)(2,1)} %dynamic-slice_bitcast_fusion.1), channel_id=1, source_target_pairs={{0,4},{4,0},{8,12},{12,8},{16,20},{20,16},{24,28},{28,24},{1,5},{5... | collective-permute-start | bytes 4718600 | tf_op jit(solution)/shard_map/ppermute | solution.py:421
  653.5 8.7 %collective-permute-start.38 = (bf16[2,512,128]{2,1,0:T(8,128)(2,1)S(1)}, bf16[2,512,128]{2,1,0:T(8,128)(2,1)S(1)}, u32[]{:S(2)}, u32[]{:S(2)}) collective-permute-start(bf16[2,512,128]{2,1,0:T(8,128)(2,1)S(1)} %dynamic-slice_bitcast_fusion.15), channel_id=1, source_target_pairs={{0,8},{4,12},{8,0},{12,4},{16,24},{20,28},{24,16},{28,20},{1,9},{5... | collective-permute-start | bytes 786440 | tf_op jit(solution)/shard_map/ppermute | solution.py:421
  659.3 11.9 %collective-permute-start.55 = (bf16[32,512]{1,0:T(8,128)(2,1)S(1)}, bf16[32,512]{1,0:T(8,128)(2,1)S(1)}, u32[]{:S(2)}, u32[]{:S(2)}) collective-permute-start(bf16[32,512]{1,0:T(8,128)(2,1)S(1)} %get-tuple-element.656), channel_id=1, source_target_pairs={{3,2},{2,1},{1,0},{7,6},{6,5},{5,4},{11,10},{10,9},{9,8},{15,14},{... | collective-permute-start | bytes 98312 | tf_op jit(solution)/shard_map/ppermute | solution.py:407
  662.2 10.5 %collective-permute-start.52 = (bf16[32,512]{1,0:T(8,128)(2,1)S(1)}, bf16[32,512]{1,0:T(8,128)(2,1)S(1)}, u32[]{:S(2)}, u32[]{:S(2)}) collective-permute-start(bf16[32,512]{1,0:T(8,128)(2,1)S(1)} %get-tuple-element.655), channel_id=1, source_target_pairs={{0,1},{1,2},{2,3},{4,5},{5,6},{6,7},{8,9},{9,10},{10,11},{12,13},{... | collective-permute-start | bytes 98312 | tf_op jit(solution)/shard_map/ppermute | solution.py:406
  667.0 9.2 %collective-permute-start.39 = (bf16[512,128]{1,0:T(8,128)(2,1)}, bf16[512,128]{1,0:T(8,128)(2,1)S(1)}, u32[]{:S(2)}, u32[]{:S(2)}) collective-permute-start(bf16[512,128]{1,0:T(8,128)(2,1)} %get-tuple-element.636), channel_id=1, source_target_pairs={{0,1},{4,5},{8,9},{12,13},{16,17},{20,21},{24,25},{28,29}} | collective-permute-start | bytes 393224 | tf_op jit(solution)/shard_map/ppermute | solution.py:406
  671.3 8.5 collective-permute-start.15
  672.7 12.6 %collective-permute-start.13 = (bf16[256,1024]{1,0:T(8,128)(2,1)S(1)}, bf16[256,1024]{1,0:T(8,128)(2,1)}, u32[]{:S(2)}, u32[]{:S(2)}) collective-permute-start(bf16[256,1024]{1,0:T(8,128)(2,1)S(1)} %fusion.110), channel_id=1, source_target_pairs={{0,1},{1,2},{4,5},{5,6},{8,9},{9,10},{12,13},{13,14},{16,17},{17,1... | collective-permute-start | bytes 1572872 | tf_op jit(solution)/shard_map/ppermute | solution.py:406
  676.2 2.1 collective-permute-start.42
  678.5 9.2 %collective-permute-start.40 = (bf16[512,128]{1,0:T(8,128)(2,1)S(1)}, bf16[512,128]{1,0:T(8,128)(2,1)S(1)}, u32[]{:S(2)}, u32[]{:S(2)}) collective-permute-start(bf16[512,128]{1,0:T(8,128)(2,1)S(1)} %get-tuple-element.634), channel_id=1, source_target_pairs={{0,1},{1,2},{4,5},{5,6},{8,9},{9,10},{12,13},{13,14},{16,17},{17,1... | collective-permute-start | bytes 393224 | tf_op jit(solution)/shard_map/ppermute | solution.py:406
  679.8 14.4 %collective-permute-start.43 = (bf16[512,128]{1,0:T(8,128)(2,1)S(1)}, bf16[512,128]{1,0:T(8,128)(2,1)S(1)}, u32[]{:S(2)}, u32[]{:S(2)}) collective-permute-start(bf16[512,128]{1,0:T(8,128)(2,1)S(1)} %get-tuple-element.635), channel_id=1, source_target_pairs={{3,2},{2,1},{7,6},{6,5},{11,10},{10,9},{15,14},{14,13},{19,18},{18... | collective-permute-start | bytes 393224 | tf_op jit(solution)/shard_map/ppermute | solution.py:407
  686.9 16.7 %collective-permute-start.16 = (bf16[256,1024]{1,0:T(8,128)(2,1)S(1)}, bf16[256,1024]{1,0:T(8,128)(2,1)S(1)}, u32[]{:S(2)}, u32[]{:S(2)}) collective-permute-start(bf16[256,1024]{1,0:T(8,128)(2,1)S(1)} %get-tuple-element.601), channel_id=1, source_target_pairs={{3,2},{2,1},{7,6},{6,5},{11,10},{10,9},{15,14},{14,13},{19,18},{18... | collective-permute-start | bytes 1572872 | tf_op jit(solution)/shard_map/ppermute | solution.py:407
  687.6 38.3 %collective-permute-start.14 = (bf16[256,1024]{1,0:T(8,128)(2,1)S(1)}, bf16[256,1024]{1,0:T(8,128)(2,1)S(1)}, u32[]{:S(2)}, u32[]{:S(2)}) collective-permute-start(bf16[256,1024]{1,0:T(8,128)(2,1)S(1)} %get-tuple-element.600), channel_id=1, source_target_pairs={{0,1},{1,2},{2,3},{4,5},{5,6},{6,7},{8,9},{9,10},{10,11},{12,13},{... | collective-permute-start | bytes 1572872 | tf_op jit(solution)/shard_map/ppermute | solution.py:406
  694.3 11.3 %collective-permute-start.44 = (bf16[512,128]{1,0:T(8,128)(2,1)S(1)}, bf16[512,128]{1,0:T(8,128)(2,1)S(1)}, u32[]{:S(2)}, u32[]{:S(2)}) collective-permute-start(bf16[512,128]{1,0:T(8,128)(2,1)S(1)} %get-tuple-element.633), channel_id=1, source_target_pairs={{3,2},{2,1},{1,0},{7,6},{6,5},{5,4},{11,10},{10,9},{9,8},{15,14},{... | collective-permute-start | bytes 393224 | tf_op jit(solution)/shard_map/ppermute | solution.py:407
  695.6 11.5 %collective-permute-start.41 = (bf16[512,128]{1,0:T(8,128)(2,1)S(1)}, bf16[512,128]{1,0:T(8,128)(2,1)S(1)}, u32[]{:S(2)}, u32[]{:S(2)}) collective-permute-start(bf16[512,128]{1,0:T(8,128)(2,1)S(1)} %get-tuple-element.632), channel_id=1, source_target_pairs={{0,1},{1,2},{2,3},{4,5},{5,6},{6,7},{8,9},{9,10},{10,11},{12,13},{... | collective-permute-start | bytes 393224 | tf_op jit(solution)/shard_map/ppermute | solution.py:406
  703.6 7.8 collective-permute-start.19
  705.7 20.3 %collective-permute-start.17 = (bf16[256,1024]{1,0:T(8,128)(2,1)S(1)}, bf16[256,1024]{1,0:T(8,128)(2,1)S(1)}, u32[]{:S(2)}, u32[]{:S(2)}) collective-permute-start(bf16[256,1024]{1,0:T(8,128)(2,1)S(1)} %fusion.109), channel_id=1, source_target_pairs={{3,2},{2,1},{1,0},{7,6},{6,5},{5,4},{11,10},{10,9},{9,8},{15,14},{... | collective-permute-start | bytes 1572872 | tf_op jit(solution)/shard_map/ppermute | solution.py:407
  707.2 9.5 %collective-permute-start.21 = (bf16[2,768,128]{2,1,0:T(8,128)(2,1)S(1)}, bf16[2,768,128]{2,1,0:T(8,128)(2,1)S(1)}, u32[]{:S(2)}, u32[]{:S(2)}) collective-permute-start(bf16[2,768,128]{2,1,0:T(8,128)(2,1)S(1)} %dynamic-slice_bitcast_fusion.13), channel_id=1, source_target_pairs={{0,16},{4,20},{8,24},{12,28},{16,0},{20,4},{24,8},{28,12},{1,17},{... | collective-permute-start | bytes 1179656 | tf_op jit(solution)/shard_map/ppermute | solution.py:421
  712.4 122.8 %collective-permute-start.20 = (bf16[768,128]{1,0:T(8,128)(2,1)}, bf16[768,128]{1,0:T(8,128)(2,1)}, u32[]{:S(2)}, u32[]{:S(2)}) collective-permute-start(bf16[768,128]{1,0:T(8,128)(2,1)} %dynamic-slice_bitcast_fusion.18), channel_id=1, source_target_pairs={{0,16},{4,20},{8,24},{12,28},{16,0},{20,4},{24,8},{28,12},{1,17},{... | collective-permute-start | bytes 589832 | tf_op jit(solution)/shard_map/ppermute | solution.py:421
  717.5 127.0 %collective-permute-start.22 = (bf16[768,128]{1,0:T(8,128)(2,1)}, bf16[768,128]{1,0:T(8,128)(2,1)}, u32[]{:S(2)}, u32[]{:S(2)}) collective-permute-start(bf16[768,128]{1,0:T(8,128)(2,1)} %dynamic-slice_bitcast_fusion.17), channel_id=1, source_target_pairs={{0,8},{4,12},{8,0},{12,4},{16,24},{20,28},{24,16},{28,20},{1,9},{5... | collective-permute-start | bytes 589832 | tf_op jit(solution)/shard_map/ppermute | solution.py:421
  724.8 72.9 %copy-start.14 = (f32[256,1024]{1,0:T(8,128)S(1)}, f32[256,1024]{1,0:T(8,128)}, u32[]{:S(2)}) copy-start(f32[256,1024]{1,0:T(8,128)} %copy-done.13) | copy-start | bytes 3145732
  724.8 72.9 %copy-start.121 = (f32[1024]{0:T(1024)S(1)}, f32[1024]{0:T(1024)}, u32[]{:S(2)}) copy-start(f32[1024]{0:T(1024)} %reshape.1311) | copy-start | bytes 12292
  724.8 75.8 %collective-permute-start.24 = (bf16[2,2,256,512]{3,2,1,0:T(8,128)(2,1)}, bf16[2,2,256,512]{3,2,1,0:T(8,128)(2,1)}, u32[]{:S(2)}, u32[]{:S(2)}) collective-permute-start(bf16[2,2,256,512]{3,2,1,0:T(8,128)(2,1)} %dynamic-slice_bitcast_fusion.3), channel_id=1, source_target_pairs={{0,8},{4,12},{8,0},{12,4},{16,24},{20,28},{24,16},{28,20},{1,9},{5... | collective-permute-start | bytes 3145736 | tf_op jit(solution)/shard_map/ppermute | solution.py:421
  796.2 24.3 %collective-permute-start.26 = (bf16[2,2,256,512]{3,2,1,0:T(8,128)(2,1)S(1)}, bf16[2,2,256,512]{3,2,1,0:T(8,128)(2,1)S(1)}, u32[]{:S(2)}, u32[]{:S(2)}) collective-permute-start(bf16[2,2,256,512]{3,2,1,0:T(8,128)(2,1)S(1)} %dynamic-slice_bitcast_fusion.2), channel_id=1, source_target_pairs={{0,16},{4,20},{8,24},{12,28},{16,0},{20,4},{24,8},{28,12},{1,17},{... | collective-permute-start | bytes 3145736 | tf_op jit(solution)/shard_map/ppermute | solution.py:421
  802.3 23.9 %collective-permute-start.25 = (bf16[2,256,512]{2,1,0:T(8,128)(2,1)S(1)}, bf16[2,256,512]{2,1,0:T(8,128)(2,1)}, u32[]{:S(2)}, u32[]{:S(2)}) collective-permute-start(bf16[2,256,512]{2,1,0:T(8,128)(2,1)S(1)} %dynamic-slice_bitcast_fusion.8), channel_id=1, source_target_pairs={{0,16},{4,20},{8,24},{12,28},{16,0},{20,4},{24,8},{28,12},{1,17},{... | collective-permute-start | bytes 1572872 | tf_op jit(solution)/shard_map/ppermute | solution.py:421
  821.7 9.5 %collective-permute-start.27 = (bf16[2,256,512]{2,1,0:T(8,128)(2,1)}, bf16[2,256,512]{2,1,0:T(8,128)(2,1)}, u32[]{:S(2)}, u32[]{:S(2)}) collective-permute-start(bf16[2,256,512]{2,1,0:T(8,128)(2,1)} %dynamic-slice_bitcast_fusion.7), channel_id=1, source_target_pairs={{0,8},{4,12},{8,0},{12,4},{16,24},{20,28},{24,16},{28,20},{1,9},{5... | collective-permute-start | bytes 1572872 | tf_op jit(solution)/shard_map/ppermute | solution.py:421
  832.6 5.2 collective-permute-start.28
  833.9 3.9 collective-permute-start.31
  838.7 10.0 %collective-permute-start.29 = (bf16[256,512]{1,0:T(8,128)(2,1)}, bf16[256,512]{1,0:T(8,128)(2,1)S(1)}, u32[]{:S(2)}, u32[]{:S(2)}) collective-permute-start(bf16[256,512]{1,0:T(8,128)(2,1)} %get-tuple-element.616), channel_id=1, source_target_pairs={{0,1},{1,2},{4,5},{5,6},{8,9},{9,10},{12,13},{13,14},{16,17},{17,1... | collective-permute-start | bytes 786440 | tf_op jit(solution)/shard_map/ppermute | solution.py:406
  843.1 5.6 collective-permute-start.32
  850.6 11.3 %collective-permute-start.33 = (bf16[256,512]{1,0:T(8,128)(2,1)}, bf16[256,512]{1,0:T(8,128)(2,1)S(1)}, u32[]{:S(2)}, u32[]{:S(2)}) collective-permute-start(bf16[256,512]{1,0:T(8,128)(2,1)} %get-tuple-element.615), channel_id=1, source_target_pairs={{3,2},{2,1},{1,0},{7,6},{6,5},{5,4},{11,10},{10,9},{9,8},{15,14},{... | collective-permute-start | bytes 786440 | tf_op jit(solution)/shard_map/ppermute | solution.py:407
  851.9 11.2 %collective-permute-start.30 = (bf16[256,512]{1,0:T(8,128)(2,1)S(1)}, bf16[256,512]{1,0:T(8,128)(2,1)S(1)}, u32[]{:S(2)}, u32[]{:S(2)}) collective-permute-start(bf16[256,512]{1,0:T(8,128)(2,1)S(1)} %get-tuple-element.614), channel_id=1, source_target_pairs={{0,1},{1,2},{2,3},{4,5},{5,6},{6,7},{8,9},{9,10},{10,11},{12,13},{... | collective-permute-start | bytes 786440 | tf_op jit(solution)/shard_map/ppermute | solution.py:406
  (199 other events, 979.0 us)
Sparse Core Ops, SparseCore 0:
  61.7 30.8 all-gather.3
  94.5 37.0 all-gather.7
  133.5 54.3 all-gather.5

commit v2 on v1

v2 whole, which is shorter than its diff:
```python
from functools import partial

import numpy as np
import jax
import jax.numpy as jnp
from jax import lax
from jax.experimental import pallas as pl
from jax.experimental.pallas import tpu as pltpu
from jax.sharding import PartitionSpec as P

MESH = pl.DeviceIdType.MESH

QHEADS = 8
KVHEADS = 2
HEAD_SIZE = 64
SSM_DIM = 64
CONV = 4


epsilon = 1e-05
rope_base = 100000000000.0
neg_large = -1e30
block_len = 128


def norm_apply(values, gain):
    factor = lax.rsqrt(jnp.mean(values * values, axis=-1, keepdims=True) + epsilon)
    return values * factor * gain


def dp_bits(index):
    core = lax.rem(index, 2)
    xbit = lax.rem(index // 2, 2)
    ybit = lax.rem(index // 4, 2)
    return core, xbit, ybit


def gather_kernel(nt, *refs):
    (tok, que, att, inn, mam, sha, sma) = refs[:7]
    (tok_f, que_f, att_f, inn_f, mam_f, sha_f, sma_f) = refs[7:14]
    (lsem, zs_send, zs_recv, t_send, t_recv, d_send, d_recv) = refs[14:]
    d = lax.axis_index("dp")
    z = lax.axis_index("tensor")
    core, xbit, ybit = dp_bits(d)
    d_core = d + 1 - 2 * core
    d_x = d + 2 - 4 * xbit
    d_y = d + 4 - 8 * ybit
    d_xy = d_x + 4 - 8 * ybit

    barrier = pltpu.get_barrier_semaphore()
    for peer in (d_core, d_x, d_y):
        pl.semaphore_signal(barrier, inc=1, device_id=(peer, z), device_id_type=MESH)
    for k in range(1, nt):
        pl.semaphore_signal(
            barrier, inc=1, device_id=(d, lax.rem(z + k, nt)), device_id_type=MESH
        )
    pl.semaphore_wait(barrier, 3 + nt - 1)

    def remote(src, dst, send, recv, dev):
        return pltpu.make_async_remote_copy(
            src_ref=src, dst_ref=dst, send_sem=send, recv_sem=recv,
            device_id=dev, device_id_type=MESH,
        )

    small = []
    for i, (src, dst) in enumerate(((sha, sha_f), (sma, sma_f))):
        for k in range(1, nt):
            copy = remote(
                src, dst.at[d, z], zs_send.at[i, k], zs_recv.at[i, k],
                (d, lax.rem(z + k, nt)),
            )
            copy.start()
            small.append(copy)
    q_rows = que.shape[0]
    cols = att.shape[1]
    i_rows = inn.shape[1]
    items = (
        (inn, lambda s: inn_f.at[:, pl.ds(s * i_rows, i_rows)]),
        (que, lambda s: que_f.at[pl.ds(s * q_rows, q_rows)]),
        (att, lambda s: att_f.at[:, pl.ds(pl.multiple_of(s * cols, cols), cols)]),
        (mam, lambda s: mam_f.at[:, pl.ds(pl.multiple_of(s * cols, cols), cols)]),
    )
    locals_ = []
    for i, (src, dst) in enumerate(
        [(tok, tok_f.at[z]), (sha, sha_f.at[d, z]), (sma, sma_f.at[d, z])]
        + [(src, at(d)) for src, at in items]
    ):
        copy = pltpu.make_async_copy(src, dst, lsem.at[i])
        copy.start()
        locals_.append(copy)
    sent = []

    def stage_one(i, src, at):
        for j, peer in enumerate((d_x, d_y, d_core)):
            copy = remote(src, at(d), d_send.at[i, j], d_recv.at[i, j], (peer, z))
            copy.start()
            sent.append(copy)

    for i, (src, at) in enumerate(items):
        stage_one(i, src, at)

    def tok_copy(slot, dirn, hop):
        dev = z + 1 if dirn == 0 else z - 1
        return remote(
            tok_f.at[slot], tok_f.at[slot], t_send.at[dirn, hop], t_recv.at[dirn, hop], (d, dev)
        )

    def own_copy(dirn):
        dev = z + 1 if dirn == 0 else z - 1
        return remote(tok, tok_f.at[z], t_send.at[dirn, 0], t_recv.at[dirn, 0], (d, dev))

    pl.when(z < nt - 1)(lambda: own_copy(0).start())
    pl.when(z > 0)(lambda: own_copy(1).start())

    locals_[1].wait()
    locals_[2].wait()
    for copy in small:
        copy.wait()
    n = len(items)
    shared_items = (
        (sha_f.at[d], lambda s: sha_f.at[s]),
        (sma_f.at[d], lambda s: sma_f.at[s]),
    )
    for i, (src, at) in enumerate(shared_items):
        stage_one(n + i, src, at)

    def wait_recv(i, j, at, slot):
        remote(at(slot), at(slot), d_send.at[i, j], d_recv.at[i, j], (d_core, z)).wait_recv()

    def forward(i, j, at, slot, peer):
        copy = remote(at(slot), at(slot), d_send.at[i, j], d_recv.at[i, j], (peer, z))
        copy.start()
        sent.append(copy)

    everything = [at for _, at in items] + [at for _, at in shared_items]
    via_y = (0, n + 1)

    def diagonal(i, at):
        wait_recv(i, 0, at, d_x)
        if i in via_y:
            forward(i, 3, at, d_x, d_y)
        forward(i, 4, at, d_x, d_core)
        wait_recv(i, 1, at, d_y)
        if i not in via_y:
            forward(i, 3, at, d_y, d_x)
        forward(i, 5, at, d_y, d_core)

    for i in range(n):
        diagonal(i, everything[i])

    def hop(dist):
        def from_left():
            tok_copy(z - dist, 0, dist - 1).wait_recv()

        def from_right():
            tok_copy(z + dist, 1, dist - 1).wait_recv()

        pl.when(z >= dist)(from_left)
        if dist < nt - 1:
            pl.when((z >= dist) & (z < nt - 1))(lambda: tok_copy(z - dist, 0, dist).start())
        pl.when(z + dist < nt)(from_right)
        if dist < nt - 1:
            pl.when((z + dist < nt) & (z > 0))(lambda: tok_copy(z + dist, 1, dist).start())

    hop(1)
    for i in range(n, n + 2):
        diagonal(i, everything[i])
    for i, at in enumerate(everything):
        wait_recv(i, 3, at, d_xy)
        forward(i, 6, at, d_xy, d_core)
    for dist in range(2, nt):
        hop(dist)
    for i, at in enumerate(everything):
        wait_recv(i, 2, at, d_core)
        for j in (4, 5, 6):
            wait_recv(i, j, at, d_core)
    for i, copy in enumerate(locals_):
        if i not in (1, 2):
            copy.wait()
    for copy in sent:
        copy.wait_send()
    pl.when(z < nt - 1)(lambda: own_copy(0).wait_send())
    pl.when(z > 0)(lambda: own_copy(1).wait_send())
    for dist in range(1, nt - 1):
        pl.when((z >= dist) & (z < nt - 1))(lambda: tok_copy(z - dist, 0, dist).wait_send())
        pl.when((z + dist < nt) & (z > 0))(lambda: tok_copy(z + dist, 1, dist).wait_send())


def gather_start(tok, que, att, inn, mam, sha, sma, nd, nt):
    if nd != 8:
        shared = lax.all_gather(sha, ("dp", "tensor"), axis=0)
        small = lax.all_gather(sma, ("dp", "tensor"), axis=0)
        return (
            lax.all_gather(tok, "tensor", axis=0),
            lax.all_gather(que, "dp", axis=0, tiled=True),
            lax.all_gather(att, "dp", axis=1, tiled=True),
            lax.all_gather(inn, "dp", axis=1, tiled=True),
            lax.all_gather(mam, "dp", axis=1, tiled=True),
            shared.reshape((nd, nt) + sha.shape),
            small.reshape((nd, nt) + sma.shape),
        )
    bf = jnp.bfloat16
    outs = (
        (nt,) + tok.shape,
        (nd * que.shape[0], que.shape[1]),
        (att.shape[0], nd * att.shape[1]),
        (2, nd * inn.shape[1], inn.shape[2]),
        (mam.shape[0], nd * mam.shape[1]),
        (nd, nt) + sha.shape,
        (nd, nt) + sma.shape,
    )
    anywhere = pl.BlockSpec(memory_space=pl.ANY)
    dma = pltpu.SemaphoreType.DMA
    return pl.pallas_call(
        partial(gather_kernel, nt),
        out_shape=[jax.ShapeDtypeStruct(s, bf) for s in outs],
        in_specs=[anywhere] * 7,
        out_specs=[anywhere] * 7,
        scratch_shapes=[
            dma((7,)), dma((2, nt)), dma((2, nt)), dma((2, nt)), dma((2, nt)),
            dma((6, 7)), dma((6, 7)),
        ],
        compiler_params=pltpu.CompilerParams(collective_id=0, has_side_effects=True),
        name="gather_start",
    )(tok, que, att, inn, mam, sha, sma)


def pick(values, index, axis=0):
    return lax.dynamic_index_in_dim(values, index, axis, keepdims=False)


def add_low(left, right):
    return (left.astype(jnp.float32) + right.astype(jnp.float32)).astype(jnp.bfloat16)


def chain_gather(values, nt):
    z = lax.axis_index("tensor")
    out = jnp.zeros((nt,) + values.shape, values.dtype)
    out = lax.dynamic_update_index_in_dim(out, values, z, 0)
    right = left = values
    for dist in range(1, nt):
        right = lax.ppermute(right, "tensor", [(i, i + 1) for i in range(dist - 1, nt - 1)])
        left = lax.ppermute(left, "tensor", [(i, i - 1) for i in range(1, nt - dist + 1)])
        pieces = out
        pieces = jnp.where(
            z >= dist,
            lax.dynamic_update_index_in_dim(pieces, right, jnp.maximum(z - dist, 0), 0),
            pieces,
        )
        out = jnp.where(
            z + dist < nt,
            lax.dynamic_update_index_in_dim(pieces, left, jnp.minimum(z + dist, nt - 1), 0),
            pieces,
        )
    return out


def chain_scatter(parts, nt):
    z = lax.axis_index("tensor")
    right = left = None
    for t in range(nt - 1):
        to_right = pick(parts, jnp.clip(nt - 1 - t + z, 0, nt - 1))
        to_left = pick(parts, jnp.clip(t - (nt - 1) + z, 0, nt - 1))
        if t > 0:
            to_right = add_low(to_right, right)
            to_left = add_low(to_left, left)
        right = lax.ppermute(to_right, "tensor", [(i, i + 1) for i in range(t + 1)])
        left = lax.ppermute(
            to_left, "tensor", [(nt - 1 - i, nt - 2 - i) for i in range(t + 1)]
        )
    f32 = jnp.float32
    return pick(parts, z).astype(f32) + right.astype(f32) + left.astype(f32)


def cube_scatter(parts, nd, last=jnp.float32):
    if nd != 8:
        return lax.psum_scatter(parts, "dp", scatter_dimension=0, tiled=False).astype(last)
    d = lax.axis_index("dp")
    core, xbit, ybit = dp_bits(d)

    def swap(values, bit):
        return lax.ppermute(values, "dp", [(i, i ^ bit) for i in range(8)])

    tail = parts.shape[1:]
    cut = parts.reshape((4, 2) + tail)
    held = add_low(pick(cut, core, 1), swap(pick(cut, 1 - core, 1), 1))
    held = held.reshape((2, 2) + tail)
    half = tail[0] // 2
    one, two = held[:, :, :half], held[:, :, half:]
    one_b = add_low(pick(one, xbit, 1), swap(pick(one, 1 - xbit, 1), 2))
    two_b = add_low(pick(two, ybit, 0), swap(pick(two, 1 - ybit, 0), 4))
    f32 = jnp.float32
    one_c = pick(one_b, ybit).astype(f32) + swap(pick(one_b, 1 - ybit), 4).astype(f32)
    two_c = pick(two_b, xbit).astype(f32) + swap(pick(two_b, 1 - xbit), 2).astype(f32)
    return jnp.concatenate([one_c, two_c], axis=0).astype(last)


def tensor_total(values):
    return lax.psum(values, "tensor")


F32, BF16 = jnp.float32, jnp.bfloat16
VMEM_LIMIT = 56 * 1024 * 1024


def dot_nn(a, b):
    return lax.dot_general(a, b, (((1,), (0,)), ((), ())), preferred_element_type=F32)


def dot_nt(a, b):
    return lax.dot_general(a, b, (((1,), (1,)), ((), ())), preferred_element_type=F32)


def dot_tn(a, b):
    return lax.dot_general(a, b, (((0,), (0,)), ((), ())), preferred_element_type=F32)


def sigmoid(v):
    return 1.0 / (1.0 + jnp.exp(-v))


def lanes_of(shape):
    return lax.broadcasted_iota(jnp.int32, shape, len(shape) - 1)


def turn(values, cosine, sine):
    lane = lanes_of(values.shape)
    other = jnp.where(
        lax.rem(lane, HEAD_SIZE) < HEAD_SIZE // 2,
        pltpu.roll(values, 128 - HEAD_SIZE // 2, 1),
        pltpu.roll(values, HEAD_SIZE // 2, 1),
    )
    return values * cosine + other * sine


def softplus(v):
    return jnp.maximum(v, 0.0) + jnp.log1p(jnp.exp(-jnp.abs(v)))


def running_sum(rows):
    lane = lanes_of(rows.shape)
    step = 1
    while step < rows.shape[1]:
        rows = rows + jnp.where(lane >= step, pltpu.roll(rows, step, 1), 0.0)
        step *= 2
    return rows


def running_sum_back(rows):
    lane = lanes_of(rows.shape)
    width = rows.shape[1]
    step = 1
    while step < width:
        rows = rows + jnp.where(lane < width - step, pltpu.roll(rows, width - step, 1), 0.0)
        step *= 2
    return rows


def stack_columns(rows_list):
    used = sum(r.shape[0] for r in rows_list)
    filler = jnp.zeros((128 - used, 128), F32)
    return jnp.concatenate(rows_list + [filler], axis=0).T


def widen(cols, base, heads):
    low = lanes_of((cols.shape[0], 128)) < SSM_DIM
    return jnp.concatenate(
        [
            jnp.where(low, cols[:, base + 2 * p : base + 2 * p + 1],
                      cols[:, base + 2 * p + 1 : base + 2 * p + 2])
            for p in range(heads // 2)
        ],
        axis=1,
    )


def conv_rows(ref, taps, first, rows):
    total = taps[CONV : CONV + 1, :] + taps[0:1, :] * ref[pl.ds(first, rows), :]
    for j in range(1, CONV):
        total = total + taps[j : j + 1, :] * ref[pl.ds(first + j, rows), :]
    return total


def forward_kernel(
    heads, kvh, tok, gain, wq, win, stp, wsh, cosine, sine, tapx, tapb, decay, bias, skip,
    a1_o, q_o, k_o, v_o, lse_o, o_o, x_o, z_o, b_o, y_o, t_o, s_o, sq_o,
    keys, vals, xs, bs, state,
):
    step = pl.program_id(0)
    rows = tok.shape[0]
    second = kvh[0] == 1

    @pl.when(step == 0)
    def _():
        xs[0:8, :] = jnp.zeros((8, xs.shape[1]), F32)
        bs[0:8, :] = jnp.zeros((8, bs.shape[1]), F32)
        state[...] = jnp.zeros(state.shape, F32)

    t = tok[...].astype(F32)
    r = lax.rsqrt(jnp.mean(t * t, axis=1, keepdims=True) + epsilon)
    a1 = (t * r * gain[...]).astype(BF16)
    a1_o[...] = a1
    q = turn(dot_nn(a1, wq[...]), cosine[...], sine[...]).astype(BF16)
    q_o[...] = q
    s = dot_nn(a1, wsh[...])
    low = lanes_of((rows, 128)) < HEAD_SIZE
    k = turn(s[:, :128], cosine[...], sine[...])
    v = s[:, 128:256]
    pick_own = low != second
    k2 = jnp.where(pick_own, k, pltpu.roll(k, 64, 1)).astype(BF16)
    v2 = jnp.where(pick_own, v, pltpu.roll(v, 64, 1))
    k_o[...] = k2
    v_o[...] = v2.astype(BF16)
    place = pl.ds(pl.multiple_of(step * rows, rows), rows)
    keys[place, :] = k2
    vals[:, place] = v2.T.astype(BF16)

    scale = HEAD_SIZE**-0.5

    def attend(blocks):
        n = blocks * rows
        shape = (rows, rows)
        allowed = lax.broadcasted_iota(jnp.int32, shape, 0) <= lanes_of(shape)
        parts = []
        for h in range(2):
            qh = jnp.where(low == (h == 0), q, jnp.zeros_like(q))
            sc = dot_nt(keys[0:n, :], qh) * scale
            last = jnp.where(allowed, sc[n - rows :, :], neg_large)
            sc = jnp.concatenate([sc[: n - rows, :], last], axis=0) if blocks > 1 else last
            top = jnp.max(sc, axis=0, keepdims=True)
            e = jnp.exp(sc - top)
            total = jnp.sum(e, axis=0, keepdims=True)
            lse_o[h : h + 1, :] = top + jnp.log(total)
            parts.append(dot_nn(vals[:, 0:n], e.astype(BF16)) / total)
        sub = lax.broadcasted_iota(jnp.int32, parts[0].shape, 0)
        o_o[...] = jnp.where(sub < HEAD_SIZE, parts[0], parts[1]).T.astype(BF16)

    for i in range(keys.shape[0] // rows):
        pl.when(step == i)(partial(attend, i + 1))

    zr = dot_nn(a1, win[0])
    z_o[...] = zr
    xr = dot_nn(a1, win[1])
    x_o[...] = xr
    br = s[:, 256:]
    b_o[...] = br
    xs[8 : 8 + rows, :] = xr
    bs[8 : 8 + rows, :] = br
    u = conv_rows(xs, tapx, 5, rows)
    x = u * sigmoid(u)
    u = conv_rows(bs, tapb, 5, rows)
    bc = (u * sigmoid(u)).astype(BF16)
    xs[0:8, :] = xs[rows : rows + 8, :]
    bs[0:8, :] = bs[rows : rows + 8, :]
    tr = dot_nt(stp[...], a1)
    t_o[...] = tr
    n_state = bc.shape[1] // 2
    tri_shape = (block_len, block_len)
    lower = lax.broadcasted_iota(jnp.int32, tri_shape, 0) >= lanes_of(tri_shape)
    half = lanes_of(tri_shape) < SSM_DIM
    for c in range(rows // block_len):
        part = slice(c * block_len, (c + 1) * block_len)
        dt = softplus(tr[:, part] + bias[...])
        cum = running_sum(dt * decay[...])
        end = cum[:, block_len - 1 :]
        cols = stack_columns([cum, jnp.exp(cum), dt * jnp.exp(end - cum)])
        xc = x[part]
        x_low = xc.astype(BF16)
        b_low = bc[part, :n_state]
        c_low = bc[part, n_state:]
        cross = dot_nt(c_low, b_low)
        grow = widen(cols, 8, heads)
        y = dot_nn(c_low, state[...].astype(BF16)) * grow + skip[...] * xc
        inner = []
        for p in range(heads // 2):
            mats = []
            for h in (2 * p, 2 * p + 1):
                gap = jnp.where(lower, cols[:, h : h + 1] - cum[h : h + 1, :], neg_large)
                mats.append((cross * jnp.exp(gap) * dt[h : h + 1, :]).astype(BF16))
            xp = x_low[:, 128 * p : 128 * p + 128]
            zero = jnp.zeros_like(xp)
            both = jnp.concatenate([jnp.where(half, xp, zero), jnp.where(half, zero, xp)], axis=0)
            inner.append(dot_nn(jnp.concatenate(mats, axis=1), both))
        y = y + jnp.concatenate(inner, axis=1)
        y_o[part, :] = y
        s_o[c] = state[...]
        carried = (xc * widen(cols, 16, heads)).astype(BF16)
        state[...] = grow[block_len - 1 :, :] * state[...] + dot_tn(b_low, carried)
        zc = zr[part]
        w = y * (zc * sigmoid(zc))
        total = jnp.sum(w * w, axis=1, keepdims=True)
        sq_o[:, part] = jnp.broadcast_to(total, (block_len, 128)).T[0:8, :]


def mixers_forward(heads, kvh, tok, gain, wq, win, stp, wsh, cosine, sine, tapx, tapb, decay, bias, skip):
    total, width = tok.shape
    rows = 256
    inner = heads * SSM_DIM
    pair = wsh.shape[1] - 256
    state = pair // 2
    chunks = rows // block_len

    def whole(v):
        return pl.BlockSpec(v.shape, lambda i: (0,) * v.ndim)

    def tall(n):
        return pl.BlockSpec((rows, n), lambda i: (i, 0))

    wide = pl.BlockSpec((8, rows), lambda i: (0, i))
    sds = jax.ShapeDtypeStruct
    return pl.pallas_call(
        partial(forward_kernel, heads),
        grid=(total // rows,),
        in_specs=[pl.BlockSpec(memory_space=pltpu.SMEM), tall(width), whole(gain), whole(wq), whole(win),
                  whole(stp), whole(wsh), tall(128), tall(128), whole(tapx), whole(tapb),
                  whole(decay), whole(bias), whole(skip)],
        out_specs=[tall(width), tall(128), tall(128), tall(128), wide, tall(128), tall(inner),
                   tall(inner), tall(pair), tall(inner), wide,
                   pl.BlockSpec((chunks, state, inner), lambda i: (i, 0, 0)), wide],
        out_shape=[sds((total, width), BF16), sds((total, 128), BF16), sds((total, 128), BF16),
                   sds((total, 128), BF16), sds((8, total), F32), sds((total, 128), BF16),
                   sds((total, inner), F32), sds((total, inner), F32), sds((total, pair), F32),
                   sds((total, inner), F32), sds((8, total), F32),
                   sds((total // block_len, state, inner), F32), sds((8, total), F32)],
        scratch_shapes=[pltpu.VMEM((total, 128), BF16), pltpu.VMEM((128, total), BF16),
                        pltpu.VMEM((rows + 8, inner), F32), pltpu.VMEM((rows + 8, pair), F32),
                        pltpu.VMEM((state, inner), F32)],
        compiler_params=pltpu.CompilerParams(vmem_limit_bytes=VMEM_LIMIT),
        cost_estimate=pl.CostEstimate(flops=int(5e9), bytes_accessed=int(15e6), transcendentals=int(4e6)),
        name="mixers_forward",
    )(kvh, tok, gain, wq, win, stp, wsh, cosine, sine, tapx, tapb, decay, bias, skip)


def attend_back_kernel(kvh, q, k2, v2, lse, do, cosine, sine, cos_all, sin_all, dq_o, dkv_o, dk, dv):
    step = pl.program_id(0)
    rows = q.shape[0]
    steps = k2.shape[0] // rows
    scale = HEAD_SIZE**-0.5
    low = lanes_of((rows, 128)) < HEAD_SIZE

    @pl.when(step == 0)
    def _():
        dk[...] = jnp.zeros(dk.shape, F32)
        dv[...] = jnp.zeros(dv.shape, F32)

    def back(blocks):
        n = blocks * rows
        shape = (rows, rows)
        allowed = lax.broadcasted_iota(jnp.int32, shape, 0) <= lanes_of(shape)
        qs, dos, ps, dss, dqs = [], [], [], [], []
        for h in range(2):
            mine = low == (h == 0)
            qh = jnp.where(mine, q[...], jnp.zeros_like(q[...]))
            doh = jnp.where(mine, do[...], jnp.zeros_like(do[...]))
            sc = dot_nt(k2[0:n, :], qh) * scale - lse[h : h + 1, :]
            last = jnp.where(allowed, sc[n - rows :, :], neg_large)
            sc = jnp.concatenate([sc[: n - rows, :], last], axis=0) if blocks > 1 else last
            p = jnp.exp(sc)
            dp = dot_nt(v2[0:n, :], doh)
            centre = jnp.sum(p * dp, axis=0, keepdims=True)
            ds = (p * (dp - centre)).astype(BF16)
            qs.append(qh)
            dos.append(doh)
            ps.append(p.astype(BF16))
            dss.append(ds)
            dqs.append(dot_tn(ds, k2[0:n, :]) * scale)
        dk[0:n, :] += dot_nn(jnp.concatenate(dss, axis=1), jnp.concatenate(qs, axis=0)) * scale
        dv[0:n, :] += dot_nn(jnp.concatenate(ps, axis=1), jnp.concatenate(dos, axis=0))
        dq_o[...] = turn(jnp.where(low, dqs[0], dqs[1]), cosine[...], -sine[...]).astype(BF16)

    for i in range(steps):
        pl.when(step == i)(partial(back, i + 1))

    @pl.when(step == steps - 1)
    def _():
        own = (lanes_of(dk.shape) < HEAD_SIZE) != (kvh[0] == 1)
        g = dk[...]
        g = turn(g + pltpu.roll(g, 64, 1), cos_all[...], -sin_all[...])
        dkv_o[:, 0:128] = jnp.where(own, g, 0.0).astype(BF16)
        g = dv[...]
        g = g + pltpu.roll(g, 64, 1)
        dkv_o[:, 128:256] = jnp.where(own, g, 0.0).astype(BF16)


def attend_back(kvh, q, k2, v2, lse, do, cosine, sine):
    total = q.shape[0]
    rows = 256

    def whole(v):
        return pl.BlockSpec(v.shape, lambda i: (0,) * v.ndim)

    tall = pl.BlockSpec((rows, 128), lambda i: (i, 0))
    wide = pl.BlockSpec((8, rows), lambda i: (0, i))
    sds = jax.ShapeDtypeStruct
    return pl.pallas_call(
        attend_back_kernel,
        grid=(total // rows,),
        in_specs=[pl.BlockSpec(memory_space=pltpu.SMEM), tall, whole(k2), whole(v2), wide, tall, tall, tall,
                  whole(cosine), whole(sine)],
        out_specs=[tall, pl.BlockSpec((total, 256), lambda i: (0, 0))],
        out_shape=[sds((total, 128), BF16), sds((total, 256), BF16)],
        scratch_shapes=[pltpu.VMEM((total, 128), F32), pltpu.VMEM((total, 128), F32)],
        compiler_params=pltpu.CompilerParams(vmem_limit_bytes=VMEM_LIMIT),
        cost_estimate=pl.CostEstimate(flops=int(2e9), bytes_accessed=int(3e6), transcendentals=int(2e6)),
        name="attend_back",
    )(kvh, q, k2, v2, lse, do, cosine, sine, cosine, sine)


def scan_back_kernel(
    heads, channels, dm, y, zr, xr, xp, br, bp, trow, states, rsum, dots, gain, tapx, tapb, decay,
    bias, skip,
    dz_o, dx_o, db_o, dt_o, gx_o, gb_o, gm_o, gh_o,
    xs, bs, dxs, dbs, dstate,
):
    step = pl.program_id(0)
    last_step = pl.num_programs(0) - 1
    first = step == last_step
    rows = block_len
    inner = heads * SSM_DIM
    n_state = br.shape[1] // 2

    @pl.when(step == 0)
    def _():
        dxs[rows : rows + 8, :] = jnp.zeros((8, inner), F32)
        dbs[rows : rows + 8, :] = jnp.zeros((8, 2 * n_state), F32)
        dstate[...] = jnp.zeros(dstate.shape, F32)
        gx_o[...] = jnp.zeros(gx_o.shape, F32)
        gb_o[...] = jnp.zeros(gb_o.shape, F32)
        gm_o[...] = jnp.zeros(gm_o.shape, F32)
        gh_o[...] = jnp.zeros(gh_o.shape, F32)

    xs[0:8, :] = jnp.where(first, 0.0, xp[...])
    bs[0:8, :] = jnp.where(first, 0.0, bp[...])
    xs[8 : 8 + rows, :] = xr[...]
    bs[8 : 8 + rows, :] = br[...]
    ux = conv_rows(xs, tapx, 5, rows)
    sx = sigmoid(ux)
    x = ux * sx
    ub = conv_rows(bs, tapb, 5, rows)
    sb = sigmoid(ub)
    bc = (ub * sb).astype(BF16)
    b_low, c_low = bc[:, :n_state], bc[:, n_state:]

    pre = trow[...] + bias[...]
    dt = softplus(pre)
    cum = running_sum(dt * decay[...])
    end = cum[:, rows - 1 :]
    fade = jnp.exp(end - cum)
    inv = lax.rsqrt(rsum[...] / channels + epsilon)
    cols = stack_columns(
        [cum, jnp.exp(cum), dt * fade, dt, inv, inv * inv * inv * dots[...] / channels]
    )
    r = cols[:, 32:33]
    kk = cols[:, 40:41]
    z = zr[...]
    sz = sigmoid(z)
    silu_z = z * sz
    yv = y[...]
    w = yv * silu_z
    dmv = dm[...]
    dw = r * gain[...] * dmv - w * kk
    gm_o[0:1, :] += jnp.sum(dmv * w * r, axis=0, keepdims=True)
    dy = dw * silu_z
    dz_o[...] = (dw * yv * sz * (1.0 + z * (1.0 - sz))).astype(BF16)
    gm_o[1:2, :] += jnp.sum(dy * x, axis=0, keepdims=True)

    grow = widen(cols, 8, heads)
    tail = widen(cols, 16, heads)
    dt_wide = widen(cols, 24, heads)
    x_low = x.astype(BF16)
    dy_low = dy.astype(BF16)
    state = states[0]
    state_low = state.astype(BF16)
    ds = dstate[...]
    ds_low = ds.astype(BF16)
    cross = dot_nt(b_low, c_low)
    shape = (rows, rows)
    upper = lax.broadcasted_iota(jnp.int32, shape, 0) <= lanes_of(shape)
    half = lanes_of(shape) < SSM_DIM
    lane = lanes_of(shape)
    dcross = jnp.zeros(shape, F32)
    col_sums = jnp.zeros(shape, F32)
    row_sums = []
    mids = []
    for p in range(heads // 2):
        span = slice(128 * p, 128 * p + 128)
        xpair, dypair = x_low[:, span], dy_low[:, span]
        zero = jnp.zeros_like(xpair)
        dys = (jnp.where(half, dypair, zero), jnp.where(half, zero, dypair))
        mats = []
        for k in range(2):
            h = 2 * p + k
            gap = jnp.where(upper, cum[h : h + 1, :] - cols[:, h : h + 1], neg_large)
            faded = jnp.exp(gap)
            mats.append((cross * faded).astype(BF16))
            t = dot_nt(xpair, dys[k]) * faded
            dt_col = cols[:, 24 + h : 25 + h]
            td = t * dt_col
            dcross = dcross + td
            row_sums.append(jnp.sum(td * cross, axis=0, keepdims=True))
            col = jnp.sum(t * cross, axis=1, keepdims=True)
            col_sums = jnp.where(lane == h, col, col_sums)
        mids.append(dot_nn(jnp.concatenate(mats, axis=1), jnp.concatenate(dys, axis=0)))
    mid = jnp.concatenate(mids, axis=1)
    row_sums = jnp.concatenate(row_sums + [jnp.zeros((8 - heads, rows), F32)], axis=0)
    col_sums = col_sums.T[0:8, :]

    dye = dy * grow
    dye_low = dye.astype(BF16)
    xd = x * tail
    xd_low = xd.astype(BF16)
    from_b = dot_nn(b_low, ds_low)
    through = dot_nn(c_low, state_low)
    dcross_low = dcross.astype(BF16)
    db = dot_nn(dcross_low, c_low) + dot_nt(xd_low, ds_low)
    dc = dot_tn(dcross_low, b_low) + dot_nt(dye_low, state_low)

    head_of = lax.broadcasted_iota(jnp.int32, (8, inner), 0)
    chan = lanes_of((8, inner)) // SSM_DIM
    ones = jnp.where(head_of == chan, 1.0, 0.0).astype(BF16)

    def by_head(v):
        high = v.astype(BF16)
        rest = (v - high.astype(F32)).astype(BF16)
        return dot_nt(ones, high) + dot_nt(ones, rest)

    grown = by_head(dye * through)
    ended = by_head(x * from_b)
    kept = jnp.sum(ds * state, axis=0, keepdims=True) * grow[rows - 1 :, :]
    kept = jnp.where(head_of == chan, kept, 0.0).sum(axis=1, keepdims=True)
    pulled = dt * fade * ended
    lane8 = lanes_of((8, rows))
    at_end = kept + jnp.sum(pulled, axis=1, keepdims=True)
    dcum = row_sums - dt * col_sums + grown - pulled + jnp.where(lane8 == rows - 1, at_end, 0.0)
    da = running_sum_back(dcum)
    ddt = col_sums + fade * ended + decay[...] * da
    dpre = ddt * sigmoid(pre)
    dt_o[...] = dpre
    gh_o[0:8, :] += da * dt * decay[...]
    gh_o[8:16, :] += dpre

    dstate[...] = grow[rows - 1 :, :] * ds + dot_tn(c_low, dye_low)
    dx = skip[...] * dy + dt_wide * mid + tail * from_b
    dux = dx * sx * (1.0 + ux * (1.0 - sx))
    dub = jnp.concatenate([db, dc], axis=1) * sb * (1.0 + ub * (1.0 - sb))
    for taps, src, d, buf, acc, out in (
        (tapx, xs, dux, dxs, gx_o, dx_o),
        (tapb, bs, dub, dbs, gb_o, db_o),
    ):
        buf[0:rows, :] = d
        total = taps[CONV - 1 : CONV, :] * d
        for j in range(CONV - 1):
            total = total + taps[j : j + 1, :] * buf[pl.ds(CONV - 1 - j, rows), :]
        out[...] = total.astype(BF16)
        for j in range(CONV):
            acc[j : j + 1, :] += jnp.sum(d * src[pl.ds(5 + j, rows), :], axis=0, keepdims=True)
        acc[CONV : CONV + 1, :] += jnp.sum(d, axis=0, keepdims=True)
        buf[rows : rows + 8, :] = d[0:8, :]


def scan_back(heads, channels, dm, y, zr, xr, br, trow, states, rsum, dots, gain, tapx, tapb, decay, bias, skip):
    total, inner = y.shape
    pair = br.shape[1]
    rows = block_len
    steps = total // rows
    per = rows // 8

    def whole(v):
        return pl.BlockSpec(v.shape, lambda i: (0,) * v.ndim)

    def tall(n):
        return pl.BlockSpec((rows, n), lambda i: (steps - 1 - i, 0))

    def before(n):
        return pl.BlockSpec((8, n), lambda i: (jnp.maximum((steps - 1 - i) * per - 1, 0), 0))

    wide = pl.BlockSpec((8, rows), lambda i: (0, steps - 1 - i))
    sds = jax.ShapeDtypeStruct

    def fixed(*shape):
        return pl.BlockSpec(shape, lambda i: (0, 0))

    return pl.pallas_call(
        partial(scan_back_kernel, heads, channels),
        grid=(steps,),
        in_specs=[tall(inner), tall(inner), tall(inner), tall(inner), before(inner), tall(pair),
                  before(pair), wide,
                  pl.BlockSpec((1, pair // 2, inner), lambda i: (steps - 1 - i, 0, 0)), wide, wide,
                  whole(gain), whole(tapx), whole(tapb), whole(decay), whole(bias), whole(skip)],
        out_specs=[tall(inner), tall(inner), tall(pair), wide, fixed(8, inner), fixed(8, pair),
                   fixed(8, inner), fixed(16, rows)],
        out_shape=[sds((total, inner), BF16), sds((total, inner), BF16), sds((total, pair), BF16),
                   sds((8, total), F32), sds((8, inner), F32), sds((8, pair), F32),
                   sds((8, inner), F32), sds((16, rows), F32)],
        scratch_shapes=[pltpu.VMEM((rows + 8, inner), F32), pltpu.VMEM((rows + 8, pair), F32),
                        pltpu.VMEM((rows + 8, inner), F32), pltpu.VMEM((rows + 8, pair), F32),
                        pltpu.VMEM((pair // 2, inner), F32)],
        compiler_params=pltpu.CompilerParams(vmem_limit_bytes=VMEM_LIMIT),
        cost_estimate=pl.CostEstimate(flops=int(4e9), bytes_accessed=int(15e6), transcendentals=int(5e6)),
        name="scan_back",
    )(dm, y, zr, xr, xr, br, br, trow, states, rsum, dots, gain, tapx, tapb,
      decay, bias, skip)


def whole_spec(v):
    return pl.BlockSpec(v.shape, lambda i: (0,) * v.ndim)


def feed_kernel(
    hid, gain, cot, whid, wdown, out_o, dh_o, dmix_o, gg_o, ghid_o, gdown_o, a2, a2t, acc, dacc
):
    step = pl.program_id(0)
    width = hid.shape[1]
    blocks = width // 128

    @pl.when(step == 0)
    def _():
        v = hid[...]
        f = lax.rsqrt(jnp.mean(v * v, axis=1, keepdims=True) + epsilon)
        low = (v * f * gain[...]).astype(BF16)
        a2[...] = low
        a2t[...] = low.T
        acc[...] = jnp.zeros(acc.shape, F32)
        dacc[...] = jnp.zeros(dacc.shape, F32)

    units = whid.shape[4]
    w_gate = whid[:, 0, 0].reshape(width, units)
    w_up = whid[:, 0, 1].reshape(width, units)
    w_down = jnp.concatenate([wdown[k, 0] for k in range(blocks)], axis=1)
    g = dot_nn(a2[...], w_gate)
    u = dot_nn(a2[...], w_up)
    s = sigmoid(g)
    f_low = (g * s * u).astype(BF16)
    c = cot[...]
    acc[...] += dot_nn(f_low, w_down)
    df = dot_nt(c, w_down)
    du = (df * g * s).astype(BF16)
    dg = (df * u * s * (1.0 + g * (1.0 - s))).astype(BF16)
    dacc[...] += dot_nt(dg, w_gate) + dot_nt(du, w_up)
    ghid_o[:, 0, 0] = dot_nn(a2t[...], dg).astype(BF16).reshape(blocks, 128, units)
    ghid_o[:, 0, 1] = dot_nn(a2t[...], du).astype(BF16).reshape(blocks, 128, units)
    gd = dot_tn(f_low, c).astype(BF16)
    for k in range(blocks):
        gdown_o[k, 0] = gd[:, 128 * k : 128 * k + 128]

    @pl.when(step == pl.num_programs(0) - 1)
    def _():
        v = hid[...]
        out_o[...] = (v + acc[...]).astype(BF16)
        f = lax.rsqrt(jnp.mean(v * v, axis=1, keepdims=True) + epsilon)
        dy = dacc[...]
        gg_o[...] = jnp.sum(dy * v * f, axis=0, keepdims=True)
        gdy = dy * gain[...]
        lean = jnp.sum(gdy * v, axis=1, keepdims=True) * (f * f * f / width)
        dh = cot[...].astype(F32) + (f * gdy - v * lean)
        dh_o[...] = dh
        dmix_o[...] = dh.astype(BF16)


def feed_forward(hid, gain, cot, whid, wdown):
    rows, width = hid.shape
    blocks, nt, _, depth, units = whid.shape
    tile = 256
    per = units // tile
    hid_spec = pl.BlockSpec((blocks, 1, 2, depth, tile), lambda i: (0, i // per, 0, 0, lax.rem(i, per)))
    down_spec = pl.BlockSpec((blocks, 1, tile, 128), lambda i: (0, i // per, lax.rem(i, per), 0))
    sds = jax.ShapeDtypeStruct

    def fixed(*shape):
        return pl.BlockSpec(shape, lambda i: (0, 0))

    return pl.pallas_call(
        feed_kernel,
        grid=(nt * per,),
        in_specs=[fixed(rows, width), fixed(1, width), fixed(rows, width), hid_spec, down_spec],
        out_specs=[fixed(rows, width), fixed(rows, width), fixed(rows, width), fixed(1, width), hid_spec,
                   down_spec],
        out_shape=[sds((rows, width), BF16), sds((rows, width), F32), sds((rows, width), BF16),
                   sds((1, width), F32), sds(whid.shape, BF16), sds(wdown.shape, BF16)],
        scratch_shapes=[pltpu.VMEM((rows, width), BF16), pltpu.VMEM((width, rows), BF16),
                        pltpu.VMEM((rows, width), F32), pltpu.VMEM((rows, width), F32)],
        compiler_params=pltpu.CompilerParams(vmem_limit_bytes=VMEM_LIMIT),
        cost_estimate=pl.CostEstimate(flops=int(1e10), bytes_accessed=int(26e6), transcendentals=int(5e5)),
        name="feed_forward",
    )(hid, gain, cot, whid, wdown)


def row_columns(rows_list, rows):
    return jnp.concatenate(
        [stack_columns([r[:, c : c + 128] for r in rows_list]) for c in range(0, rows, 128)], axis=0
    )


def mix_kernel(channels, o, y, z, sq, gain, watt, wmam, m_o, part_o):
    rows = o.shape[0]
    r = row_columns([lax.rsqrt(sq[...] / channels + epsilon)], rows)[:, 0:1]
    zv = z[...]
    m = (y[...] * (zv * sigmoid(zv)) * r * gain[...]).astype(BF16)
    m_o[...] = m
    part_o[...] = (dot_nn(o[...], watt[...]) + dot_nn(m, wmam[...])).astype(BF16)


def mix_parts(channels, o, y, z, sq, gain, watt, wmam):
    total, inner = y.shape
    width = watt.shape[1]
    rows = 256

    def tall(n):
        return pl.BlockSpec((rows, n), lambda i: (i, 0))

    wide = pl.BlockSpec((8, rows), lambda i: (0, i))
    sds = jax.ShapeDtypeStruct
    return pl.pallas_call(
        partial(mix_kernel, channels),
        grid=(total // rows,),
        in_specs=[tall(128), tall(inner), tall(inner), wide, whole_spec(gain), whole_spec(watt),
                  whole_spec(wmam)],
        out_specs=[tall(inner), tall(width)],
        out_shape=[sds((total, inner), BF16), sds((total, width), BF16)],
        compiler_params=pltpu.CompilerParams(vmem_limit_bytes=VMEM_LIMIT),
        cost_estimate=pl.CostEstimate(flops=int(1e9), bytes_accessed=int(7e6), transcendentals=int(4e5)),
        name="mix_parts",
    )(o, y, z, sq, gain, watt, wmam)


def unmix_kernel(dmix, y, z, gain, watt, wmam, do_o, dm_o, dot_o):
    rows = dmix.shape[0]
    g = dmix[...]
    do_o[...] = dot_nt(g, watt[...]).astype(BF16)
    dm = dot_nt(g, wmam[...])
    dm_o[...] = dm
    zv = z[...]
    dots = jnp.sum(dm * gain[...] * (y[...] * (zv * sigmoid(zv))), axis=1, keepdims=True)
    for c in range(0, rows, 128):
        dot_o[:, c : c + 128] = jnp.broadcast_to(dots[c : c + 128], (128, 128)).T[0:8, :]


def unmix(dmix, y, z, gain, watt, wmam):
    total, inner = y.shape
    rows = 256

    def tall(n):
        return pl.BlockSpec((rows, n), lambda i: (i, 0))

    wide = pl.BlockSpec((8, rows), lambda i: (0, i))
    sds = jax.ShapeDtypeStruct
    return pl.pallas_call(
        unmix_kernel,
        grid=(total // rows,),
        in_specs=[tall(dmix.shape[1]), tall(inner), tall(inner), whole_spec(gain), whole_spec(watt),
                  whole_spec(wmam)],
        out_specs=[tall(128), tall(inner), wide],
        out_shape=[sds((total, 128), BF16), sds((total, inner), F32), sds((8, total), F32)],
        compiler_params=pltpu.CompilerParams(vmem_limit_bytes=VMEM_LIMIT),
        cost_estimate=pl.CostEstimate(flops=int(1e9), bytes_accessed=int(7e6), transcendentals=int(4e5)),
        name="unmix",
    )(dmix, y, z, gain, watt, wmam)


def down_kernel(dq, dz, dx, dkv, db, drow, wq, win, stp, wsh, part_o):
    total = dot_nt(dq[...], wq[...]) + dot_nt(dz[...], win[0]) + dot_nt(dx[...], win[1])
    total = total + dot_nt(dkv[...], wsh[:, 0:256]) + dot_nt(db[...], wsh[:, 256:])
    total = total + dot_tn(drow[...].astype(BF16), stp[...])
    part_o[...] = total.astype(BF16)


def down_parts(dq, dz, dx, dkv, db, drow, wq, win, stp, wsh):
    total, inner = dz.shape
    width = wq.shape[0]
    rows = 256

    def tall(v):
        return pl.BlockSpec((rows, v.shape[1]), lambda i: (i, 0))

    wide = pl.BlockSpec((8, rows), lambda i: (0, i))
    return pl.pallas_call(
        down_kernel,
        grid=(total // rows,),
        in_specs=[tall(dq), tall(dz), tall(dx), tall(dkv), tall(db), wide, whole_spec(wq), whole_spec(win),
                  whole_spec(stp), whole_spec(wsh)],
        out_specs=pl.BlockSpec((rows, width), lambda i: (i, 0)),
        out_shape=jax.ShapeDtypeStruct((total, width), BF16),
        compiler_params=pltpu.CompilerParams(vmem_limit_bytes=VMEM_LIMIT),
        cost_estimate=pl.CostEstimate(flops=int(3e9), bytes_accessed=int(8e6), transcendentals=0),
        name="down_parts",
    )(dq, dz, dx, dkv, db, drow, wq, win, stp, wsh)


def weight_kernel(a1, dq, dz, dx, dkv, db, drow, o, m, dmix, piece_o, shared_o, step_o, ot, mt):
    step = pl.program_id(0)

    @pl.when(step == 0)
    def _():
        ot[...] = o[...].T
        mt[...] = m[...].T

    a = a1[...]
    step_o[...] = dot_nn(drow[...].astype(BF16), a)
    at = a.T
    inner = dz.shape[1]

    def by_rows(values, first):
        for j in range(values.shape[1] // 128):
            piece_o[:, first + 128 * j : first + 128 * (j + 1), :] = (
                values[:, 128 * j : 128 * (j + 1)].reshape(2, 128, 128)
            )

    def by_lanes(values, first):
        n = values.shape[0]
        for k in range(2):
            piece_o[k, first : first + n, :] = values[:, 128 * k : 128 * (k + 1)]

    g = dmix[...]
    by_rows(dot_nn(at, dq[...]).astype(BF16), 0)
    by_lanes(dot_nn(ot[...], g).astype(BF16), 128)
    by_rows(dot_nn(at, dz[...]).astype(BF16), 256)
    by_rows(dot_nn(at, dx[...]).astype(BF16), 256 + inner)
    by_lanes(dot_nn(mt[...], g).astype(BF16), 256 + 2 * inner)
    shared_o[:, :, 0:256] = dot_nn(at, dkv[...]).astype(BF16).reshape(2, 128, 256)
    shared_o[:, :, 256:] = dot_nn(at, db[...]).astype(BF16).reshape(2, 128, db.shape[1])


def weight_pieces(a1, dq, dz, dx, dkv, db, drow, o, m, dmix):
    total, width = a1.shape
    inner = dz.shape[1]
    n = 256 + 3 * inner
    shared = 256 + db.shape[1]
    cols = pl.BlockSpec((total, 256), lambda i: (0, i))
    sds = jax.ShapeDtypeStruct
    args = (dq, dz, dx, dkv, db, drow, o, m)
    return pl.pallas_call(
        weight_kernel,
        grid=(width // 256,),
        in_specs=[cols] + [whole_spec(v) for v in args] + [cols],
        out_specs=[pl.BlockSpec((2, n, 128), lambda i: (i, 0, 0)),
                   pl.BlockSpec((2, 128, shared), lambda i: (i, 0, 0)),
                   pl.BlockSpec((8, 256), lambda i: (0, i))],
        out_shape=[sds((width // 128, n, 128), BF16), sds((width // 128, 128, shared), BF16),
                   sds((8, width), F32)],
        scratch_shapes=[pltpu.VMEM((128, total), BF16), pltpu.VMEM((inner, total), BF16)],
        compiler_params=pltpu.CompilerParams(vmem_limit_bytes=VMEM_LIMIT),
        cost_estimate=pl.CostEstimate(flops=int(4e9), bytes_accessed=int(12e6), transcendentals=0),
        name="weight_pieces",
    )(a1, *args, dmix)


def rope_wide(length):
    half = HEAD_SIZE // 2
    inverse = rope_base ** (-np.arange(half) * (2.0 / HEAD_SIZE))
    angles = np.arange(length)[:, None] * inverse[None, :]
    c, s = np.cos(angles), np.sin(angles)
    return (
        jnp.asarray(np.concatenate([c, c, c, c], axis=1), F32),
        jnp.asarray(np.concatenate([-s, s, -s, s], axis=1), F32),
    )


def to_blocks(full, axis, nt):
    if axis == 1:
        two, width, cols = full.shape
        return full.reshape(2, 8, width // 8, nt, cols // nt).transpose(1, 3, 0, 2, 4)
    rows, width = full.shape
    return full.reshape(nt, rows // nt, 8, width // 8).transpose(2, 0, 1, 3)


def per_device(
    nd,
    nt,
    tokens,
    query_proj,
    attend_out,
    inner_proj,
    step_proj,
    mamba_out,
    hidden_proj,
    down_proj,
    channel_taps,
    mixer_gain,
    decay_log,
    step_bias,
    skip_weight,
    shared_proj,
    norm_gains,
    shared_taps,
    cotangent,
):
    tensor_index = lax.axis_index("tensor")
    d = lax.axis_index("dp")
    local_rows, width = tokens.shape
    group_rows = local_rows * nt
    heads = step_proj.shape[1]
    inner = heads * SSM_DIM
    channels = inner * nt
    units = down_proj.shape[0]
    small_parts = [channel_taps, mixer_gain, norm_gains, shared_taps, step_proj.T]
    flat = jnp.concatenate([p.reshape(-1) for p in small_parts])
    small_len = -(-flat.shape[0] // 2048) * 2048
    small = jnp.pad(flat, (0, small_len - flat.shape[0])).reshape(-1, 128)
    (tok_full, full_query, full_attend, full_inner, full_mamba, sha, sma) = gather_start(
        tokens, query_proj, attend_out, inner_proj, mamba_out, shared_proj, small, nd, nt
    )
    hid_in, down_in = hidden_proj, down_proj
    if nd == 8:
        full_hidden = lax.all_gather(hid_in, ("dp", "tensor"), axis=0).reshape(
            (nd, nt) + hidden_proj.shape
        )
        full_down = lax.all_gather(down_in, ("dp", "tensor"), axis=0).reshape(
            (nd, nt) + down_proj.shape
        )
    else:
        full_hidden = lax.all_gather(hid_in, "tensor", axis=2, tiled=True)
        full_hidden = to_blocks(lax.all_gather(full_hidden, "dp", axis=1, tiled=True), 1, nt)
        full_down = lax.all_gather(down_in, "tensor", axis=0, tiled=True)
        full_down = to_blocks(lax.all_gather(full_down, "dp", axis=1, tiled=True), 0, nt)

    full_shared = sha.reshape(width, -1)
    sma = sma.reshape(nd, nt, small_len)

    def small_piece(index):
        start = sum(p.size for p in small_parts[:index])
        part = small_parts[index]
        return sma[:, :, start : start + part.size].reshape((nd, nt) + part.shape)

    taps_x = pick(small_piece(0), tensor_index, 1).transpose(1, 2, 0, 3).reshape(CONV + 1, inner)
    gain_mix = pick(small_piece(1), tensor_index, 1).transpose(1, 0, 2).reshape(1, inner)
    full_norms = small_piece(2).transpose(2, 0, 1, 3).reshape(2, width).astype(F32)
    taps_b = small_piece(3).transpose(2, 0, 1, 3).reshape(CONV + 1, -1)
    step_rows = pick(small_piece(4), tensor_index, 1).transpose(1, 0, 2).reshape(heads, width)
    step_rows = jnp.pad(step_rows, ((0, 8 - heads), (0, 0)))
    taps_x = jnp.pad(taps_x.astype(F32), ((0, 7 - CONV), (0, 0)))
    taps_b = jnp.pad(taps_b.astype(F32), ((0, 7 - CONV), (0, 0)))
    gain_mix = gain_mix.astype(F32)
    gain_first = full_norms[0:1]
    gain_second = full_norms[1:2]

    def head_rows(values):
        return jnp.pad(jnp.broadcast_to(values[:, None], (heads, 128)), ((0, 8 - heads), (0, 0)))

    decay = head_rows(-jnp.exp(decay_log.astype(F32)))
    bias = head_rows(step_bias.astype(F32))
    skip = jnp.repeat(skip_weight.astype(F32), SSM_DIM)[None, :]
    q_heads = query_proj.shape[1] // HEAD_SIZE
    kv_head = (tensor_index * q_heads // (QHEADS // KVHEADS)).astype(jnp.int32).reshape(1)
    cosine, sine = rope_wide(group_rows)

    (a1, q, k2, v2, lse, o, xr, zr, br, y, trow, states, squares) = mixers_forward(
        heads, kv_head, tok_full.reshape(group_rows, width), gain_first, full_query, full_inner, step_rows,
        full_shared, cosine, sine, taps_x, taps_b, decay, bias, skip,
    )
    squares = jnp.broadcast_to(tensor_total(squares[0:1]), (8, group_rows))
    m, mix_part = mix_parts(channels, o, y, zr, squares, gain_mix, full_attend, full_mamba)
    hidden = tokens.astype(F32) + chain_scatter(mix_part.reshape(nt, local_rows, width), nt)
    layer_out, dh, dmix, grad_gain_two, hid_pieces, down_pieces = feed_forward(
        hidden, gain_second, cotangent, full_hidden, full_down
    )
    grad_mix = chain_gather(dmix, nt).reshape(group_rows, width)
    if nd == 8:
        hid_sum = cube_scatter(hid_pieces, nd, BF16)
        down_sum = cube_scatter(down_pieces, nd, BF16)
        gradient_hidden = chain_scatter(hid_sum, nt)
        gradient_down = chain_scatter(down_sum, nt)
    else:
        hid_full = hid_pieces.transpose(2, 0, 3, 1, 4).reshape(2, nd, width // nd, nt, units)
        hid_sum = cube_scatter(hid_full.transpose(1, 3, 0, 2, 4), nd, BF16)
        down_full = down_pieces.transpose(1, 2, 0, 3).reshape(nt, units, nd, width // nd)
        down_sum = cube_scatter(down_full.transpose(2, 0, 1, 3), nd, BF16)
        gradient_hidden = chain_scatter(hid_sum, nt)
        gradient_down = chain_scatter(down_sum, nt)

    do, dm, dots = unmix(grad_mix, y, zr, gain_mix, full_attend, full_mamba)
    dots = jnp.broadcast_to(tensor_total(dots[0:1]), (8, group_rows))
    dq, dkv = attend_back(kv_head, q, k2, v2, lse, do, cosine, sine)
    dz, dx, db, drow, grad_tx, grad_tb, grad_rows, grad_heads = scan_back(
        heads, channels, dm, y, zr, xr, br, trow, states, squares, dots, gain_mix, taps_x, taps_b, decay, bias,
        skip,
    )
    part_one = down_parts(dq, dz, dx, dkv, db, drow, full_query, full_inner, step_rows, full_shared)
    grad_normed_one = chain_scatter(part_one.reshape(nt, local_rows, width), nt)
    token_f32 = tokens.astype(F32)
    _, norm_one_back = jax.vjp(norm_apply, token_f32, gain_first[0])
    grad_from_one, grad_gain_one = norm_one_back(grad_normed_one)
    gradient_tokens = (dh + grad_from_one).astype(BF16)

    pieces, shared_pieces, grad_step = weight_pieces(a1, dq, dz, dx, dkv, db, drow, o, m, grad_mix)
    block = width // nd
    q_cols = query_proj.shape[1]
    cuts = [0, q_cols, q_cols + attend_out.shape[0]]
    cuts += [cuts[2] + inner, cuts[2] + 2 * inner, cuts[2] + 3 * inner]

    def from_rows(values):
        return values.reshape(8, -1, 128, 128).transpose(0, 2, 1, 3).reshape(width, -1)

    def from_lanes(values):
        return values.transpose(1, 0, 2).reshape(-1, width)

    if nd == 8:
        mixer_sum = cube_scatter(pieces, nd)
        got = [mixer_sum[cuts[i] : cuts[i + 1]] for i in range(5)]

        def back_rows(values):
            return values.reshape(-1, 128, 128).transpose(1, 0, 2).reshape(128, -1)

        gradient_query = back_rows(got[0])
        gradient_attend = got[1]
        gradient_inner = jnp.stack([back_rows(got[2]), back_rows(got[3])])
        gradient_mamba = got[4]
    else:
        got = [pieces[:, cuts[i] : cuts[i + 1]] for i in range(5)]

        def over_rows(values):
            return cube_scatter(from_rows(values).reshape(nd, block, -1), nd)

        def over_lanes(values):
            return cube_scatter(from_lanes(values).reshape(-1, nd, block).transpose(1, 0, 2), nd)

        gradient_query = over_rows(got[0])
        gradient_attend = over_lanes(got[1])
        gradient_inner = jnp.stack([over_rows(got[2]), over_rows(got[3])])
        gradient_mamba = over_lanes(got[4])
    shared_cut = shared_pieces.reshape(nd, nt, width // (nd * nt), -1)
    gradient_shared = chain_scatter(cube_scatter(shared_cut, nd, BF16), nt)

    n_tap = CONV + 1
    over_all = jnp.concatenate(
        [grad_gain_one, grad_gain_two.reshape(-1), grad_tb[:n_tap].reshape(-1)]
    )
    over_dp = jnp.concatenate(
        [
            grad_tx[:n_tap].reshape(-1),
            grad_rows[0],
            grad_rows[1].reshape(heads, SSM_DIM).sum(axis=1),
            grad_heads[:heads].sum(axis=1),
            grad_heads[8 : 8 + heads].sum(axis=1),
            grad_step[:heads].reshape(-1),
        ]
    )
    n_all = over_all.shape[0]
    over_dp = lax.psum(jnp.concatenate([over_all, over_dp]), "dp")
    over_all = lax.psum(over_dp[:n_all], "tensor")
    over_dp = over_dp[n_all:]
    place = d * nt + tensor_index
    norm_w = width // (nd * nt)
    gradient_norms = lax.dynamic_slice_in_dim(
        over_all[: 2 * width].reshape(2, width), place * norm_w, norm_w, 1
    )
    tap_w = shared_taps.shape[1]
    gradient_taps = lax.dynamic_slice_in_dim(
        over_all[2 * width :].reshape(n_tap, -1), place * tap_w, tap_w, 1
    )
    part = mixer_gain.shape[1]
    n_taps = n_tap * inner
    chan = over_dp[:n_taps].reshape(n_tap, heads, SSM_DIM)
    gain = over_dp[n_taps : n_taps + inner].reshape(heads, SSM_DIM)
    gradient_channel = lax.dynamic_slice_in_dim(chan, d * part, part, 2)
    gradient_mixer = lax.dynamic_slice_in_dim(gain, d * part, part, 1)
    rest = over_dp[n_taps + inner :]
    gradient_skip = rest[:heads]
    gradient_decay = rest[heads : 2 * heads]
    gradient_bias = rest[2 * heads : 3 * heads]
    step_all = rest[3 * heads :].reshape(heads, width)
    gradient_step = lax.dynamic_slice_in_dim(step_all, d * block, block, 1).T
    return (
        layer_out,
        gradient_tokens,
        gradient_query,
        gradient_attend,
        gradient_inner,
        gradient_step,
        gradient_mamba,
        gradient_hidden,
        gradient_down,
        gradient_channel,
        gradient_mixer,
        gradient_decay,
        gradient_bias,
        gradient_skip,
        gradient_shared,
        gradient_norms,
        gradient_taps,
    )


def solution(mesh):
    placed = (
        P(("dp", "tensor"), None),
        P("dp", "tensor"),
        P("tensor", "dp"),
        P(None, "dp", "tensor"),
        P("dp", "tensor"),
        P("tensor", "dp"),
        P(None, "dp", "tensor"),
        P("tensor", "dp"),
        P(None, "tensor", "dp"),
        P("tensor", "dp"),
        P("tensor"),
        P("tensor"),
        P("tensor"),
        P(("dp", "tensor"), None),
        P(None, ("dp", "tensor")),
        P(None, ("dp", "tensor")),
        P(("dp", "tensor"), None),
    )
    return jax.shard_map(
        partial(per_device, mesh.shape["dp"], mesh.shape["tensor"]),
        mesh=mesh,
        in_specs=placed,
        out_specs=(
            P(("dp", "tensor"), None),
            P(("dp", "tensor"), None),
            P("dp", "tensor"),
            P("tensor", "dp"),
            P(None, "dp", "tensor"),
            P("dp", "tensor"),
            P("tensor", "dp"),
            P(None, "dp", "tensor"),
            P("tensor", "dp"),
            P(None, "tensor", "dp"),
            P("tensor", "dp"),
            P("tensor"),
            P("tensor"),
            P("tensor"),
            P(("dp", "tensor"), None),
            P(None, ("dp", "tensor")),
            P(None, ("dp", "tensor")),
        ),
        check_vma=False,
    )
```

time: 886 us -> 584 us (0.66)
  local copies, waits for them, and re-layouts: 226 us -> 49.7 us
  matrix products: 144 us -> 0 us
  Pallas kernels: 49.2 us -> 167 us
  other arithmetic: 117 us -> 41.5 us
  blocking collectives: 97.6 us -> 61.8 us
  starting transfers between devices: 101 us -> 112 us
    dot_general x47 -> x0, matrix products: 142 us -> none  [the longest x10 31.2 us: right_contract(): jnp.einsum('mk,dk->md', left, right, preferred_element_type=jnp.float32)]
    pallas_call x0 -> x8, Pallas kernels: none -> 106 us  [the longest x1 23.2 us: scan_back(): pl.pallas_call(partial(scan_back_kernel, heads, channels), grid=(steps,),...]
    dynamic_slice x36 -> x1, local copies, waits for them, and re-layouts: 39.5 us -> 0.66 us  [per_device(): lax.dynamic_slice_in_dim(over_all[2 * width:].reshape(n_tap, -1), place *...]
    ppermute x20, waiting for transfers between devices: 55.3 us -> 20.8 us  [swap(): return lax.ppermute(values, 'dp', [(i, i ^ bit) for i in range(8)])]
    another operation x9 -> x2, local copies, waits for them, and re-layouts: 32.2 us -> 0.72 us  [the longest x1 0.64 us: per_device(): skip = jnp.repeat(skip_weight.astype(F32), SSM_DIM)[None, :]]
    unnamed x427 -> x66, local copies, waits for them, and re-layouts: 34.7 us -> 4.7 us
    reduce_sum x16 -> x2, other arithmetic: 27.2 us -> 1.29 us  [the longest x1 0.66 us: per_device(): grad_heads[8:8 + heads].sum(axis=1)]
    ppermute x15, waiting for transfers between devices: 26.3 us -> 50.1 us  [chain_scatter(): right = lax.ppermute(to_right, 'tensor', [(i, i + 1) for i in range(t + 1)])]
  transfers between devices with their start and end apart: 59 -> 58, of which waited for: 23 -> 26; matrix products, arithmetic and copies ran while one was open for 51% -> 15% of each run, Pallas kernels for 0% -> 26%
where the time goes in v2:
time: 584 us; the launch traced here: 574 us
  Pallas kernels  167 us (29%)
  waiting for transfers between devices  125 us (21%)
  starting transfers between devices  112 us (19%)
  blocking collectives  61.8 us (11%)
  local copies, waits for them, and re-layouts  49.7 us (9%)
  other arithmetic  41.5 us (7%)
  between operations  15.7 us (3%)
    ppermute x15, starting transfers between devices, chain_scatter(): right = lax.ppermute(to_right, 'tensor', [(i, i + 1) for i in range(t + 1)])  61.7 us
    pallas_call x1, Pallas kernels, gather_start(): pl.pallas_call(partial(gather_kernel, nt), out_shape=[jax.ShapeDtypeStruc...  61.4 us
    ppermute x15, waiting for transfers between devices, chain_scatter(): right = lax.ppermute(to_right, 'tensor', [(i, i + 1) for i in range(t + 1)])  50.1 us
    ppermute x3, waiting for transfers between devices, chain_gather(): lax.ppermute(left, 'tensor', [(i, i - 1) for i in range(1, nt - dist + 1)])  25.5 us
    ppermute x20, starting transfers between devices, swap(): return lax.ppermute(values, 'dp', [(i, i ^ bit) for i in range(8)])  25.1 us
    pallas_call x1, Pallas kernels, scan_back(): pl.pallas_call(partial(scan_back_kernel, heads, channels), grid=(steps,),...  23.2 us
    ppermute x15, waiting for transfers between devices, chain_scatter(): lax.ppermute(to_left, 'tensor', [(nt - 1 - i, nt - 2 - i) for i in range(...  23.1 us
    pallas_call x1, Pallas kernels, mixers_forward(): pl.pallas_call(partial(forward_kernel, heads), grid=(total // rows,), in_...  23 us
  transfers between devices with their start and end apart: 58, of which 26 were waited for; matrix products, arithmetic and copies ran while one was open for 15% of the time, Pallas kernels for 26%

profile of v2, /device:TPU:0, one launch (start us, length us, event | category | flops | bytes accessed | tf_op | source)
XLA Modules:
  0.0 573.6 jit_solution(11544135421304299499)
XLA Ops:
  13.2 61.4 %gather_start.1 = (bf16[4,256,1024]{2,1,0:T(8,128)(2,1)}, bf16[1024,128]{1,0:T(8,128)(2,1)}, bf16[128,1024]{1,0:T(8,128)(2,1)}, bf16[2,1024,384]{2,1,0:T(8,128)(...) custom-call(bf16[256,1024]{1,0:T(8,128)(2,1)} %refs_0_.1, ...), custom_call_target="tpu_custom_call" | custom-call | tf_op jit(solution)/shard_map/gather_start/pallas_call | solution.py:214
  81.4 23.0 %mixers_forward.1 = (bf16[1024,1024]{1,0:T(8,128)(2,1)}, bf16[1024,128]{1,0:T(8,128)(2,1)}, bf16[1024,128]{1,0:T(8,128)(2,1)}, bf16[1024,128]{1,0:T(8,128)(2,1)}...) custom-call(s32[1]{0:T(128)} %bitcast.kvh, ...), custom_call_target="tpu_custom_call" | custom-call | flops 5000000000 | bytes 15000000 | tf_op jit(solution)/shard_map/mixers_forward/pallas_call | solution.py:511
  106.0 10.5 %psum.28 = f32[1024]{0:T(1024)S(1)} all-reduce(f32[1024]{0:T(1024)S(1)} %bitcast.374), channel_id=1, replica_groups=mesh['dp'=8,'tensor'=4] {'tensor'}, use_global_device_ids=true, to_apply=%region_0.1 | all-reduce | flops 1024 | bytes 8192 | tf_op jit(solution)/shard_map/psum | solution.py:299
  117.2 6.2 %mix_parts.1 = (bf16[1024,384]{1,0:T(8,128)(2,1)}, bf16[1024,1024]{1,0:T(8,128)(2,1)}) custom-call(bf16[1024,128]{1,0:T(8,128)(2,1)} %get-tuple-element.66.o, f32[1024,384]{1,0:T(8,128)} %get-tuple-element.67.y, f32[1024,384]{1,0:T(8,128)} %get-tuple-element.68.z.zr, f32[8,1024]{1,0:T(8,128)} %broadcast_in_dim.56.sq.rsum, f32[1,384]{1,0:T(1,128)} %reshape.334.gain, ...), custom_call_target="tpu_custom_call" | custom-call | flops 1000000000 | bytes 7000000 | tf_op jit(solution)/shard_map/mix_parts/pallas_call | solution.py:913
  123.4 2.2 dynamic-slice_bitcast_fusion.13
  128.9 14.2 %collective-permute-done = bf16[256,1024]{1,0:T(8,128)(2,1)S(1)} collective-permute-done((bf16[256,1024]{1,0:T(8,128)(2,1)S(1)}, bf16[256,1024]{1,0:T(8,128)(2,1)S(1)}, u32[]{:S(2)}, u32[]{:S(2)}) %collective-permute-start) | collective-permute-done | bytes 524320 | tf_op jit(solution)/shard_map/ppermute | solution.py:267
  143.2 5.2 collective-permute-start.1
  148.4 19.8 %collective-permute-done.1 = bf16[256,1024]{1,0:T(8,128)(2,1)} collective-permute-done((bf16[256,1024]{1,0:T(8,128)(2,1)S(1)}, bf16[256,1024]{1,0:T(8,128)(2,1)}, u32[]{:S(2)}, u32[]{:S(2)}) %collective-permute-start.1) | collective-permute-done | bytes 524320 | tf_op jit(solution)/shard_map/ppermute | solution.py:267
  168.2 2.6 fusion.24
  172.2 4.4 collective-permute-start.2
  176.6 2.0 fusion.22
  180.8 2.7 collective-permute-done.2
  183.5 14.0 %collective-permute-done.5 = bf16[256,1024]{1,0:T(8,128)(2,1)} collective-permute-done((bf16[256,1024]{1,0:T(8,128)(2,1)}, bf16[256,1024]{1,0:T(8,128)(2,1)}, u32[]{:S(2)}, u32[]{:S(2)}) %collective-permute-start.5) | collective-permute-done | bytes 524320 | tf_op jit(solution)/shard_map/ppermute | solution.py:268
  197.6 2.3 fusion.7
  199.9 20.1 %feed_forward.1 = (bf16[256,1024]{1,0:T(8,128)(2,1)}, f32[256,1024]{1,0:T(8,128)}, bf16[256,1024]{1,0:T(8,128)(2,1)}, f32[1,1024]{1,0:T(1,128)}, bf16[8,4,2,128,...) custom-call(f32[256,1024]{1,0:T(8,128)} %get-tuple-element.191.hid, f32[1,1024]{1,0:T(1,128)} %slice.148.gain, ...), custom_call_target="tpu_custom_call" | custom-call | flops 10000000000 | bytes 26000000 | tf_op jit(solution)/shard_map/feed_forward/pallas_call | solution.py:872
  220.1 4.1 collective-permute-start.6
  226.5 4.6 collective-permute-done.6
  231.8 3.2 dynamic-slice_bitcast_fusion.1
  236.9 4.7 dynamic-slice_bitcast_fusion
  242.7 11.1 %collective-permute-done.9 = bf16[256,1024]{1,0:T(8,128)(2,1)S(1)} collective-permute-done((bf16[256,1024]{1,0:T(8,128)(2,1)S(1)}, bf16[256,1024]{1,0:T(8,128)(2,1)S(1)}, u32[]{:S(2)}, u32[]{:S(2)}) %collective-permute-start.9) | collective-permute-done | bytes 524320 | tf_op jit(solution)/shard_map/ppermute | solution.py:243
  255.8 13.7 %collective-permute-done.11 = bf16[256,1024]{1,0:T(8,128)(2,1)S(1)} collective-permute-done((bf16[256,1024]{1,0:T(8,128)(2,1)S(1)}, bf16[256,1024]{1,0:T(8,128)(2,1)S(1)}, u32[]{:S(2)}, u32[]{:S(2)}) %collective-permute-start.11) | collective-permute-done | bytes 524320 | tf_op jit(solution)/shard_map/ppermute | solution.py:243
  271.0 5.9 %unmix.1 = (bf16[1024,128]{1,0:T(8,128)(2,1)}, f32[1024,384]{1,0:T(8,128)}, f32[8,1024]{1,0:T(8,128)}) custom-call(bf16[1024,1024]{1,0:T(8,128)(2,1)} %bitcast.337, f32[1024,384]{1,0:T(8,128)} %get-tuple-element.67.y, f32[1024,384]{1,0:T(8,128)} %get-tuple-element.68.z.zr, f32[1,384]{1,0:T(1,128)} %reshape.334.gain, ...), custom_call_target="tpu_custom_call" | custom-call | flops 1000000000 | bytes 7000000 | tf_op jit(solution)/shard_map/unmix/pallas_call | solution.py:947
  277.7 8.7 %psum.29 = f32[1024]{0:T(1024)S(1)} all-reduce(f32[1024]{0:T(1024)S(1)} %bitcast.375), channel_id=1, replica_groups=mesh['dp'=8,'tensor'=4] {'tensor'}, use_global_device_ids=true, to_apply=%region_1.2 | all-reduce | flops 1024 | bytes 8192 | tf_op jit(solution)/shard_map/psum | solution.py:299
  286.4 9.1 %attend_back.1 = (bf16[1024,128]{1,0:T(8,128)(2,1)}, bf16[1024,256]{1,0:T(8,128)(2,1)}) custom-call(s32[1]{0:T(128)} %bitcast.kvh, bf16[1024,128]{1,0:T(8,128)(2,1)} %get-tuple-element.75.q, bf16[1024,128]{1,0:T(8,128)(2,1)} %get-tuple-element.76.k2, bf16[1024,128]{1,0:T(8,128)(2,1)} %get-tuple-element.77.v2, f32[8,1024]{1,0:T(8,128)} %get-tuple-element.78.lse, ...), custom_call_target="tpu_custom_call" | custom-call | flops 2000000000 | bytes 3000000 | tf_op jit(solution)/shard_map/attend_back/pallas_call | solution.py:595
  296.1 23.2 %scan_back.1 = (bf16[1024,384]{1,0:T(8,128)(2,1)}, bf16[1024,384]{1,0:T(8,128)(2,1)}, bf16[1024,256]{1,0:T(8,128)(2,1)}, f32[8,1024]{1,0:T(8,128)}, f32[8,384]{1...) custom-call(f32[1024,384]{1,0:T(8,128)} %get-tuple-element.82.dm, ...), custom_call_target="tpu_custom_call" | custom-call | flops 4000000000 | bytes 15000000 | tf_op jit(solution)/shard_map/scan_back/pallas_call | solution.py:783
  319.3 9.7 %weight_pieces.1 = (bf16[8,1408,128]{2,1,0:T(8,128)(2,1)}, bf16[8,128,512]{2,1,0:T(8,128)(2,1)}, f32[8,1024]{1,0:T(8,128)}) custom-call(bf16[1024,1024]{1,0:T(8,128)(2,1)} %get-tuple-element.93.a1, bf16[1024,128]{1,0:T(8,128)(2,1)} %get-tuple-element.81.dq, bf16[1024,384]{1,0:T(8,128)(2,1)} %get-tuple-element.88.dz, bf16[1024,384]{1,0:T(8,128)(2,1)} %get-tuple-element.89.dx, ...), custom_call_target="tpu_custom_call" | custom-call | flops 4000000000 | bytes 12000000 | tf_op jit(solution)/shard_map/weight_pieces/pallas_call | solution.py:1031
  329.1 1.9 dynamic-slice_bitcast_fusion.5
  331.8 8.5 %down_parts.1 = bf16[1024,1024]{1,0:T(8,128)(2,1)} custom-call(bf16[1024,128]{1,0:T(8,128)(2,1)} %get-tuple-element.81.dq, bf16[1024,384]{1,0:T(8,128)(2,1)} %get-tuple-element.88.dz, bf16[1024,384]{1,0:T(8,128)(2,1)} %get-tuple-element.89.dx, bf16[1024,256]{1,0:T(8,128)(2,1)} %get-tuple-element.90.dkv, bf16[1024,256]{1,0:T(8,128)(2,1)} %get-tuple-element.91.db, ...), custom_call_target="tpu_custom_call" | custom-call | flops 3000000000 | bytes 8000000 | tf_op jit(solution)/shard_map/down_parts/pallas_call | solution.py:976
  340.2 2.3 dynamic-slice_bitcast_fusion.11
  342.5 4.1 collective-permute-start.12
  349.7 2.8 fusion.1
  356.1 7.4 %collective-permute-start.46 = (bf16[2,2,32,512]{3,2,1,0:T(8,128)(2,1)S(1)}, bf16[2,2,32,512]{3,2,1,0:T(8,128)(2,1)S(1)}, u32[]{:S(2)}, u32[]{:S(2)}) collective-permute-start(bf16[2,2,32,512]{3,2,1,0:T(8,128)(2,1)S(1)} %dynamic-slice_bitcast_fusion.21), channel_id=1, source_target_pairs={{0,8},{4,12},{8,0},{12,4},{16,24},{20,28},{24,16},{28,20},{1,9},{5... | collective-permute-start | bytes 393224 | tf_op jit(solution)/shard_map/ppermute | solution.py:282
  363.5 3.9 collective-permute-start.49
  367.4 1.8 collective-permute-start.47
  369.7 2.1 collective-permute-done.47
  376.5 4.2 collective-permute-start.51
  382.4 6.1 %collective-permute-start.52 = (bf16[32,512]{1,0:T(8,128)(2,1)S(1)}, bf16[32,512]{1,0:T(8,128)(2,1)S(1)}, u32[]{:S(2)}, u32[]{:S(2)}) collective-permute-start(bf16[32,512]{1,0:T(8,128)(2,1)S(1)} %get-tuple-element.197), channel_id=1, source_target_pairs={{0,1},{1,2},{2,3},{4,5},{5,6},{6,7},{8,9},{9,10},{10,11},{12,13},{... | collective-permute-start | bytes 98312 | tf_op jit(solution)/shard_map/ppermute | solution.py:267
  390.2 4.2 collective-permute-done.35
  395.4 1.8 collective-permute-start.36
  397.8 3.0 collective-permute-done.38
  400.8 4.2 collective-permute-start.13
  405.4 2.2 collective-permute-start.39
  408.4 3.4 collective-permute-done.13
  414.7 4.4 collective-permute-start.14
  419.3 4.2 collective-permute-start.40
  424.8 3.7 collective-permute-done.40
  428.6 4.8 collective-permute-start.41
  437.6 4.6 collective-permute-done.44
  446.5 5.3 collective-permute-done.22
  451.9 3.7 fusion
  457.3 1.8 collective-permute-start.26
  464.7 1.8 pad_maximum_fusion
  466.5 1.9 copy.87
  469.1 2.4 fusion.10
  472.3 22.7 %psum.30 = f32[11794]{0:T(1024)S(1)} all-reduce(f32[11794]{0:T(1024)S(1)} %concatenate.23), channel_id=1, replica_groups=mesh['dp'=8,'tensor'=4] {'dp'}, use_global_device_ids=true, to_apply=%region_8.9 | all-reduce | flops 11794 | bytes 94352 | tf_op jit(solution)/shard_map/psum | solution.py:1238
  495.0 19.8 %psum.31 = f32[3328]{0:T(1024)S(1)} all-reduce(f32[3328]{0:T(1024)S(1)} %slice.205), channel_id=1, replica_groups=mesh['dp'=8,'tensor'=4] {'tensor'}, use_global_device_ids=true, to_apply=%region_9.10 | all-reduce | flops 3328 | bytes 26624 | tf_op jit(solution)/shard_map/psum | solution.py:1239
  514.9 2.0 fusion.3
  524.3 2.9 collective-permute-done.27
  528.4 2.8 collective-permute-done.25
  533.4 2.0 collective-permute-start.28
  540.2 4.4 collective-permute-start.29
  545.3 2.3 fusion.6
  548.7 8.5 %collective-permute-start.30 = (bf16[2,128,512]{2,1,0:T(8,128)(2,1)S(1)}, bf16[2,128,512]{2,1,0:T(8,128)(2,1)S(1)}, u32[]{:S(2)}, u32[]{:S(2)}) collective-permute-start(bf16[2,128,512]{2,1,0:T(8,128)(2,1)S(1)} %get-tuple-element.176), channel_id=1, source_target_pairs={{0,1},{1,2},{2,3},{4,5},{5,6},{6,7},{8,9},{9,10},{10,11},{12,13},{... | collective-permute-start | bytes 786440 | tf_op jit(solution)/shard_map/ppermute | solution.py:267
  561.1 4.4 collective-permute-done.33
  (289 shorter events, 94.7 us)
Async XLA Ops:
  7.2 70.4 %copy-start.25 = (bf16[6]{0:T(256)(128)(2,1)S(1)}, bf16[6]{0:T(256)(128)(2,1)}, u32[]{:S(2)}) copy-start(bf16[6]{0:T(256)(128)(2,1)} %param.31) | copy-start | bytes 40
  7.2 71.7 %copy-start.26 = (bf16[6]{0:T(256)(128)(2,1)S(1)}, bf16[6]{0:T(256)(128)(2,1)}, u32[]{:S(2)}) copy-start(bf16[6]{0:T(256)(128)(2,1)} %param.29) | copy-start | bytes 40
  7.2 71.7 %copy-start.27 = (bf16[6]{0:T(256)(128)(2,1)S(1)}, bf16[6]{0:T(256)(128)(2,1)}, u32[]{:S(2)}) copy-start(bf16[6]{0:T(256)(128)(2,1)} %param.30) | copy-start | bytes 40
  7.2 192.7 %all-gather.7.cloned.1.call-start = ((), (), s32[]{:S(2)}) async-start(), calls=%async_computation.1 | async-start | bytes 4325376 | tf_op jit(solution)/shard_map/all_gather | solution.py:1107
  8.0 192.0 %all-gather.5.cloned.1.call-start = ((), (), s32[]{:S(2)}) async-start(), calls=%async_computation | async-start | bytes 8650752 | tf_op jit(solution)/shard_map/all_gather | solution.py:1104
  125.6 17.4 %collective-permute-start = (bf16[256,1024]{1,0:T(8,128)(2,1)S(1)}, bf16[256,1024]{1,0:T(8,128)(2,1)S(1)}, u32[]{:S(2)}, u32[]{:S(2)}) collective-permute-start(bf16[256,1024]{1,0:T(8,128)(2,1)S(1)} %get-tuple-element.172), channel_id=1, source_target_pairs={{0,1},{4,5},{8,9},{12,13},{16,17},{20,21},{24,25},{28,29}} | collective-permute-start | bytes 1572872 | tf_op jit(solution)/shard_map/ppermute | solution.py:267
  127.4 21.0 %collective-permute-start.3 = (bf16[256,1024]{1,0:T(8,128)(2,1)}, bf16[256,1024]{1,0:T(8,128)(2,1)}, u32[]{:S(2)}, u32[]{:S(2)}) collective-permute-start(bf16[256,1024]{1,0:T(8,128)(2,1)} %get-tuple-element.173), channel_id=1, source_target_pairs={{3,2},{7,6},{11,10},{15,14},{19,18},{23,22},{27,26},{31,30}} | collective-permute-start | bytes 1572872 | tf_op jit(solution)/shard_map/ppermute | solution.py:268
  143.2 25.0 %collective-permute-start.1 = (bf16[256,1024]{1,0:T(8,128)(2,1)S(1)}, bf16[256,1024]{1,0:T(8,128)(2,1)}, u32[]{:S(2)}, u32[]{:S(2)}) collective-permute-start(bf16[256,1024]{1,0:T(8,128)(2,1)S(1)} %fusion.23), channel_id=1, source_target_pairs={{0,1},{1,2},{4,5},{5,6},{8,9},{9,10},{12,13},{13,14},{16,17},{17,1... | collective-permute-start | bytes 1572872 | tf_op jit(solution)/shard_map/ppermute | solution.py:267
  148.4 49.2 %copy-start.2 = (bf16[256,1024]{1,0:T(8,128)(2,1)S(1)}, bf16[256,1024]{1,0:T(8,128)(2,1)}, u32[]{:S(2)}) copy-start(bf16[256,1024]{1,0:T(8,128)(2,1)} %refs_0_.1) | copy-start | bytes 1572868
  170.8 5.8 %collective-permute-start.4 = (bf16[256,1024]{1,0:T(8,128)(2,1)}, bf16[256,1024]{1,0:T(8,128)(2,1)}, u32[]{:S(2)}, u32[]{:S(2)}) collective-permute-start(bf16[256,1024]{1,0:T(8,128)(2,1)} %get-tuple-element.171), channel_id=1, source_target_pairs={{3,2},{2,1},{7,6},{6,5},{11,10},{10,9},{15,14},{14,13},{19,18},{18... | collective-permute-start | bytes 1572872 | tf_op jit(solution)/shard_map/ppermute | solution.py:268
  172.2 11.3 %collective-permute-start.2 = (bf16[256,1024]{1,0:T(8,128)(2,1)}, bf16[256,1024]{1,0:T(8,128)(2,1)S(1)}, u32[]{:S(2)}, u32[]{:S(2)}) collective-permute-start(bf16[256,1024]{1,0:T(8,128)(2,1)} %get-tuple-element.170), channel_id=1, source_target_pairs={{0,1},{1,2},{2,3},{4,5},{5,6},{6,7},{8,9},{9,10},{10,11},{12,13},{... | collective-permute-start | bytes 1572872 | tf_op jit(solution)/shard_map/ppermute | solution.py:267
  178.6 19.0 %collective-permute-start.5 = (bf16[256,1024]{1,0:T(8,128)(2,1)}, bf16[256,1024]{1,0:T(8,128)(2,1)}, u32[]{:S(2)}, u32[]{:S(2)}) collective-permute-start(bf16[256,1024]{1,0:T(8,128)(2,1)} %fusion.22), channel_id=1, source_target_pairs={{3,2},{2,1},{1,0},{7,6},{6,5},{5,4},{11,10},{10,9},{9,8},{15,14},{... | collective-permute-start | bytes 1572872 | tf_op jit(solution)/shard_map/ppermute | solution.py:268
  220.1 11.0 %collective-permute-start.6 = (bf16[256,1024]{1,0:T(8,128)(2,1)}, bf16[256,1024]{1,0:T(8,128)(2,1)S(1)}, u32[]{:S(2)}, u32[]{:S(2)}) collective-permute-start(bf16[256,1024]{1,0:T(8,128)(2,1)} %get-tuple-element.79), channel_id=1, source_target_pairs={{0,1},{1,2},{2,3},{4,5},{5,6},{6,7},{8,9},{9,10},{10,11},{12,13},{... | collective-permute-start | bytes 1572872 | tf_op jit(solution)/shard_map/ppermute | solution.py:242
  224.3 11.3 %collective-permute-start.7 = (bf16[256,1024]{1,0:T(8,128)(2,1)}, bf16[256,1024]{1,0:T(8,128)(2,1)S(1)}, u32[]{:S(2)}, u32[]{:S(2)}) collective-permute-start(bf16[256,1024]{1,0:T(8,128)(2,1)} %get-tuple-element.79), channel_id=1, source_target_pairs={{1,0},{2,1},{3,2},{5,4},{6,5},{7,6},{9,8},{10,9},{11,10},{13,12},{... | collective-permute-start | bytes 1572872 | tf_op jit(solution)/shard_map/ppermute | solution.py:243
  231.1 10.6 %collective-permute-start.8 = (bf16[256,1024]{1,0:T(8,128)(2,1)S(1)}, bf16[256,1024]{1,0:T(8,128)(2,1)S(1)}, u32[]{:S(2)}, u32[]{:S(2)}) collective-permute-start(bf16[256,1024]{1,0:T(8,128)(2,1)S(1)} %collective-permute-done.6), channel_id=1, source_target_pairs={{1,2},{2,3},{5,6},{6,7},{9,10},{10,11},{13,14},{14,15},{17,18},{18... | collective-permute-start | bytes 1572872 | tf_op jit(solution)/shard_map/ppermute | solution.py:242
  235.0 114.8 %collective-permute-start.34 = (bf16[4,4,512,128]{3,2,1,0:T(8,128)(2,1)}, bf16[4,4,512,128]{3,2,1,0:T(8,128)(2,1)}, u32[]{:S(2)}, u32[]{:S(2)}) collective-permute-start(bf16[4,4,512,128]{3,2,1,0:T(8,128)(2,1)} %dynamic-slice_bitcast_fusion.1), channel_id=1, source_target_pairs={{0,4},{4,0},{8,12},{12,8},{16,20},{20,16},{24,28},{28,24},{1,5},{5... | collective-permute-start | bytes 6291464 | tf_op jit(solution)/shard_map/ppermute | solution.py:282
  235.6 18.2 %collective-permute-start.9 = (bf16[256,1024]{1,0:T(8,128)(2,1)S(1)}, bf16[256,1024]{1,0:T(8,128)(2,1)S(1)}, u32[]{:S(2)}, u32[]{:S(2)}) collective-permute-start(bf16[256,1024]{1,0:T(8,128)(2,1)S(1)} %collective-permute-done.7), channel_id=1, source_target_pairs={{1,0},{2,1},{5,4},{6,5},{9,8},{10,9},{13,12},{14,13},{17,16},{18,1... | collective-permute-start | bytes 1572872 | tf_op jit(solution)/shard_map/ppermute | solution.py:243
  241.6 210.3 %collective-permute-start.23 = (bf16[4,4,2,128,512]{4,3,2,1,0:T(8,128)(2,1)}, bf16[4,4,2,128,512]{4,3,2,1,0:T(8,128)(2,1)}, u32[]{:S(2)}, u32[]{:S(2)}) collective-permute-start(bf16[4,4,2,128,512]{4,3,2,1,0:T(8,128)(2,1)} %dynamic-slice_bitcast_fusion), channel_id=1, source_target_pairs={{0,4},{4,0},{8,12},{12,8},{16,20},{20,16},{24,28},{28,24},{1,5},{5... | collective-permute-start | bytes 12582920 | tf_op jit(solution)/shard_map/ppermute | solution.py:282
  241.8 13.8 %collective-permute-start.10 = (bf16[256,1024]{1,0:T(8,128)(2,1)S(1)}, bf16[256,1024]{1,0:T(8,128)(2,1)S(1)}, u32[]{:S(2)}, u32[]{:S(2)}) collective-permute-start(bf16[256,1024]{1,0:T(8,128)(2,1)S(1)} %collective-permute-done.8), channel_id=1, source_target_pairs={{2,3},{6,7},{10,11},{14,15},{18,19},{22,23},{26,27},{30,31}} | collective-permute-start | bytes 1572872 | tf_op jit(solution)/shard_map/ppermute | solution.py:242
  253.8 15.6 %collective-permute-start.11 = (bf16[256,1024]{1,0:T(8,128)(2,1)S(1)}, bf16[256,1024]{1,0:T(8,128)(2,1)S(1)}, u32[]{:S(2)}, u32[]{:S(2)}) collective-permute-start(bf16[256,1024]{1,0:T(8,128)(2,1)S(1)} %collective-permute-done.9), channel_id=1, source_target_pairs={{1,0},{5,4},{9,8},{13,12},{17,16},{21,20},{25,24},{29,28}} | collective-permute-start | bytes 1572872 | tf_op jit(solution)/shard_map/ppermute | solution.py:243
  331.0 21.7 %collective-permute-start.45 = (bf16[4,4,32,512]{3,2,1,0:T(8,128)(2,1)}, bf16[4,4,32,512]{3,2,1,0:T(8,128)(2,1)}, u32[]{:S(2)}, u32[]{:S(2)}) collective-permute-start(bf16[4,4,32,512]{3,2,1,0:T(8,128)(2,1)} %dynamic-slice_bitcast_fusion.5), channel_id=1, source_target_pairs={{0,4},{4,0},{8,12},{12,8},{16,20},{20,16},{24,28},{28,24},{1,5},{5... | collective-permute-start | bytes 1572872 | tf_op jit(solution)/shard_map/ppermute | solution.py:282
  342.5 38.3 %collective-permute-start.12 = (bf16[256,1024]{1,0:T(8,128)(2,1)}, bf16[256,1024]{1,0:T(8,128)(2,1)S(1)}, u32[]{:S(2)}, u32[]{:S(2)}) collective-permute-start(bf16[256,1024]{1,0:T(8,128)(2,1)} %get-tuple-element.168), channel_id=1, source_target_pairs={{0,1},{4,5},{8,9},{12,13},{16,17},{20,21},{24,25},{28,29}} | collective-permute-start | bytes 1572872 | tf_op jit(solution)/shard_map/ppermute | solution.py:267
  348.8 74.7 %collective-permute-start.18 = (bf16[4,1408,128]{2,1,0:T(8,128)(2,1)S(1)}, bf16[4,1408,128]{2,1,0:T(8,128)(2,1)S(1)}, u32[]{:S(2)}, u32[]{:S(2)}) collective-permute-start(bf16[4,1408,128]{2,1,0:T(8,128)(2,1)S(1)} %dynamic-slice_bitcast_fusion.2), channel_id=1, source_target_pairs={{0,4},{4,0},{8,12},{12,8},{16,20},{20,16},{24,28},{28,24},{1,5},{5... | collective-permute-start | bytes 4325384 | tf_op jit(solution)/shard_map/ppermute | solution.py:282
  355.0 8.4 %collective-permute-start.48 = (bf16[2,2,32,512]{3,2,1,0:T(8,128)(2,1)S(1)}, bf16[2,2,32,512]{3,2,1,0:T(8,128)(2,1)S(1)}, u32[]{:S(2)}, u32[]{:S(2)}) collective-permute-start(bf16[2,2,32,512]{3,2,1,0:T(8,128)(2,1)S(1)} %dynamic-slice_bitcast_fusion.20), channel_id=1, source_target_pairs={{0,16},{4,20},{8,24},{12,28},{16,0},{20,4},{24,8},{28,12},{1,17},{... | collective-permute-start | bytes 393224 | tf_op jit(solution)/shard_map/ppermute | solution.py:282
  356.1 11.3 %collective-permute-start.46 = (bf16[2,2,32,512]{3,2,1,0:T(8,128)(2,1)S(1)}, bf16[2,2,32,512]{3,2,1,0:T(8,128)(2,1)S(1)}, u32[]{:S(2)}, u32[]{:S(2)}) collective-permute-start(bf16[2,2,32,512]{3,2,1,0:T(8,128)(2,1)S(1)} %dynamic-slice_bitcast_fusion.21), channel_id=1, source_target_pairs={{0,8},{4,12},{8,0},{12,4},{16,24},{20,28},{24,16},{28,20},{1,9},{5... | collective-permute-start | bytes 393224 | tf_op jit(solution)/shard_map/ppermute | solution.py:282
  363.5 6.1 %collective-permute-start.49 = (bf16[2,32,512]{2,1,0:T(8,128)(2,1)S(1)}, bf16[2,32,512]{2,1,0:T(8,128)(2,1)S(1)}, u32[]{:S(2)}, u32[]{:S(2)}) collective-permute-start(bf16[2,32,512]{2,1,0:T(8,128)(2,1)S(1)} %dynamic-slice_bitcast_fusion.22), channel_id=1, source_target_pairs={{0,8},{4,12},{8,0},{12,4},{16,24},{20,28},{24,16},{28,20},{1,9},{5... | collective-permute-start | bytes 196616 | tf_op jit(solution)/shard_map/ppermute | solution.py:282
  367.4 4.3 collective-permute-start.47
  371.9 2.9 collective-permute-start.50
  373.2 3.3 collective-permute-start.53
  374.7 13.8 %collective-permute-start.37 = (bf16[2,2,512,128]{3,2,1,0:T(8,128)(2,1)S(1)}, bf16[2,2,512,128]{3,2,1,0:T(8,128)(2,1)S(1)}, u32[]{:S(2)}, u32[]{:S(2)}) collective-permute-start(bf16[2,2,512,128]{3,2,1,0:T(8,128)(2,1)S(1)} %dynamic-slice_bitcast_fusion.6), channel_id=1, source_target_pairs={{0,16},{4,20},{8,24},{12,28},{16,0},{20,4},{24,8},{28,12},{1,17},{... | collective-permute-start | bytes 1572872 | tf_op jit(solution)/shard_map/ppermute | solution.py:282
  376.5 5.8 %collective-permute-start.51 = (bf16[32,512]{1,0:T(8,128)(2,1)S(1)}, bf16[32,512]{1,0:T(8,128)(2,1)S(1)}, u32[]{:S(2)}, u32[]{:S(2)}) collective-permute-start(bf16[32,512]{1,0:T(8,128)(2,1)S(1)} %get-tuple-element.199), channel_id=1, source_target_pairs={{0,1},{1,2},{4,5},{5,6},{8,9},{9,10},{12,13},{13,14},{16,17},{17,1... | collective-permute-start | bytes 98312 | tf_op jit(solution)/shard_map/ppermute | solution.py:267
  380.8 1.6 collective-permute-start.54
  382.3 12.1 %collective-permute-start.35 = (bf16[2,2,512,128]{3,2,1,0:T(8,128)(2,1)S(1)}, bf16[2,2,512,128]{3,2,1,0:T(8,128)(2,1)S(1)}, u32[]{:S(2)}, u32[]{:S(2)}) collective-permute-start(bf16[2,2,512,128]{3,2,1,0:T(8,128)(2,1)S(1)} %dynamic-slice_bitcast_fusion.7), channel_id=1, source_target_pairs={{0,8},{4,12},{8,0},{12,4},{16,24},{20,28},{24,16},{28,20},{1,9},{5... | collective-permute-start | bytes 1572872 | tf_op jit(solution)/shard_map/ppermute | solution.py:282
  382.4 12.2 %collective-permute-start.52 = (bf16[32,512]{1,0:T(8,128)(2,1)S(1)}, bf16[32,512]{1,0:T(8,128)(2,1)S(1)}, u32[]{:S(2)}, u32[]{:S(2)}) collective-permute-start(bf16[32,512]{1,0:T(8,128)(2,1)S(1)} %get-tuple-element.197), channel_id=1, source_target_pairs={{0,1},{1,2},{2,3},{4,5},{5,6},{6,7},{8,9},{9,10},{10,11},{12,13},{... | collective-permute-start | bytes 98312 | tf_op jit(solution)/shard_map/ppermute | solution.py:267
  388.6 6.8 %collective-permute-start.55 = (bf16[32,512]{1,0:T(8,128)(2,1)S(1)}, bf16[32,512]{1,0:T(8,128)(2,1)S(1)}, u32[]{:S(2)}, u32[]{:S(2)}) collective-permute-start(bf16[32,512]{1,0:T(8,128)(2,1)S(1)} %get-tuple-element.198), channel_id=1, source_target_pairs={{3,2},{2,1},{1,0},{7,6},{6,5},{5,4},{11,10},{10,9},{9,8},{15,14},{... | collective-permute-start | bytes 98312 | tf_op jit(solution)/shard_map/ppermute | solution.py:268
  394.4 6.4 %collective-permute-start.38 = (bf16[2,512,128]{2,1,0:T(8,128)(2,1)S(1)}, bf16[2,512,128]{2,1,0:T(8,128)(2,1)S(1)}, u32[]{:S(2)}, u32[]{:S(2)}) collective-permute-start(bf16[2,512,128]{2,1,0:T(8,128)(2,1)S(1)} %dynamic-slice_bitcast_fusion.16), channel_id=1, source_target_pairs={{0,8},{4,12},{8,0},{12,4},{16,24},{20,28},{24,16},{28,20},{1,9},{5... | collective-permute-start | bytes 786440 | tf_op jit(solution)/shard_map/ppermute | solution.py:282
  394.7 13.0 %collective-permute-start.15 = (bf16[256,1024]{1,0:T(8,128)(2,1)S(1)}, bf16[256,1024]{1,0:T(8,128)(2,1)S(1)}, u32[]{:S(2)}, u32[]{:S(2)}) collective-permute-start(bf16[256,1024]{1,0:T(8,128)(2,1)S(1)} %copy-done.18), channel_id=1, source_target_pairs={{3,2},{7,6},{11,10},{15,14},{19,18},{23,22},{27,26},{31,30}} | collective-permute-start | bytes 1572872 | tf_op jit(solution)/shard_map/ppermute | solution.py:268
  395.4 9.8 %collective-permute-start.36 = (bf16[2,512,128]{2,1,0:T(8,128)(2,1)S(1)}, bf16[2,512,128]{2,1,0:T(8,128)(2,1)S(1)}, u32[]{:S(2)}, u32[]{:S(2)}) collective-permute-start(bf16[2,512,128]{2,1,0:T(8,128)(2,1)S(1)} %dynamic-slice_bitcast_fusion.17), channel_id=1, source_target_pairs={{0,16},{4,20},{8,24},{12,28},{16,0},{20,4},{24,8},{28,12},{1,17},{... | collective-permute-start | bytes 786440 | tf_op jit(solution)/shard_map/ppermute | solution.py:282
  400.8 11.1 %collective-permute-start.13 = (bf16[256,1024]{1,0:T(8,128)(2,1)S(1)}, bf16[256,1024]{1,0:T(8,128)(2,1)S(1)}, u32[]{:S(2)}, u32[]{:S(2)}) collective-permute-start(bf16[256,1024]{1,0:T(8,128)(2,1)S(1)} %fusion.18), channel_id=1, source_target_pairs={{0,1},{1,2},{4,5},{5,6},{8,9},{9,10},{12,13},{13,14},{16,17},{17,1... | collective-permute-start | bytes 1572872 | tf_op jit(solution)/shard_map/ppermute | solution.py:267
  405.4 9.3 %collective-permute-start.39 = (bf16[512,128]{1,0:T(8,128)(2,1)S(1)}, bf16[512,128]{1,0:T(8,128)(2,1)S(1)}, u32[]{:S(2)}, u32[]{:S(2)}) collective-permute-start(bf16[512,128]{1,0:T(8,128)(2,1)S(1)} %get-tuple-element.188), channel_id=1, source_target_pairs={{0,1},{4,5},{8,9},{12,13},{16,17},{20,21},{24,25},{28,29}} | collective-permute-start | bytes 393224 | tf_op jit(solution)/shard_map/ppermute | solution.py:267
  407.6 11.5 %collective-permute-start.42 = (bf16[512,128]{1,0:T(8,128)(2,1)S(1)}, bf16[512,128]{1,0:T(8,128)(2,1)S(1)}, u32[]{:S(2)}, u32[]{:S(2)}) collective-permute-start(bf16[512,128]{1,0:T(8,128)(2,1)S(1)} %get-tuple-element.189), channel_id=1, source_target_pairs={{3,2},{7,6},{11,10},{15,14},{19,18},{23,22},{27,26},{31,30}} | collective-permute-start | bytes 393224 | tf_op jit(solution)/shard_map/ppermute | solution.py:268
  413.0 20.3 %collective-permute-start.16 = (bf16[256,1024]{1,0:T(8,128)(2,1)S(1)}, bf16[256,1024]{1,0:T(8,128)(2,1)S(1)}, u32[]{:S(2)}, u32[]{:S(2)}) collective-permute-start(bf16[256,1024]{1,0:T(8,128)(2,1)S(1)} %get-tuple-element.167), channel_id=1, source_target_pairs={{3,2},{2,1},{7,6},{6,5},{11,10},{10,9},{15,14},{14,13},{19,18},{18... | collective-permute-start | bytes 1572872 | tf_op jit(solution)/shard_map/ppermute | solution.py:268
  414.7 54.4 %collective-permute-start.14 = (bf16[256,1024]{1,0:T(8,128)(2,1)}, bf16[256,1024]{1,0:T(8,128)(2,1)S(1)}, u32[]{:S(2)}, u32[]{:S(2)}) collective-permute-start(bf16[256,1024]{1,0:T(8,128)(2,1)} %get-tuple-element.166), channel_id=1, source_target_pairs={{0,1},{1,2},{2,3},{4,5},{5,6},{6,7},{8,9},{9,10},{10,11},{12,13},{... | collective-permute-start | bytes 1572872 | tf_op jit(solution)/shard_map/ppermute | solution.py:267
  419.3 9.2 %collective-permute-start.40 = (bf16[512,128]{1,0:T(8,128)(2,1)S(1)}, bf16[512,128]{1,0:T(8,128)(2,1)S(1)}, u32[]{:S(2)}, u32[]{:S(2)}) collective-permute-start(bf16[512,128]{1,0:T(8,128)(2,1)S(1)} %get-tuple-element.186), channel_id=1, source_target_pairs={{0,1},{1,2},{4,5},{5,6},{8,9},{9,10},{12,13},{13,14},{16,17},{17,1... | collective-permute-start | bytes 393224 | tf_op jit(solution)/shard_map/ppermute | solution.py:267
  423.5 5.0 collective-permute-start.43
  424.2 27.7 %slice-start = ((s8[8388608]{0:T(1024)(128)(4,1)}), s8[4194304]{0:T(1024)(128)(4,1)S(1)}, s32[]{:S(2)}) async-start(s8[8388608]{0:T(1024)(128)(4,1)} %bitcast.342), calls=%async_computation.2 | async-start | bytes 8388608
  428.5 15.8 %collective-permute-start.21 = (bf16[2,704,128]{2,1,0:T(8,128)(2,1)S(1)}, bf16[2,704,128]{2,1,0:T(8,128)(2,1)S(1)}, u32[]{:S(2)}, u32[]{:S(2)}) collective-permute-start(bf16[2,704,128]{2,1,0:T(8,128)(2,1)S(1)} %dynamic-slice_bitcast_fusion.14), channel_id=1, source_target_pairs={{0,16},{4,20},{8,24},{12,28},{16,0},{20,4},{24,8},{28,12},{1,17},{... | collective-permute-start | bytes 1081352 | tf_op jit(solution)/shard_map/ppermute | solution.py:282
  428.6 7.3 %collective-permute-start.41 = (bf16[512,128]{1,0:T(8,128)(2,1)S(1)}, bf16[512,128]{1,0:T(8,128)(2,1)S(1)}, u32[]{:S(2)}, u32[]{:S(2)}) collective-permute-start(bf16[512,128]{1,0:T(8,128)(2,1)S(1)} %get-tuple-element.184), channel_id=1, source_target_pairs={{0,1},{1,2},{2,3},{4,5},{5,6},{6,7},{8,9},{9,10},{10,11},{12,13},{... | collective-permute-start | bytes 393224 | tf_op jit(solution)/shard_map/ppermute | solution.py:267
  433.4 8.8 %collective-permute-start.44 = (bf16[512,128]{1,0:T(8,128)(2,1)S(1)}, bf16[512,128]{1,0:T(8,128)(2,1)S(1)}, u32[]{:S(2)}, u32[]{:S(2)}) collective-permute-start(bf16[512,128]{1,0:T(8,128)(2,1)S(1)} %get-tuple-element.185), channel_id=1, source_target_pairs={{3,2},{2,1},{1,0},{7,6},{6,5},{5,4},{11,10},{10,9},{9,8},{15,14},{... | collective-permute-start | bytes 393224 | tf_op jit(solution)/shard_map/ppermute | solution.py:268
  435.9 10.3 %collective-permute-start.19 = (bf16[2,704,128]{2,1,0:T(8,128)(2,1)S(1)}, bf16[2,704,128]{2,1,0:T(8,128)(2,1)S(1)}, u32[]{:S(2)}, u32[]{:S(2)}) collective-permute-start(bf16[2,704,128]{2,1,0:T(8,128)(2,1)S(1)} %dynamic-slice_bitcast_fusion.15), channel_id=1, source_target_pairs={{0,8},{4,12},{8,0},{12,4},{16,24},{20,28},{24,16},{28,20},{1,9},{5... | collective-permute-start | bytes 1081352 | tf_op jit(solution)/shard_map/ppermute | solution.py:282
  442.2 26.9 %collective-permute-start.17 = (bf16[256,1024]{1,0:T(8,128)(2,1)}, bf16[256,1024]{1,0:T(8,128)(2,1)}, u32[]{:S(2)}, u32[]{:S(2)}) collective-permute-start(bf16[256,1024]{1,0:T(8,128)(2,1)} %fusion.17), channel_id=1, source_target_pairs={{3,2},{2,1},{1,0},{7,6},{6,5},{5,4},{11,10},{10,9},{9,8},{15,14},{... | collective-permute-start | bytes 1572872 | tf_op jit(solution)/shard_map/ppermute | solution.py:268
  444.4 7.4 %collective-permute-start.22 = (bf16[704,128]{1,0:T(8,128)(2,1)S(1)}, bf16[704,128]{1,0:T(8,128)(2,1)S(1)}, u32[]{:S(2)}, u32[]{:S(2)}) collective-permute-start(bf16[704,128]{1,0:T(8,128)(2,1)S(1)} %dynamic-slice_bitcast_fusion.18), channel_id=1, source_target_pairs={{0,8},{4,12},{8,0},{12,4},{16,24},{20,28},{24,16},{28,20},{1,9},{5... | collective-permute-start | bytes 540680 | tf_op jit(solution)/shard_map/ppermute | solution.py:282
  446.3 12.8 %collective-permute-start.20 = (bf16[704,128]{1,0:T(8,128)(2,1)S(1)}, bf16[704,128]{1,0:T(8,128)(2,1)S(1)}, u32[]{:S(2)}, u32[]{:S(2)}) collective-permute-start(bf16[704,128]{1,0:T(8,128)(2,1)S(1)} %dynamic-slice_bitcast_fusion.19), channel_id=1, source_target_pairs={{0,16},{4,20},{8,24},{12,28},{16,0},{20,4},{24,8},{28,12},{1,17},{... | collective-permute-start | bytes 540680 | tf_op jit(solution)/shard_map/ppermute | solution.py:282
  457.3 57.6 %collective-permute-start.26 = (bf16[2,2,2,128,512]{4,3,2,1,0:T(8,128)(2,1)}, bf16[2,2,2,128,512]{4,3,2,1,0:T(8,128)(2,1)}, u32[]{:S(2)}, u32[]{:S(2)}) collective-permute-start(bf16[2,2,2,128,512]{4,3,2,1,0:T(8,128)(2,1)} %dynamic-slice_bitcast_fusion.3), channel_id=1, source_target_pairs={{0,16},{4,20},{8,24},{12,28},{16,0},{20,4},{24,8},{28,12},{1,17},{... | collective-permute-start | bytes 3145736 | tf_op jit(solution)/shard_map/ppermute | solution.py:282
  460.2 57.6 %collective-permute-start.24 = (bf16[2,2,2,128,512]{4,3,2,1,0:T(8,128)(2,1)}, bf16[2,2,2,128,512]{4,3,2,1,0:T(8,128)(2,1)}, u32[]{:S(2)}, u32[]{:S(2)}) collective-permute-start(bf16[2,2,2,128,512]{4,3,2,1,0:T(8,128)(2,1)} %dynamic-slice_bitcast_fusion.4), channel_id=1, source_target_pairs={{0,8},{4,12},{8,0},{12,4},{16,24},{20,28},{24,16},{28,20},{1,9},{5... | collective-permute-start | bytes 3145736 | tf_op jit(solution)/shard_map/ppermute | solution.py:282
  469.1 47.8 %copy-start.13 = (bf16[256,1024]{1,0:T(8,128)(2,1)}, bf16[256,1024]{1,0:T(8,128)(2,1)S(1)}, u32[]{:S(2)}) copy-start(bf16[256,1024]{1,0:T(8,128)(2,1)S(1)} %collective-permute-done.14) | copy-start | bytes 1572868
  517.8 9.4 %collective-permute-start.27 = (bf16[2,2,128,512]{3,2,1,0:T(8,128)(2,1)}, bf16[2,2,128,512]{3,2,1,0:T(8,128)(2,1)S(1)}, u32[]{:S(2)}, u32[]{:S(2)}) collective-permute-start(bf16[2,2,128,512]{3,2,1,0:T(8,128)(2,1)} %dynamic-slice_bitcast_fusion.8), channel_id=1, source_target_pairs={{0,8},{4,12},{8,0},{12,4},{16,24},{20,28},{24,16},{28,20},{1,9},{5... | collective-permute-start | bytes 1572872 | tf_op jit(solution)/shard_map/ppermute | solution.py:282
  520.5 10.6 %collective-permute-start.25 = (bf16[2,2,128,512]{3,2,1,0:T(8,128)(2,1)}, bf16[2,2,128,512]{3,2,1,0:T(8,128)(2,1)}, u32[]{:S(2)}, u32[]{:S(2)}) collective-permute-start(bf16[2,2,128,512]{3,2,1,0:T(8,128)(2,1)} %dynamic-slice_bitcast_fusion.9), channel_id=1, source_target_pairs={{0,16},{4,20},{8,24},{12,28},{16,0},{20,4},{24,8},{28,12},{1,17},{... | collective-permute-start | bytes 1572872 | tf_op jit(solution)/shard_map/ppermute | solution.py:282
  533.4 5.5 collective-permute-start.28
  535.4 3.5 collective-permute-start.31
  540.2 8.3 %collective-permute-start.29 = (bf16[2,128,512]{2,1,0:T(8,128)(2,1)S(1)}, bf16[2,128,512]{2,1,0:T(8,128)(2,1)S(1)}, u32[]{:S(2)}, u32[]{:S(2)}) collective-permute-start(bf16[2,128,512]{2,1,0:T(8,128)(2,1)S(1)} %get-tuple-element.178), channel_id=1, source_target_pairs={{0,1},{1,2},{4,5},{5,6},{8,9},{9,10},{12,13},{13,14},{16,17},{17,1... | collective-permute-start | bytes 786440 | tf_op jit(solution)/shard_map/ppermute | solution.py:267
  544.6 3.9 collective-permute-start.32
  548.7 12.4 %collective-permute-start.30 = (bf16[2,128,512]{2,1,0:T(8,128)(2,1)S(1)}, bf16[2,128,512]{2,1,0:T(8,128)(2,1)S(1)}, u32[]{:S(2)}, u32[]{:S(2)}) collective-permute-start(bf16[2,128,512]{2,1,0:T(8,128)(2,1)S(1)} %get-tuple-element.176), channel_id=1, source_target_pairs={{0,1},{1,2},{2,3},{4,5},{5,6},{6,7},{8,9},{9,10},{10,11},{12,13},{... | collective-permute-start | bytes 786440 | tf_op jit(solution)/shard_map/ppermute | solution.py:267
  557.3 8.3 %collective-permute-start.33 = (bf16[2,128,512]{2,1,0:T(8,128)(2,1)S(1)}, bf16[2,128,512]{2,1,0:T(8,128)(2,1)S(1)}, u32[]{:S(2)}, u32[]{:S(2)}) collective-permute-start(bf16[2,128,512]{2,1,0:T(8,128)(2,1)S(1)} %get-tuple-element.177), channel_id=1, source_target_pairs={{3,2},{2,1},{1,0},{7,6},{6,5},{5,4},{11,10},{10,9},{9,8},{15,14},{... | collective-permute-start | bytes 786440 | tf_op jit(solution)/shard_map/ppermute | solution.py:268
  (24 other events, 222.3 us)
Sparse Core Ops, SparseCore 0:
  11.0 68.2 all-gather.6
  82.3 88.2 all-gather.4

commit v3 on v2

--- a/solution.py
+++ b/solution.py
@@ -233,28 +233,6 @@
     return (left.astype(jnp.float32) + right.astype(jnp.float32)).astype(jnp.bfloat16)
 
 
-def chain_gather(values, nt):
-    z = lax.axis_index("tensor")
-    out = jnp.zeros((nt,) + values.shape, values.dtype)
-    out = lax.dynamic_update_index_in_dim(out, values, z, 0)
-    right = left = values
-    for dist in range(1, nt):
-        right = lax.ppermute(right, "tensor", [(i, i + 1) for i in range(dist - 1, nt - 1)])
-        left = lax.ppermute(left, "tensor", [(i, i - 1) for i in range(1, nt - dist + 1)])
-        pieces = out
-        pieces = jnp.where(
-            z >= dist,
-            lax.dynamic_update_index_in_dim(pieces, right, jnp.maximum(z - dist, 0), 0),
-            pieces,
-        )
-        out = jnp.where(
-            z + dist < nt,
-            lax.dynamic_update_index_in_dim(pieces, left, jnp.minimum(z + dist, nt - 1), 0),
-            pieces,
-        )
-    return out
-
-
 def chain_scatter(parts, nt):
     z = lax.axis_index("tensor")
     right = left = None
@@ -293,10 +271,6 @@
     one_c = pick(one_b, ybit).astype(f32) + swap(pick(one_b, 1 - ybit), 4).astype(f32)
     two_c = pick(two_b, xbit).astype(f32) + swap(pick(two_b, 1 - xbit), 2).astype(f32)
     return jnp.concatenate([one_c, two_c], axis=0).astype(last)
-
-
-def tensor_total(values):
-    return lax.psum(values, "tensor")
 
 
 F32, BF16 = jnp.float32, jnp.bfloat16
@@ -891,72 +865,6 @@
     )
 
 
-def mix_kernel(channels, o, y, z, sq, gain, watt, wmam, m_o, part_o):
-    rows = o.shape[0]
-    r = row_columns([lax.rsqrt(sq[...] / channels + epsilon)], rows)[:, 0:1]
-    zv = z[...]
-    m = (y[...] * (zv * sigmoid(zv)) * r * gain[...]).astype(BF16)
-    m_o[...] = m
-    part_o[...] = (dot_nn(o[...], watt[...]) + dot_nn(m, wmam[...])).astype(BF16)
-
-
-def mix_parts(channels, o, y, z, sq, gain, watt, wmam):
-    total, inner = y.shape
-    width = watt.shape[1]
-    rows = 256
-
-    def tall(n):
-        return pl.BlockSpec((rows, n), lambda i: (i, 0))
-
-    wide = pl.BlockSpec((8, rows), lambda i: (0, i))
-    sds = jax.ShapeDtypeStruct
-    return pl.pallas_call(
-        partial(mix_kernel, channels),
-        grid=(total // rows,),
-        in_specs=[tall(128), tall(inner), tall(inner), wide, whole_spec(gain), whole_spec(watt),
-                  whole_spec(wmam)],
-        out_specs=[tall(inner), tall(width)],
-        out_shape=[sds((total, inner), BF16), sds((total, width), BF16)],
-        compiler_params=pltpu.CompilerParams(vmem_limit_bytes=VMEM_LIMIT),
-        cost_estimate=pl.CostEstimate(flops=int(1e9), bytes_accessed=int(7e6), transcendentals=int(4e5)),
-        name="mix_parts",
-    )(o, y, z, sq, gain, watt, wmam)
-
-
-def unmix_kernel(dmix, y, z, gain, watt, wmam, do_o, dm_o, dot_o):
-    rows = dmix.shape[0]
-    g = dmix[...]
-    do_o[...] = dot_nt(g, watt[...]).astype(BF16)
-    dm = dot_nt(g, wmam[...])
-    dm_o[...] = dm
-    zv = z[...]
-    dots = jnp.sum(dm * gain[...] * (y[...] * (zv * sigmoid(zv))), axis=1, keepdims=True)
-    for c in range(0, rows, 128):
-        dot_o[:, c : c + 128] = jnp.broadcast_to(dots[c : c + 128], (128, 128)).T[0:8, :]
-
-
-def unmix(dmix, y, z, gain, watt, wmam):
-    total, inner = y.shape
-    rows = 256
-
-    def tall(n):
-        return pl.BlockSpec((rows, n), lambda i: (i, 0))
-
-    wide = pl.BlockSpec((8, rows), lambda i: (0, i))
-    sds = jax.ShapeDtypeStruct
-    return pl.pallas_call(
-        unmix_kernel,
-        grid=(total // rows,),
-        in_specs=[tall(dmix.shape[1]), tall(inner), tall(inner), whole_spec(gain), whole_spec(watt),
-                  whole_spec(wmam)],
-        out_specs=[tall(128), tall(inner), wide],
-        out_shape=[sds((total, 128), BF16), sds((total, inner), F32), sds((8, total), F32)],
-        compiler_params=pltpu.CompilerParams(vmem_limit_bytes=VMEM_LIMIT),
-        cost_estimate=pl.CostEstimate(flops=int(1e9), bytes_accessed=int(7e6), transcendentals=int(4e5)),
-        name="unmix",
-    )(dmix, y, z, gain, watt, wmam)
-
-
 def down_kernel(dq, dz, dx, dkv, db, drow, wq, win, stp, wsh, part_o):
     total = dot_nt(dq[...], wq[...]) + dot_nt(dz[...], win[0]) + dot_nt(dx[...], win[1])
     total = total + dot_nt(dkv[...], wsh[:, 0:256]) + dot_nt(db[...], wsh[:, 256:])
@@ -1042,6 +950,510 @@
         cost_estimate=pl.CostEstimate(flops=int(4e9), bytes_accessed=int(12e6), transcendentals=0),
         name="weight_pieces",
     )(a1, *args, dmix)
+
+
+def remote_copy(src, dst, send, recv, dev):
+    return pltpu.make_async_remote_copy(
+        src_ref=src, dst_ref=dst, send_sem=send, recv_sem=recv, device_id=dev, device_id_type=MESH
+    )
+
+
+def greet(peers):
+    barrier = pltpu.get_barrier_semaphore()
+    for peer in peers:
+        pl.semaphore_signal(barrier, inc=1, device_id=peer, device_id_type=MESH)
+    pl.semaphore_wait(barrier, len(peers))
+
+
+def other_quarters(d, z, nt):
+    return [(d, lax.rem(z + k, nt)) for k in range(1, nt)]
+
+
+class Exchange:
+    def __init__(self, own, landed, send, recv, d, z, nt):
+        self.own, self.landed, self.z, self.nt = own, landed, z, nt
+        self.copies = [
+            remote_copy(own, landed.at[k - 1], send.at[k - 1], recv.at[k - 1], peer)
+            for k, peer in enumerate(other_quarters(d, z, nt), 1)
+        ]
+
+    def start(self):
+        for copy in self.copies:
+            copy.start()
+
+    def wait(self):
+        for copy in self.copies:
+            copy.wait()
+
+    def total(self):
+        total = None
+        for q in range(self.nt):
+            value = jnp.where(self.z == q, self.own[...].astype(F32), 0.0)
+            for k in range(1, self.nt):
+                value = value + jnp.where(
+                    lax.rem(self.z - k + self.nt, self.nt) == q, self.landed[k - 1].astype(F32), 0.0
+                )
+            total = value if total is None else total + value
+        return total
+
+
+class ChainScatter:
+    def __init__(self, parts, bufs, landed, send, recv, d, z, nt):
+        self.parts, self.bufs, self.landed = parts, bufs, landed
+        self.send, self.recv = send, recv
+        self.d, self.z, self.nt = d, z, nt
+
+    def active(self, way, t):
+        z, nt = self.z, self.nt
+        if way == 0:
+            return (z <= t) & (z < nt - 1)
+        return (nt - 1 - z <= t) & (z > 0)
+
+    def copy(self, way, t):
+        dev = (self.d, self.z + 1 if way == 0 else self.z - 1)
+        return remote_copy(
+            self.bufs.at[way, t], self.landed.at[way, t], self.send.at[way, t], self.recv.at[way, t], dev
+        )
+
+    def arrives(self, way, t):
+        z, nt = self.z, self.nt
+        if way == 0:
+            return (z >= 1) & (z - 1 <= t)
+        return (z < nt - 1) & (nt - 2 - z <= t)
+
+    def step(self, t):
+        z, nt = self.z, self.nt
+        for way in range(2):
+            q = nt - 1 - t + z if way == 0 else t - (nt - 1) + z
+
+            def run():
+                value = self.parts[q]
+                if t > 0:
+                    came = self.arrives(way, t - 1)
+
+                    @pl.when(came)
+                    def _():
+                        self.copy(way, t - 1).wait_recv()
+                        total = value.astype(F32) + self.landed[way, t - 1].astype(F32)
+                        self.bufs[way, t] = total.astype(BF16)
+
+                    @pl.when(jnp.logical_not(came))
+                    def _():
+                        self.bufs[way, t] = value
+                else:
+                    self.bufs[way, t] = value
+                self.copy(way, t).start()
+
+            pl.when(self.active(way, t))(run)
+
+    def finish(self, out):
+        out[...] = self.parts[self.z].astype(F32)
+        t = self.nt - 2
+        for way in range(2):
+
+            @pl.when(self.arrives(way, t))
+            def _():
+                self.copy(way, t).wait_recv()
+                out[...] += self.landed[way, t].astype(F32)
+
+    def drain(self):
+        for way in range(2):
+            for t in range(self.nt - 1):
+                pl.when(self.active(way, t))(self.copy(way, t).wait_send)
+
+
+def chain_scratch(nt, rows, width):
+    dma = pltpu.SemaphoreType.DMA
+    return [
+        pltpu.VMEM((2, nt - 1, rows, width), BF16),
+        pltpu.VMEM((2, nt - 1, rows, width), BF16),
+        dma((2, nt - 1)),
+        dma((2, nt - 1)),
+    ]
+
+
+def mix_scatter_kernel(
+    channels, nt, o, y, z_in, sq, gain, watt, wmam, tok,
+    m_o, sq_o, hid_o,
+    sq_land, sq_send, sq_recv, parts, bufs, landed, c_send, c_recv,
+):
+    d = lax.axis_index("dp")
+    z = lax.axis_index("tensor")
+    rows = tok.shape[0]
+    greet(other_quarters(d, z, nt))
+    squares = Exchange(sq, sq_land, sq_send, sq_recv, d, z, nt)
+    squares.start()
+    chain = ChainScatter(parts, bufs, landed, c_send, c_recv, d, z, nt)
+    squares.wait()
+    sq_o[...] = squares.total()
+
+    def part(q):
+        at = pl.ds(pl.multiple_of(q * rows, rows), rows)
+        total = sq_o[:, at]
+        r = row_columns([lax.rsqrt(total / channels + epsilon)], rows)[:, 0:1]
+        zv = z_in[at, :]
+        m = (y[at, :] * (zv * sigmoid(zv)) * r * gain[...]).astype(BF16)
+        m_o[at, :] = m
+        parts[q] = (dot_nn(o[at, :], watt[...]) + dot_nn(m, wmam[...])).astype(BF16)
+
+    first = jnp.where(z < nt // 2, nt - 1, 0)
+    part(first)
+    chain.step(0)
+
+    def rest(i, carry):
+        part(lax.rem(first + 1 + i, nt))
+        return carry
+
+    lax.fori_loop(0, nt - 1, rest, 0)
+    for t in range(1, nt - 1):
+        chain.step(t)
+    chain.finish(hid_o)
+    hid_o[...] += tok[...].astype(F32)
+    chain.drain()
+
+
+def mix_scatter(channels, nt, o, y, zr, sq, gain, watt, wmam, tok):
+    total, inner = y.shape
+    rows, width = tok.shape
+    dma = pltpu.SemaphoreType.DMA
+    sds = jax.ShapeDtypeStruct
+    vmem = pl.BlockSpec(memory_space=pltpu.VMEM)
+    return pl.pallas_call(
+        partial(mix_scatter_kernel, channels, nt),
+        in_specs=[vmem] * 8,
+        out_specs=[vmem] * 3,
+        out_shape=[sds((total, inner), BF16), sds((8, total), F32), sds((rows, width), F32)],
+        scratch_shapes=[pltpu.VMEM((nt - 1, 8, total), F32), dma((nt - 1,)), dma((nt - 1,)),
+                        pltpu.VMEM((nt, rows, width), BF16)] + chain_scratch(nt, rows, width),
+        compiler_params=pltpu.CompilerParams(
+            vmem_limit_bytes=VMEM_LIMIT, collective_id=1, has_side_effects=True
+        ),
+        cost_estimate=pl.CostEstimate(flops=int(1e9), bytes_accessed=int(130e6), transcendentals=int(4e5)),
+        name="mix_scatter",
+    )(o, y, zr, sq, gain, watt, wmam, tok)
+
+
+class ChainGather:
+    def __init__(self, own, slots, send, recv, d, z, nt):
+        self.own, self.slots, self.send, self.recv = own, slots, send, recv
+        self.d, self.z, self.nt = d, z, nt
+
+    def copy(self, way, dist):
+        dev = (self.d, self.z + 1 if way == 0 else self.z - 1)
+        slot = self.z - dist if way == 0 else self.z + dist
+        src = self.own if dist == 0 else self.slots.at[slot]
+        return remote_copy(src, self.slots.at[slot], self.send.at[way, dist], self.recv.at[way, dist], dev)
+
+    def landing(self, way, dist):
+        slot = self.z - dist if way == 0 else self.z + dist
+        return remote_copy(
+            self.slots.at[slot], self.slots.at[slot], self.send.at[way, dist - 1],
+            self.recv.at[way, dist - 1], (self.d, self.z),
+        )
+
+    def has(self, way, dist):
+        return self.z >= dist if way == 0 else self.z + dist < self.nt
+
+    def goes_on(self, way):
+        return self.z < self.nt - 1 if way == 0 else self.z > 0
+
+    def start(self):
+        for way in range(2):
+            pl.when(self.goes_on(way))(self.copy(way, 0).start)
+
+    def hop(self, dist):
+        for way in range(2):
+            pl.when(self.has(way, dist))(self.landing(way, dist).wait_recv)
+            if dist < self.nt - 1:
+                pl.when(self.has(way, dist) & self.goes_on(way))(self.copy(way, dist).start)
+
+    def drain(self):
+        for way in range(2):
+            pl.when(self.goes_on(way))(self.copy(way, 0).wait_send)
+            for dist in range(1, self.nt - 1):
+                pl.when(self.has(way, dist) & self.goes_on(way))(self.copy(way, dist).wait_send)
+
+
+def unmix_gather_kernel(
+    nt, dmix, y, z_in, gain, watt, wmam,
+    g_o, do_o, dm_o, dot_o,
+    slots, g_send, g_recv, dot_own, dot_land, d_send, d_recv,
+):
+    d = lax.axis_index("dp")
+    z = lax.axis_index("tensor")
+    rows = dmix.shape[0]
+    greet(other_quarters(d, z, nt))
+    chain = ChainGather(dmix, slots, g_send, g_recv, d, z, nt)
+    chain.start()
+
+    def work(q, g):
+        at = pl.ds(pl.multiple_of(q * rows, rows), rows)
+        g_o[at, :] = g
+        do_o[at, :] = dot_nt(g, watt[...]).astype(BF16)
+        dm = dot_nt(g, wmam[...])
+        dm_o[at, :] = dm
+        zv = z_in[at, :]
+        dots = jnp.sum(dm * gain[...] * (y[at, :] * (zv * sigmoid(zv))), axis=1, keepdims=True)
+        turned = [jnp.broadcast_to(dots[c : c + 128], (128, 128)).T[0:8, :] for c in range(0, rows, 128)]
+        dot_own[:, at] = jnp.concatenate(turned, axis=1)
+
+    work(z, dmix[...])
+    for dist in range(1, nt):
+        chain.hop(dist)
+
+        def side(way, carry):
+            q = jnp.where(way == 0, z - dist, z + dist)
+
+            @pl.when((q >= 0) & (q < nt))
+            def _():
+                work(q, slots[q])
+
+            return carry
+
+        lax.fori_loop(0, 2, side, 0)
+    dots = Exchange(dot_own, dot_land, d_send, d_recv, d, z, nt)
+    dots.start()
+    chain.drain()
+    dots.wait()
+    dot_o[...] = dots.total()
+
+
+def unmix_gather(nt, dmix, y, zr, gain, watt, wmam):
+    total, inner = y.shape
+    rows, width = dmix.shape
+    dma = pltpu.SemaphoreType.DMA
+    sds = jax.ShapeDtypeStruct
+    vmem = pl.BlockSpec(memory_space=pltpu.VMEM)
+    return pl.pallas_call(
+        partial(unmix_gather_kernel, nt),
+        in_specs=[vmem] * 6,
+        out_specs=[vmem] * 4,
+        out_shape=[sds((total, width), BF16), sds((total, 128), BF16), sds((total, inner), F32),
+                   sds((8, total), F32)],
+        scratch_shapes=[pltpu.VMEM((nt, rows, width), BF16), dma((2, nt - 1)), dma((2, nt - 1)),
+                        pltpu.VMEM((8, total), F32), pltpu.VMEM((nt - 1, 8, total), F32),
+                        dma((nt - 1,)), dma((nt - 1,))],
+        compiler_params=pltpu.CompilerParams(
+            vmem_limit_bytes=VMEM_LIMIT, collective_id=2, has_side_effects=True
+        ),
+        cost_estimate=pl.CostEstimate(flops=int(1e9), bytes_accessed=int(130e6), transcendentals=int(4e5)),
+        name="unmix_gather",
+    )(dmix, y, zr, gain, watt, wmam)
+
+
+def add_refs(left, right):
+    return left.astype(F32) + right.astype(F32)
+
+
+class CubeScatter:
+    def __init__(self, pieces, bufs, send, recv, peers, bits, z):
+        (self.rc, self.held, self.r1, self.r2, self.ob, self.tb, self.r3, self.r4) = bufs
+        self.p = pieces
+        self.half = pieces.shape[3] // 2
+        self.core, self.x, self.y = bits
+        d_core, d_x, d_y = peers
+        half = self.half
+        n = pieces.shape[3]
+        core, x, y = bits
+        lo, hi = pl.ds(0, half), pl.ds(half, n - half)
+        mk = remote_copy
+        self.c0 = mk(pieces.at[:, :, 1 - core], self.rc, send.at[0], recv.at[0], (d_core, z))
+        self.c1 = mk(self.held.at[:, 1 - x, lo], self.r1, send.at[1], recv.at[1], (d_x, z))
+        self.c2 = mk(self.held.at[1 - y, :, hi], self.r2, send.at[2], recv.at[2], (d_y, z))
+        self.c3 = mk(self.ob.at[1 - y], self.r3, send.at[3], recv.at[3], (d_y, z))
+        self.c4 = mk(self.tb.at[1 - x], self.r4, send.at[4], recv.at[4], (d_x, z))
+
+    def start(self):
+        self.c0.start()
+
+    def middle(self):
+        self.c0.wait_recv()
+        for i in range(2):
+            for j in range(2):
+                self.held[i, j] = add_refs(self.p[i, j, self.core], self.rc[i, j]).astype(BF16)
+        self.c1.start()
+        self.c2.start()
+
+    def last(self):
+        half = self.half
+        self.c1.wait_recv()
+        for i in range(2):
+            self.ob[i] = add_refs(self.held[i, self.x, 0:half], self.r1[i]).astype(BF16)
+        self.c3.start()
+        self.c2.wait_recv()
+        for i in range(2):
+            self.tb[i] = add_refs(self.held[self.y, i, half:], self.r2[i]).astype(BF16)
+        self.c4.start()
+
+    def finish(self, out):
+        half = self.half
+        self.c3.wait_recv()
+        out[0:half] = add_refs(self.ob[self.y], self.r3[...]).astype(out.dtype)
+        self.c4.wait_recv()
+        out[half:] = add_refs(self.tb[self.x], self.r4[...]).astype(out.dtype)
+
+    def drain(self):
+        for copy in (self.c0, self.c1, self.c2, self.c3, self.c4):
+            copy.wait_send()
+
+
+def cube_scratch(n, lanes):
+    dma = pltpu.SemaphoreType.DMA
+    half = n // 2
+    return [
+        pltpu.VMEM((2, 2, n, lanes), BF16),
+        pltpu.VMEM((2, 2, n, lanes), BF16),
+        pltpu.VMEM((2, half, lanes), BF16),
+        pltpu.VMEM((2, n - half, lanes), BF16),
+        pltpu.VMEM((2, half, lanes), BF16),
+        pltpu.VMEM((2, n - half, lanes), BF16),
+        pltpu.VMEM((half, lanes), BF16),
+        pltpu.VMEM((n - half, lanes), BF16),
+        dma((5,)),
+        dma((5,)),
+    ]
+
+
+class CubeTotal:
+    def __init__(self, held, landed, send, recv, peers, z):
+        self.held, self.landed = held, landed
+        self.copies = [
+            remote_copy(held.at[i], landed.at[i], send.at[i], recv.at[i], (peer, z))
+            for i, peer in enumerate(peers)
+        ]
+
+    def start(self, i):
+        self.copies[i].start()
+
+    def take(self, i):
+        self.copies[i].wait_recv()
+        self.held[i + 1] = self.held[i] + self.landed[i]
+
+    def drain(self):
+        for copy in self.copies:
+            copy.wait_send()
+
+
+def norm_back(dy, tok, gain, dh, out, ggain):
+    v = tok[...].astype(F32)
+    width = v.shape[1]
+    f = lax.rsqrt(jnp.mean(v * v, axis=1, keepdims=True) + epsilon)
+    ggain(jnp.sum(dy * v * f, axis=0, keepdims=True))
+    gdy = dy * gain[...]
+    lean = jnp.sum(gdy * v, axis=1, keepdims=True) * (f * f * f / width)
+    out[...] = (dh[...] + (f * gdy - v * lean)).astype(BF16)
+
+
+def tail_kernel(
+    nt, n_all, parts, tok, gain, dh, pieces, shared, small,
+    gt_o, mix_o, sh_o, small_o, norm_o,
+    da, bufs, landed, c_send, c_recv, *rest,
+):
+    cube_a, rest = rest[:10], rest[10:]
+    cube_b, rest = rest[:10], rest[10:]
+    (sh_sum, sh_land, sh_send, sh_recv) = rest[:4]
+    (sm_held, sm_land, sm_send, sm_recv, all_own, all_land, all_send, all_recv) = rest[4:12]
+    (ng_held, ng_land, ng_send, ng_recv, ngz_land, ngz_send, ngz_recv) = rest[12:]
+    d = lax.axis_index("dp")
+    z = lax.axis_index("tensor")
+    bits = dp_bits(d)
+    core, x, y = bits
+    peers = (d + 1 - 2 * core, d + 2 - 4 * x, d + 4 - 8 * y)
+    greet([(p, z) for p in peers] + other_quarters(d, z, nt))
+    chain = ChainScatter(parts, bufs, landed, c_send, c_recv, d, z, nt)
+    chain.step(0)
+    one = CubeScatter(pieces, cube_a[:8], cube_a[8], cube_a[9], peers, bits, z)
+    two = CubeScatter(shared, cube_b[:8], cube_b[8], cube_b[9], peers, bits, z)
+    sums = CubeTotal(sm_held, sm_land, sm_send, sm_recv, peers, z)
+    sm_held[0] = small[...]
+    sums.start(0)
+    two.start()
+    one.start()
+    sums.take(0)
+    sums.start(1)
+    two.middle()
+    one.middle()
+    sums.take(1)
+    sums.start(2)
+    chain.step(1)
+    sums.take(2)
+    all_own[...] = sm_held[3, 0:n_all, :]
+    over_all = Exchange(all_own, all_land, all_send, all_recv, d, z, nt)
+    over_all.start()
+    two.last()
+    one.last()
+    two.finish(sh_sum)
+    per = sh_sum.shape[0] // nt
+    copies = []
+    for k in range(1, nt):
+        q = lax.rem(z + k, nt)
+        rows = pl.ds(pl.multiple_of(q * per, per), per)
+        copies.append(
+            remote_copy(sh_sum.at[rows], sh_land.at[k - 1], sh_send.at[k - 1], sh_recv.at[k - 1], (d, q))
+        )
+        copies[-1].start()
+    for t in range(2, nt - 1):
+        chain.step(t)
+    one.finish(mix_o)
+    small_o[...] = sm_held[3]
+    over_all.wait()
+    small_o[0:n_all, :] = over_all.total()
+    for copy in copies:
+        copy.wait()
+    total = sh_sum[pl.ds(pl.multiple_of(z * per, per), per), :].astype(F32)
+    for k in range(nt - 1):
+        total = total + sh_land[k].astype(F32)
+    sh_o[...] = total
+    chain.finish(da)
+
+    def keep(row):
+        for k in range(8):
+            ng_held[0, k : k + 1, :] = row[:, 128 * k : 128 * k + 128]
+
+    norm_back(da[...], tok, gain, dh, gt_o, keep)
+    norms = CubeTotal(ng_held, ng_land, ng_send, ng_recv, peers, z)
+    for i in range(3):
+        norms.start(i)
+        norms.take(i)
+    last = Exchange(ng_held.at[3], ngz_land, ngz_send, ngz_recv, d, z, nt)
+    last.start()
+    last.wait()
+    norm_o[...] = last.total()
+    for thing in (chain, one, two, sums, norms):
+        thing.drain()
+
+
+def tail(nt, n_all, parts, tok, gain, dh, pieces, shared, small):
+    rows, width = tok.shape
+    n, lanes = pieces.shape[1:]
+    s_rows, s_lanes = shared.shape[1:]
+    m_rows = small.shape[0]
+    dma = pltpu.SemaphoreType.DMA
+    sds = jax.ShapeDtypeStruct
+    vmem = pl.BlockSpec(memory_space=pltpu.VMEM)
+    pieces = pieces.reshape(2, 2, 2, n, lanes)
+    shared = shared.reshape(2, 2, 2, s_rows, s_lanes)
+    return pl.pallas_call(
+        partial(tail_kernel, nt, n_all),
+        in_specs=[vmem] * 7,
+        out_specs=[vmem] * 5,
+        out_shape=[sds((rows, width), BF16), sds((n, lanes), F32), sds((s_rows // nt, s_lanes), F32),
+                   sds((m_rows, 128), F32), sds((8, 128), F32)],
+        scratch_shapes=[pltpu.VMEM((rows, width), F32)] + chain_scratch(nt, rows, width)
+        + cube_scratch(n, lanes) + cube_scratch(s_rows, s_lanes)
+        + [pltpu.VMEM((s_rows, s_lanes), BF16), pltpu.VMEM((nt - 1, s_rows // nt, s_lanes), BF16),
+           dma((nt - 1,)), dma((nt - 1,)),
+           pltpu.VMEM((4, m_rows, 128), F32), pltpu.VMEM((3, m_rows, 128), F32), dma((3,)), dma((3,)),
+           pltpu.VMEM((n_all, 128), F32), pltpu.VMEM((nt - 1, n_all, 128), F32), dma((nt - 1,)),
+           dma((nt - 1,)),
+           pltpu.VMEM((4, 8, 128), F32), pltpu.VMEM((3, 8, 128), F32), dma((3,)), dma((3,)),
+           pltpu.VMEM((nt - 1, 8, 128), F32), dma((nt - 1,)), dma((nt - 1,))],
+        compiler_params=pltpu.CompilerParams(
+            vmem_limit_bytes=VMEM_LIMIT, collective_id=3, has_side_effects=True
+        ),
+        cost_estimate=pl.CostEstimate(flops=int(1e7), bytes_accessed=int(150e6), transcendentals=0),
+        name="tail",
+    )(parts, tok, gain, dh, pieces, shared, small)
 
 
 def rope_wide(length):
@@ -1147,13 +1559,13 @@
         heads, kv_head, tok_full.reshape(group_rows, width), gain_first, full_query, full_inner, step_rows,
         full_shared, cosine, sine, taps_x, taps_b, decay, bias, skip,
     )
-    squares = jnp.broadcast_to(tensor_total(squares[0:1]), (8, group_rows))
-    m, mix_part = mix_parts(channels, o, y, zr, squares, gain_mix, full_attend, full_mamba)
-    hidden = tokens.astype(F32) + chain_scatter(mix_part.reshape(nt, local_rows, width), nt)
+    m, squares, hidden = mix_scatter(
+        channels, nt, o, y, zr, squares, gain_mix, full_attend, full_mamba, tokens
+    )
     layer_out, dh, dmix, grad_gain_two, hid_pieces, down_pieces = feed_forward(
         hidden, gain_second, cotangent, full_hidden, full_down
     )
-    grad_mix = chain_gather(dmix, nt).reshape(group_rows, width)
+    grad_mix, do, dm, dots = unmix_gather(nt, dmix, y, zr, gain_mix, full_attend, full_mamba)
     if nd == 8:
         hid_sum = cube_scatter(hid_pieces, nd, BF16)
         down_sum = cube_scatter(down_pieces, nd, BF16)
@@ -1167,20 +1579,12 @@
         gradient_hidden = chain_scatter(hid_sum, nt)
         gradient_down = chain_scatter(down_sum, nt)
 
-    do, dm, dots = unmix(grad_mix, y, zr, gain_mix, full_attend, full_mamba)
-    dots = jnp.broadcast_to(tensor_total(dots[0:1]), (8, group_rows))
     dq, dkv = attend_back(kv_head, q, k2, v2, lse, do, cosine, sine)
     dz, dx, db, drow, grad_tx, grad_tb, grad_rows, grad_heads = scan_back(
         heads, channels, dm, y, zr, xr, br, trow, states, squares, dots, gain_mix, taps_x, taps_b, decay, bias,
         skip,
     )
     part_one = down_parts(dq, dz, dx, dkv, db, drow, full_query, full_inner, step_rows, full_shared)
-    grad_normed_one = chain_scatter(part_one.reshape(nt, local_rows, width), nt)
-    token_f32 = tokens.astype(F32)
-    _, norm_one_back = jax.vjp(norm_apply, token_f32, gain_first[0])
-    grad_from_one, grad_gain_one = norm_one_back(grad_normed_one)
-    gradient_tokens = (dh + grad_from_one).astype(BF16)
-
     pieces, shared_pieces, grad_step = weight_pieces(a1, dq, dz, dx, dkv, db, drow, o, m, grad_mix)
     block = width // nd
     q_cols = query_proj.shape[1]
@@ -1193,37 +1597,8 @@
     def from_lanes(values):
         return values.transpose(1, 0, 2).reshape(-1, width)
 
-    if nd == 8:
-        mixer_sum = cube_scatter(pieces, nd)
-        got = [mixer_sum[cuts[i] : cuts[i + 1]] for i in range(5)]
-
-        def back_rows(values):
-            return values.reshape(-1, 128, 128).transpose(1, 0, 2).reshape(128, -1)
-
-        gradient_query = back_rows(got[0])
-        gradient_attend = got[1]
-        gradient_inner = jnp.stack([back_rows(got[2]), back_rows(got[3])])
-        gradient_mamba = got[4]
-    else:
-        got = [pieces[:, cuts[i] : cuts[i + 1]] for i in range(5)]
-
-        def over_rows(values):
-            return cube_scatter(from_rows(values).reshape(nd, block, -1), nd)
-
-        def over_lanes(values):
-            return cube_scatter(from_lanes(values).reshape(-1, nd, block).transpose(1, 0, 2), nd)
-
-        gradient_query = over_rows(got[0])
-        gradient_attend = over_lanes(got[1])
-        gradient_inner = jnp.stack([over_rows(got[2]), over_rows(got[3])])
-        gradient_mamba = over_lanes(got[4])
-    shared_cut = shared_pieces.reshape(nd, nt, width // (nd * nt), -1)
-    gradient_shared = chain_scatter(cube_scatter(shared_cut, nd, BF16), nt)
-
     n_tap = CONV + 1
-    over_all = jnp.concatenate(
-        [grad_gain_one, grad_gain_two.reshape(-1), grad_tb[:n_tap].reshape(-1)]
-    )
+    over_all = jnp.concatenate([grad_gain_two.reshape(-1), grad_tb[:n_tap].reshape(-1)])
     over_dp = jnp.concatenate(
         [
             grad_tx[:n_tap].reshape(-1),
@@ -1234,19 +1609,61 @@
             grad_step[:heads].reshape(-1),
         ]
     )
-    n_all = over_all.shape[0]
-    over_dp = lax.psum(jnp.concatenate([over_all, over_dp]), "dp")
-    over_all = lax.psum(over_dp[:n_all], "tensor")
-    over_dp = over_dp[n_all:]
+
+    def in_rows(values):
+        return jnp.pad(values, (0, -values.shape[0] % 1024)).reshape(-1, 128)
+
+    rows_all = in_rows(over_all)
+    n_all = rows_all.shape[0]
+    small_sums = jnp.concatenate([rows_all, in_rows(over_dp)], axis=0)
+    parts = part_one.reshape(nt, local_rows, width)
+    if nd == 8:
+        gradient_tokens, mixer_sum, gradient_shared, small_sums, grad_gain_one = tail(
+            nt, n_all, parts, tokens, gain_first, dh, pieces, shared_pieces, small_sums
+        )
+        grad_gain_one = grad_gain_one.reshape(1, width)
+        got = [mixer_sum[cuts[i] : cuts[i + 1]] for i in range(5)]
+
+        def back_rows(values):
+            return values.reshape(-1, 128, 128).transpose(1, 0, 2).reshape(128, -1)
+
+        gradient_query = back_rows(got[0])
+        gradient_attend = got[1]
+        gradient_inner = jnp.stack([back_rows(got[2]), back_rows(got[3])])
+        gradient_mamba = got[4]
+    else:
+        token_f32 = tokens.astype(F32)
+        _, norm_one_back = jax.vjp(norm_apply, token_f32, gain_first[0])
+        grad_from_one, grad_gain_one = norm_one_back(chain_scatter(parts, nt))
+        gradient_tokens = (dh + grad_from_one).astype(BF16)
+        got = [pieces[:, cuts[i] : cuts[i + 1]] for i in range(5)]
+
+        def over_rows(values):
+            return cube_scatter(from_rows(values).reshape(nd, block, -1), nd)
+
+        def over_lanes(values):
+            return cube_scatter(from_lanes(values).reshape(-1, nd, block).transpose(1, 0, 2), nd)
+
+        gradient_query = over_rows(got[0])
+        gradient_attend = over_lanes(got[1])
+        gradient_inner = jnp.stack([over_rows(got[2]), over_rows(got[3])])
+        gradient_mamba = over_lanes(got[4])
+        shared_cut = shared_pieces.reshape(nd, nt, width // (nd * nt), -1)
+        gradient_shared = chain_scatter(cube_scatter(shared_cut, nd, BF16), nt)
+        small_sums = lax.psum(small_sums, "dp")
+        small_sums = jnp.concatenate(
+            [lax.psum(small_sums[:n_all], "tensor"), small_sums[n_all:]], axis=0
+        )
+        grad_gain_one = lax.psum(grad_gain_one, ("dp", "tensor")).reshape(1, width)
+    over_all = small_sums[:n_all].reshape(-1)
+    over_dp = small_sums[n_all:].reshape(-1)
     place = d * nt + tensor_index
     norm_w = width // (nd * nt)
-    gradient_norms = lax.dynamic_slice_in_dim(
-        over_all[: 2 * width].reshape(2, width), place * norm_w, norm_w, 1
-    )
+    both_norms = jnp.concatenate([grad_gain_one, over_all[:width].reshape(1, width)], axis=0)
+    gradient_norms = lax.dynamic_slice_in_dim(both_norms, place * norm_w, norm_w, 1)
     tap_w = shared_taps.shape[1]
-    gradient_taps = lax.dynamic_slice_in_dim(
-        over_all[2 * width :].reshape(n_tap, -1), place * tap_w, tap_w, 1
-    )
+    tap_all = over_all[width : width + n_tap * taps_b.shape[1]].reshape(n_tap, -1)
+    gradient_taps = lax.dynamic_slice_in_dim(tap_all, place * tap_w, tap_w, 1)
     part = mixer_gain.shape[1]
     n_taps = n_tap * inner
     chan = over_dp[:n_taps].reshape(n_tap, heads, SSM_DIM)
@@ -1257,7 +1674,7 @@
     gradient_skip = rest[:heads]
     gradient_decay = rest[heads : 2 * heads]
     gradient_bias = rest[2 * heads : 3 * heads]
-    step_all = rest[3 * heads :].reshape(heads, width)
+    step_all = rest[3 * heads : 3 * heads + heads * width].reshape(heads, width)
     gradient_step = lax.dynamic_slice_in_dim(step_all, d * block, block, 1).T
     return (
         layer_out,

time: 584 us -> 488 us (0.84)
  Pallas kernels: 167 us -> 338 us
  waiting for transfers between devices: 125 us -> 41.9 us
  starting transfers between devices: 112 us -> 30.6 us
  blocking collectives: 61.8 us -> 0 us
  other arithmetic: 41.5 us -> 16 us
  local copies, waits for them, and re-layouts: 49.7 us -> 36.7 us
    pallas_call x2 -> x3, Pallas kernels: 12.2 us -> 183 us  [the longest x1 71.1 us: mix_scatter(): pl.pallas_call(partial(mix_scatter_kernel, channels, nt), in_specs=[vmem]...]
    psum x4 -> x0, blocking collectives: 61.8 us -> none  [the longest x1 22.7 us: per_device(): over_dp = lax.psum(jnp.concatenate([over_all, over_dp]), 'dp')]
    ppermute x15 -> x6, waiting for transfers between devices: 50.1 us -> 2.12 us  [chain_scatter(): right = lax.ppermute(to_right, 'tensor', [(i, i + 1) for i in range(t + 1)])]
    ppermute x15 -> x6, starting transfers between devices: 61.7 us -> 19.7 us  [chain_scatter(): right = lax.ppermute(to_right, 'tensor', [(i, i + 1) for i in range(t + 1)])]
    ppermute x6 -> x0, waiting for transfers between devices: 30.1 us -> none  [the longest x3 25.5 us: chain_gather(): lax.ppermute(left, 'tensor', [(i, i - 1) for i in range(1, nt - dist + 1)])]
    ppermute x15 -> x6, waiting for transfers between devices: 23.1 us -> 0.02 us  [chain_scatter(): lax.ppermute(to_left, 'tensor', [(nt - 1 - i, nt - 2 - i) for i in range(...]
    ppermute x20 -> x10, starting transfers between devices: 25.1 us -> 5.49 us  [swap(): return lax.ppermute(values, 'dp', [(i, i ^ bit) for i in range(8)])]
    ppermute x20 -> x10, waiting for transfers between devices: 20.8 us -> 38.3 us  [swap(): return lax.ppermute(values, 'dp', [(i, i ^ bit) for i in range(8)])]
  transfers between devices with their start and end apart: 58 -> 24, of which waited for: 26 -> 6; matrix products, arithmetic and copies ran while one was open for 15% -> 10% of each run, Pallas kernels for 26% -> 66%
where the time goes in v3:
time: 488 us; the launch traced here: 478 us
  Pallas kernels  338 us (69%)
  waiting for transfers between devices  41.9 us (9%)
  local copies, waits for them, and re-layouts  36.7 us (8%)
  starting transfers between devices  30.6 us (6%)
  other arithmetic  16 us (3%)
  between operations  15.2 us (3%)
    pallas_call x1, Pallas kernels, mix_scatter(): pl.pallas_call(partial(mix_scatter_kernel, channels, nt), in_specs=[vmem]...  71.1 us
    pallas_call x1, Pallas kernels, gather_start(): pl.pallas_call(partial(gather_kernel, nt), out_shape=[jax.ShapeDtypeStruc...  61.4 us
    pallas_call x1, Pallas kernels, tail(): pl.pallas_call(partial(tail_kernel, nt, n_all), in_specs=[vmem] * 7, out_...  58.9 us
    pallas_call x1, Pallas kernels, unmix_gather(): pl.pallas_call(partial(unmix_gather_kernel, nt), in_specs=[vmem] * 6, out...  52.9 us
    ppermute x10, waiting for transfers between devices, swap(): return lax.ppermute(values, 'dp', [(i, i ^ bit) for i in range(8)])  38.3 us
    pallas_call x1, Pallas kernels, scan_back(): pl.pallas_call(partial(scan_back_kernel, heads, channels), grid=(steps,),...  23.3 us
    pallas_call x1, Pallas kernels, mixers_forward(): pl.pallas_call(partial(forward_kernel, heads), grid=(total // rows,), in_...  23.1 us
    pallas_call x1, Pallas kernels, feed_forward(): pl.pallas_call(feed_kernel, grid=(nt * per,), in_specs=[fixed(rows, width...  20.1 us
  transfers between devices with their start and end apart: 24, of which 6 were waited for; matrix products, arithmetic and copies ran while one was open for 10% of the time, Pallas kernels for 66%

profile of v3, /device:TPU:0, one launch (start us, length us, event | category | flops | bytes accessed | tf_op | source)
XLA Modules:
  0.0 478.5 jit_solution(14088570407228113570)
XLA Ops:
  7.3 0.7 all-gather.7.cloned.1.call-update
  8.0 0.7 all-gather.5.cloned.1.call-update
  8.7 0.8 reshape.234
  9.5 0.8 reshape.235
  10.3 0.7 reshape.236
  11.0 0.8 reshape.237
  11.8 0.8 concatenate.23
  13.2 61.4 %gather_start.1 = (bf16[4,256,1024]{2,1,0:T(8,128)(2,1)}, bf16[1024,128]{1,0:T(8,128)(2,1)}, bf16[128,1024]{1,0:T(8,128)(2,1)}, bf16[2,1024,384]{2,1,0:T(8,128)(...) custom-call(bf16[256,1024]{1,0:T(8,128)(2,1)} %tok.3, ...), custom_call_target="tpu_custom_call" | custom-call | tf_op jit(solution)/shard_map/gather_start/pallas_call | solution.py:214
  74.6 0.9 reshape.241
  76.6 0.7 slice.118.gain
  78.4 0.7 reshape.270.gain
  79.1 0.7 slice.124.gain
  82.9 23.1 %mixers_forward.1 = (bf16[1024,1024]{1,0:T(8,128)(2,1)}, bf16[1024,128]{1,0:T(8,128)(2,1)}, bf16[1024,128]{1,0:T(8,128)(2,1)}, bf16[1024,128]{1,0:T(8,128)(2,1)}...) custom-call(s32[1]{0:T(128)} %bitcast.kvh, ...), custom_call_target="tpu_custom_call" | custom-call | flops 5000000000 | bytes 15000000 | tf_op jit(solution)/shard_map/mixers_forward/pallas_call | solution.py:485
  106.0 71.1 %mix_scatter.1 = (bf16[1024,384]{1,0:T(8,128)(2,1)}, f32[8,1024]{1,0:T(8,128)}, f32[256,1024]{1,0:T(8,128)}) custom-call(bf16[1024,128]{1,0:T(8,128)(2,1)} %get-tuple-element.73.o, f32[1024,384]{1,0:T(8,128)} %get-tuple-element.74.y, f32[1024,384]{1,0:T(8,128)} %get-tuple-element.75.z_in.zr, f32[8,1024]{1,0:T(8,128)} %get-tuple-element.76.sq, ...), custom_call_target="tpu_custom_call" | custom-call | flops 1000000000 | bytes 130000000 | tf_op jit(solution)/shard_map/mix_scatter/pallas_call | solution.py:1121
  177.2 20.1 %feed_forward.1 = (bf16[256,1024]{1,0:T(8,128)(2,1)}, f32[256,1024]{1,0:T(8,128)}, bf16[256,1024]{1,0:T(8,128)(2,1)}, f32[1,1024]{1,0:T(1,128)}, bf16[8,4,2,128,...) custom-call(f32[256,1024]{1,0:T(8,128)} %get-tuple-element.79.hid, f32[1,1024]{1,0:T(1,128)} %slice.124.gain, ...), custom_call_target="tpu_custom_call" | custom-call | flops 10000000000 | bytes 26000000 | tf_op jit(solution)/shard_map/feed_forward/pallas_call | solution.py:846
  197.3 4.6 dynamic-slice_bitcast_fusion
  201.9 52.9 %unmix_gather.1 = (bf16[1024,1024]{1,0:T(8,128)(2,1)}, bf16[1024,128]{1,0:T(8,128)(2,1)}, f32[1024,384]{1,0:T(8,128)}, f32[8,1024]{1,0:T(8,128)}) custom-call(bf16[256,1024]{1,0:T(8,128)(2,1)} %get-tuple-element.85.dmix, f32[1024,384]{1,0:T(8,128)} %get-tuple-element.74.y, f32[1024,384]{1,0:T(8,128)} %get-tuple-element.75.z_in.zr, f32[1,384]{1,0:T(1,128)} %reshape.270.gain, ...), custom_call_target="tpu_custom_call" | custom-call | flops 1000000000 | bytes 130000000 | tf_op jit(solution)/shard_map/unmix_gather/pallas_call | solution.py:1227
  254.8 23.3 %scan_back.1 = (bf16[1024,384]{1,0:T(8,128)(2,1)}, bf16[1024,384]{1,0:T(8,128)(2,1)}, bf16[1024,256]{1,0:T(8,128)(2,1)}, f32[8,1024]{1,0:T(8,128)}, f32[8,384]{1...) custom-call(f32[1024,384]{1,0:T(8,128)} %get-tuple-element.88.dm, ...), custom_call_target="tpu_custom_call" | custom-call | flops 4000000000 | bytes 15000000 | tf_op jit(solution)/shard_map/scan_back/pallas_call | solution.py:757
  278.1 0.7 reshape.253
  278.8 9.3 %attend_back.1 = (bf16[1024,128]{1,0:T(8,128)(2,1)}, bf16[1024,256]{1,0:T(8,128)(2,1)}) custom-call(s32[1]{0:T(128)} %bitcast.kvh, bf16[1024,128]{1,0:T(8,128)(2,1)} %get-tuple-element.81.q, bf16[1024,128]{1,0:T(8,128)(2,1)} %get-tuple-element.82.k2, bf16[1024,128]{1,0:T(8,128)(2,1)} %get-tuple-element.83.v2, f32[8,1024]{1,0:T(8,128)} %get-tuple-element.84.lse, ...), custom_call_target="tpu_custom_call" | custom-call | flops 2000000000 | bytes 3000000 | tf_op jit(solution)/shard_map/attend_back/pallas_call | solution.py:569
  288.0 9.7 %weight_pieces.1 = (bf16[8,1408,128]{2,1,0:T(8,128)(2,1)}, bf16[8,128,512]{2,1,0:T(8,128)(2,1)}, f32[8,1024]{1,0:T(8,128)}) custom-call(bf16[1024,1024]{1,0:T(8,128)(2,1)} %get-tuple-element.101.a1, bf16[1024,128]{1,0:T(8,128)(2,1)} %get-tuple-element.87.dq, bf16[1024,384]{1,0:T(8,128)(2,1)} %get-tuple-element.95.dz, ...), custom_call_target="tpu_custom_call" | custom-call | flops 4000000000 | bytes 12000000 | tf_op jit(solution)/shard_map/weight_pieces/pallas_call | solution.py:939
  297.8 0.8 reshape.256
  298.6 3.1 dynamic-slice_bitcast_fusion.1
  301.7 0.8 slice_reduce_fusion.2
  303.6 8.4 %down_parts.1 = bf16[1024,1024]{1,0:T(8,128)(2,1)} custom-call(bf16[1024,128]{1,0:T(8,128)(2,1)} %get-tuple-element.87.dq, bf16[1024,384]{1,0:T(8,128)(2,1)} %get-tuple-element.95.dz, bf16[1024,384]{1,0:T(8,128)(2,1)} %get-tuple-element.96.dx, bf16[1024,256]{1,0:T(8,128)(2,1)} %get-tuple-element.97.dkv, bf16[1024,256]{1,0:T(8,128)(2,1)} %get-tuple-element.98.db, ...), custom_call_target="tpu_custom_call" | custom-call | flops 3000000000 | bytes 8000000 | tf_op jit(solution)/shard_map/down_parts/pallas_call | solution.py:884
  312.0 58.9 %tail.1 = (bf16[256,1024]{1,0:T(8,128)(2,1)}, f32[1408,128]{1,0:T(8,128)}, f32[32,512]{1,0:T(8,128)}, f32[96,128]{1,0:T(8,128)}, f32[8,128]{1,0:T(8,128)}) custom-call(bf16[4,256,1024]{2,1,0:T(8,128)(2,1)} %bitcast.189, bf16[256,1024]{1,0:T(8,128)(2,1)} %tok.3, f32[1,1024]{1,0:T(1,128)} %slice.118.gain, f32[256,1024]{1,0:T(8,128)} %get-tuple-element.100.dh, ...), custom_call_target="tpu_custom_call" | custom-call | flops 10000000 | bytes 150000000 | tf_op jit(solution)/shard_map/tail/pallas_call | solution.py:1436
  370.9 0.7 slice.144
  371.6 0.7 slice.145
  372.3 1.8 fusion.53
  374.3 0.8 slice_bitcast_fusion
  376.0 0.7 constant_dynamic-slice_fusion.2
  376.6 0.7 constant_dynamic-slice_fusion.3
  377.9 1.5 fusion.54
  379.4 2.1 fusion.1
  382.0 0.9 collective-permute-start.12
  382.9 5.0 %fusion = bf16[4,4,2,128,512]{4,3,2,1,0:T(8,128)(2,1)S(1)} fusion(bf16[4,4,2,128,512]{4,3,2,1,0:T(8,128)(2,1)} %collective-permute-done, bf16[4,2,4,2,128,512]{5,4,3,2,1,0:T(8,128)(2,1)} %bitcast.185, s32[]{:T(128)S(6)} %select_n.93), kind=kLoop, calls=%fused_computation.1 | loop fusion | flops 8388608 | bytes 12582916 | tf_op jit(solution)/shard_map/convert_element_type | solution.py:233
  388.4 1.6 collective-permute-start.3
  390.0 6.8 %collective-permute-done.14 = bf16[2,2,512,128]{3,2,1,0:T(8,128)(2,1)S(1)} collective-permute-done((bf16[2,2,512,128]{3,2,1,0:T(8,128)(2,1)S(1)}, bf16[2,2,512,128]{3,2,1,0:T(8,128)(2,1)S(1)}, u32[]{:S(2)}, u32[]{:S(2)}) %collective-permute-start.14) | collective-permute-done | bytes 524320 | tf_op jit(solution)/shard_map/ppermute | solution.py:260
  397.5 1.7 collective-permute-start.15
  399.4 26.0 %collective-permute-done.15 = bf16[2,512,128]{2,1,0:T(8,128)(2,1)S(1)} collective-permute-done((bf16[2,512,128]{2,1,0:T(8,128)(2,1)S(1)}, bf16[2,512,128]{2,1,0:T(8,128)(2,1)S(1)}, u32[]{:S(2)}, u32[]{:S(2)}) %collective-permute-start.15) | collective-permute-done | bytes 262176 | tf_op jit(solution)/shard_map/ppermute | solution.py:260
  427.2 2.5 collective-permute-start.16
  429.7 0.7 collective-permute-start.19
  430.4 4.8 %collective-permute-done.4 = bf16[2,2,128,512]{3,2,1,0:T(8,128)(2,1)S(1)} collective-permute-done((bf16[2,2,128,512]{3,2,1,0:T(8,128)(2,1)S(1)}, bf16[2,2,128,512]{3,2,1,0:T(8,128)(2,1)S(1)}, u32[]{:S(2)}, u32[]{:S(2)}) %collective-permute-start.4) | collective-permute-done | bytes 524320 | tf_op jit(solution)/shard_map/ppermute | solution.py:260
  435.3 0.7 collective-permute-done.2
  436.4 2.5 collective-permute-start.5
  438.9 0.7 collective-permute-start.8
  439.6 1.3 fusion.49
  440.9 0.7 slice.150
  441.8 1.3 collective-permute-start.17
  443.1 0.7 collective-permute-start.20
  443.8 1.6 collective-permute-done.5
  445.7 4.4 collective-permute-start.6
  450.1 0.7 collective-permute-start.9
  450.8 0.7 constant_dynamic-slice_fusion
  451.4 0.7 slice.149
  452.1 0.8 fusion.32
  453.0 3.2 collective-permute-start.18
  456.1 1.3 collective-permute-start.21
  457.7 1.4 collective-permute-start.10
  459.2 5.8 %collective-permute-start.7 = (bf16[2,128,512]{2,1,0:T(8,128)(2,1)S(1)}, bf16[2,128,512]{2,1,0:T(8,128)(2,1)S(1)}, u32[]{:S(2)}, u32[]{:S(2)}) collective-permute-start(bf16[2,128,512]{2,1,0:T(8,128)(2,1)S(1)} %get-tuple-element.178), channel_id=1, source_target_pairs={{0,1},{1,2},{2,3},{4,5},{5,6},{6,7},{8,9},{9,10},{10,11},{12,13},{... | collective-permute-start | bytes 786440 | tf_op jit(solution)/shard_map/ppermute | solution.py:245
  465.6 0.9 copy.79
  466.5 1.8 fusion.33
  468.8 1.0 fusion.14
  469.8 0.8 copy.95
  (127 shorter events, 15.1 us)
Async XLA Ops:
  7.2 70.4 %copy-start.6 = (bf16[6]{0:T(256)(128)(2,1)S(1)}, bf16[6]{0:T(256)(128)(2,1)}, u32[]{:S(2)}) copy-start(bf16[6]{0:T(256)(128)(2,1)} %param.31) | copy-start | bytes 40
  7.2 73.2 %copy-start.7 = (bf16[6]{0:T(256)(128)(2,1)S(1)}, bf16[6]{0:T(256)(128)(2,1)}, u32[]{:S(2)}) copy-start(bf16[6]{0:T(256)(128)(2,1)} %param.29) | copy-start | bytes 40
  7.2 73.2 %copy-start.8 = (bf16[6]{0:T(256)(128)(2,1)S(1)}, bf16[6]{0:T(256)(128)(2,1)}, u32[]{:S(2)}) copy-start(bf16[6]{0:T(256)(128)(2,1)} %param.30) | copy-start | bytes 40
  7.2 169.9 %all-gather.7.cloned.1.call-start = ((), (), s32[]{:S(2)}) async-start(), calls=%async_computation.1 | async-start | bytes 4325376 | tf_op jit(solution)/shard_map/all_gather | solution.py:1519
  8.0 169.2 %all-gather.5.cloned.1.call-start = ((), (), s32[]{:S(2)}) async-start(), calls=%async_computation | async-start | bytes 8650752 | tf_op jit(solution)/shard_map/all_gather | solution.py:1516
  201.9 181.0 %collective-permute-start = (bf16[4,4,2,128,512]{4,3,2,1,0:T(8,128)(2,1)}, bf16[4,4,2,128,512]{4,3,2,1,0:T(8,128)(2,1)}, u32[]{:S(2)}, u32[]{:S(2)}) collective-permute-start(bf16[4,4,2,128,512]{4,3,2,1,0:T(8,128)(2,1)} %dynamic-slice_bitcast_fusion), channel_id=1, source_target_pairs={{0,4},{4,0},{8,12},{12,8},{16,20},{20,16},{24,28},{28,24},{1,5},{5... | collective-permute-start | bytes 12582920 | tf_op jit(solution)/shard_map/ppermute | solution.py:260
  298.6 4.1 copy-start.2
  298.6 4.2 copy-start.3
  298.6 4.4 copy-start.5
  301.7 77.8 %collective-permute-start.11 = (bf16[4,4,512,128]{3,2,1,0:T(8,128)(2,1)}, bf16[4,4,512,128]{3,2,1,0:T(8,128)(2,1)S(1)}, u32[]{:S(2)}, u32[]{:S(2)}) collective-permute-start(bf16[4,4,512,128]{3,2,1,0:T(8,128)(2,1)} %dynamic-slice_bitcast_fusion.1), channel_id=1, source_target_pairs={{0,4},{4,0},{8,12},{12,8},{16,20},{20,16},{24,28},{28,24},{1,5},{5... | collective-permute-start | bytes 6291464 | tf_op jit(solution)/shard_map/ppermute | solution.py:260
  381.8 14.9 %collective-permute-start.14 = (bf16[2,2,512,128]{3,2,1,0:T(8,128)(2,1)S(1)}, bf16[2,2,512,128]{3,2,1,0:T(8,128)(2,1)S(1)}, u32[]{:S(2)}, u32[]{:S(2)}) collective-permute-start(bf16[2,2,512,128]{3,2,1,0:T(8,128)(2,1)S(1)} %dynamic-slice_bitcast_fusion.4), channel_id=1, source_target_pairs={{0,16},{4,20},{8,24},{12,28},{16,0},{20,4},{24,8},{28,12},{1,17},{... | collective-permute-start | bytes 1572872 | tf_op jit(solution)/shard_map/ppermute | solution.py:260
  382.0 17.2 %collective-permute-start.12 = (bf16[2,2,512,128]{3,2,1,0:T(8,128)(2,1)S(1)}, bf16[2,2,512,128]{3,2,1,0:T(8,128)(2,1)S(1)}, u32[]{:S(2)}, u32[]{:S(2)}) collective-permute-start(bf16[2,2,512,128]{3,2,1,0:T(8,128)(2,1)S(1)} %dynamic-slice_bitcast_fusion.5), channel_id=1, source_target_pairs={{0,8},{4,12},{8,0},{12,4},{16,24},{20,28},{24,16},{28,20},{1,9},{5... | collective-permute-start | bytes 1572872 | tf_op jit(solution)/shard_map/ppermute | solution.py:260
  388.4 37.2 %collective-permute-start.3 = (bf16[2,2,2,128,512]{4,3,2,1,0:T(8,128)(2,1)S(1)}, bf16[2,2,2,128,512]{4,3,2,1,0:T(8,128)(2,1)S(1)}, u32[]{:S(2)}, u32[]{:S(2)}) collective-permute-start(bf16[2,2,2,128,512]{4,3,2,1,0:T(8,128)(2,1)S(1)} %dynamic-slice_bitcast_fusion.2), channel_id=1, source_target_pairs={{0,16},{4,20},{8,24},{12,28},{16,0},{20,4},{24,8},{28,12},{1,17},{... | collective-permute-start | bytes 3145736 | tf_op jit(solution)/shard_map/ppermute | solution.py:260
  397.0 29.4 %collective-permute-start.1 = (bf16[2,2,2,128,512]{4,3,2,1,0:T(8,128)(2,1)S(1)}, bf16[2,2,2,128,512]{4,3,2,1,0:T(8,128)(2,1)S(1)}, u32[]{:S(2)}, u32[]{:S(2)}) collective-permute-start(bf16[2,2,2,128,512]{4,3,2,1,0:T(8,128)(2,1)S(1)} %dynamic-slice_bitcast_fusion.3), channel_id=1, source_target_pairs={{0,8},{4,12},{8,0},{12,4},{16,24},{20,28},{24,16},{28,20},{1,9},{5... | collective-permute-start | bytes 3145736 | tf_op jit(solution)/shard_map/ppermute | solution.py:260
  397.5 28.0 %collective-permute-start.15 = (bf16[2,512,128]{2,1,0:T(8,128)(2,1)S(1)}, bf16[2,512,128]{2,1,0:T(8,128)(2,1)S(1)}, u32[]{:S(2)}, u32[]{:S(2)}) collective-permute-start(bf16[2,512,128]{2,1,0:T(8,128)(2,1)S(1)} %dynamic-slice_bitcast_fusion.8), channel_id=1, source_target_pairs={{0,8},{4,12},{8,0},{12,4},{16,24},{20,28},{24,16},{28,20},{1,9},{5... | collective-permute-start | bytes 786440 | tf_op jit(solution)/shard_map/ppermute | solution.py:260
  399.3 27.6 %collective-permute-start.13 = (bf16[2,512,128]{2,1,0:T(8,128)(2,1)S(1)}, bf16[2,512,128]{2,1,0:T(8,128)(2,1)S(1)}, u32[]{:S(2)}, u32[]{:S(2)}) collective-permute-start(bf16[2,512,128]{2,1,0:T(8,128)(2,1)S(1)} %dynamic-slice_bitcast_fusion.9), channel_id=1, source_target_pairs={{0,16},{4,20},{8,24},{12,28},{16,0},{20,4},{24,8},{28,12},{1,17},{... | collective-permute-start | bytes 786440 | tf_op jit(solution)/shard_map/ppermute | solution.py:260
  425.9 9.2 %collective-permute-start.4 = (bf16[2,2,128,512]{3,2,1,0:T(8,128)(2,1)S(1)}, bf16[2,2,128,512]{3,2,1,0:T(8,128)(2,1)S(1)}, u32[]{:S(2)}, u32[]{:S(2)}) collective-permute-start(bf16[2,2,128,512]{3,2,1,0:T(8,128)(2,1)S(1)} %dynamic-slice_bitcast_fusion.6), channel_id=1, source_target_pairs={{0,8},{4,12},{8,0},{12,4},{16,24},{20,28},{24,16},{28,20},{1,9},{5... | collective-permute-start | bytes 1572872 | tf_op jit(solution)/shard_map/ppermute | solution.py:260
  426.8 9.2 %collective-permute-start.2 = (bf16[2,2,128,512]{3,2,1,0:T(8,128)(2,1)S(1)}, bf16[2,2,128,512]{3,2,1,0:T(8,128)(2,1)S(1)}, u32[]{:S(2)}, u32[]{:S(2)}) collective-permute-start(bf16[2,2,128,512]{3,2,1,0:T(8,128)(2,1)S(1)} %dynamic-slice_bitcast_fusion.7), channel_id=1, source_target_pairs={{0,16},{4,20},{8,24},{12,28},{16,0},{20,4},{24,8},{28,12},{1,17},{... | collective-permute-start | bytes 1572872 | tf_op jit(solution)/shard_map/ppermute | solution.py:260
  427.2 14.4 %collective-permute-start.16 = (bf16[512,128]{1,0:T(8,128)(2,1)S(1)}, bf16[512,128]{1,0:T(8,128)(2,1)S(1)}, u32[]{:S(2)}, u32[]{:S(2)}) collective-permute-start(bf16[512,128]{1,0:T(8,128)(2,1)S(1)} %get-tuple-element.193), channel_id=1, source_target_pairs={{0,1},{4,5},{8,9},{12,13},{16,17},{20,21},{24,25},{28,29}} | collective-permute-start | bytes 393224 | tf_op jit(solution)/shard_map/ppermute | solution.py:245
  429.7 11.9 %collective-permute-start.19 = (bf16[512,128]{1,0:T(8,128)(2,1)S(1)}, bf16[512,128]{1,0:T(8,128)(2,1)S(1)}, u32[]{:S(2)}, u32[]{:S(2)}) collective-permute-start(bf16[512,128]{1,0:T(8,128)(2,1)S(1)} %get-tuple-element.194), channel_id=1, source_target_pairs={{3,2},{7,6},{11,10},{15,14},{19,18},{23,22},{27,26},{31,30}} | collective-permute-start | bytes 393224 | tf_op jit(solution)/shard_map/ppermute | solution.py:246
  436.4 9.0 %collective-permute-start.5 = (bf16[2,128,512]{2,1,0:T(8,128)(2,1)S(1)}, bf16[2,128,512]{2,1,0:T(8,128)(2,1)S(1)}, u32[]{:S(2)}, u32[]{:S(2)}) collective-permute-start(bf16[2,128,512]{2,1,0:T(8,128)(2,1)S(1)} %get-tuple-element.182), channel_id=1, source_target_pairs={{0,1},{4,5},{8,9},{12,13},{16,17},{20,21},{24,25},{28,29}} | collective-permute-start | bytes 786440 | tf_op jit(solution)/shard_map/ppermute | solution.py:245
  438.9 6.5 %collective-permute-start.8 = (bf16[2,128,512]{2,1,0:T(8,128)(2,1)S(1)}, bf16[2,128,512]{2,1,0:T(8,128)(2,1)S(1)}, u32[]{:S(2)}, u32[]{:S(2)}) collective-permute-start(bf16[2,128,512]{2,1,0:T(8,128)(2,1)S(1)} %get-tuple-element.183), channel_id=1, source_target_pairs={{3,2},{7,6},{11,10},{15,14},{19,18},{23,22},{27,26},{31,30}} | collective-permute-start | bytes 786440 | tf_op jit(solution)/shard_map/ppermute | solution.py:246
  441.8 10.3 %collective-permute-start.17 = (bf16[512,128]{1,0:T(8,128)(2,1)S(1)}, bf16[512,128]{1,0:T(8,128)(2,1)S(1)}, u32[]{:S(2)}, u32[]{:S(2)}) collective-permute-start(bf16[512,128]{1,0:T(8,128)(2,1)S(1)} %get-tuple-element.191), channel_id=1, source_target_pairs={{0,1},{1,2},{4,5},{5,6},{8,9},{9,10},{12,13},{13,14},{16,17},{17,1... | collective-permute-start | bytes 393224 | tf_op jit(solution)/shard_map/ppermute | solution.py:245
  443.1 9.0 %collective-permute-start.20 = (bf16[512,128]{1,0:T(8,128)(2,1)S(1)}, bf16[512,128]{1,0:T(8,128)(2,1)S(1)}, u32[]{:S(2)}, u32[]{:S(2)}) collective-permute-start(bf16[512,128]{1,0:T(8,128)(2,1)S(1)} %get-tuple-element.192), channel_id=1, source_target_pairs={{3,2},{2,1},{7,6},{6,5},{11,10},{10,9},{15,14},{14,13},{19,18},{18... | collective-permute-start | bytes 393224 | tf_op jit(solution)/shard_map/ppermute | solution.py:246
  445.7 19.3 %copy-start.4 = (f32[8,128]{1,0:T(8,128)S(1)}, f32[8,128]{1,0:T(8,128)}, u32[]{:S(2)}) copy-start(f32[8,128]{1,0:T(8,128)} %get-tuple-element.118) | copy-start | bytes 12292
  445.7 11.7 %collective-permute-start.6 = (bf16[2,128,512]{2,1,0:T(8,128)(2,1)S(1)}, bf16[2,128,512]{2,1,0:T(8,128)(2,1)S(1)}, u32[]{:S(2)}, u32[]{:S(2)}) collective-permute-start(bf16[2,128,512]{2,1,0:T(8,128)(2,1)S(1)} %get-tuple-element.180), channel_id=1, source_target_pairs={{0,1},{1,2},{4,5},{5,6},{8,9},{9,10},{12,13},{13,14},{16,17},{17,1... | collective-permute-start | bytes 786440 | tf_op jit(solution)/shard_map/ppermute | solution.py:245
  450.1 7.3 %collective-permute-start.9 = (bf16[2,128,512]{2,1,0:T(8,128)(2,1)S(1)}, bf16[2,128,512]{2,1,0:T(8,128)(2,1)S(1)}, u32[]{:S(2)}, u32[]{:S(2)}) collective-permute-start(bf16[2,128,512]{2,1,0:T(8,128)(2,1)S(1)} %get-tuple-element.181), channel_id=1, source_target_pairs={{3,2},{2,1},{7,6},{6,5},{11,10},{10,9},{15,14},{14,13},{19,18},{18... | collective-permute-start | bytes 786440 | tf_op jit(solution)/shard_map/ppermute | solution.py:246
  453.0 13.5 %collective-permute-start.18 = (bf16[512,128]{1,0:T(8,128)(2,1)}, bf16[512,128]{1,0:T(8,128)(2,1)}, u32[]{:S(2)}, u32[]{:S(2)}) collective-permute-start(bf16[512,128]{1,0:T(8,128)(2,1)} %get-tuple-element.189), channel_id=1, source_target_pairs={{0,1},{1,2},{2,3},{4,5},{5,6},{6,7},{8,9},{9,10},{10,11},{12,13},{... | collective-permute-start | bytes 393224 | tf_op jit(solution)/shard_map/ppermute | solution.py:245
  456.1 10.4 %collective-permute-start.21 = (bf16[512,128]{1,0:T(8,128)(2,1)}, bf16[512,128]{1,0:T(8,128)(2,1)}, u32[]{:S(2)}, u32[]{:S(2)}) collective-permute-start(bf16[512,128]{1,0:T(8,128)(2,1)} %get-tuple-element.190), channel_id=1, source_target_pairs={{3,2},{2,1},{1,0},{7,6},{6,5},{5,4},{11,10},{10,9},{9,8},{15,14},{... | collective-permute-start | bytes 393224 | tf_op jit(solution)/shard_map/ppermute | solution.py:246
  457.7 12.0 %copy-start = (bf16[256,1024]{1,0:T(8,128)(2,1)S(1)}, bf16[256,1024]{1,0:T(8,128)(2,1)}, u32[]{:S(2)}) copy-start(bf16[256,1024]{1,0:T(8,128)(2,1)} %get-tuple-element.218) | copy-start | bytes 1572868
  457.7 10.6 %collective-permute-start.10 = (bf16[2,128,512]{2,1,0:T(8,128)(2,1)S(1)}, bf16[2,128,512]{2,1,0:T(8,128)(2,1)S(1)}, u32[]{:S(2)}, u32[]{:S(2)}) collective-permute-start(bf16[2,128,512]{2,1,0:T(8,128)(2,1)S(1)} %get-tuple-element.179), channel_id=1, source_target_pairs={{3,2},{2,1},{1,0},{7,6},{6,5},{5,4},{11,10},{10,9},{9,8},{15,14},{... | collective-permute-start | bytes 786440 | tf_op jit(solution)/shard_map/ppermute | solution.py:246
  459.2 9.6 %collective-permute-start.7 = (bf16[2,128,512]{2,1,0:T(8,128)(2,1)S(1)}, bf16[2,128,512]{2,1,0:T(8,128)(2,1)S(1)}, u32[]{:S(2)}, u32[]{:S(2)}) collective-permute-start(bf16[2,128,512]{2,1,0:T(8,128)(2,1)S(1)} %get-tuple-element.178), channel_id=1, source_target_pairs={{0,1},{1,2},{2,3},{4,5},{5,6},{6,7},{8,9},{9,10},{10,11},{12,13},{... | collective-permute-start | bytes 786440 | tf_op jit(solution)/shard_map/ppermute | solution.py:245
  466.5 4.1 copy-start.1
Sparse Core Ops, SparseCore 0:
  11.0 68.3 all-gather.6
  82.3 94.5 all-gather.4

commit v4 on v3

--- a/solution.py
+++ b/solution.py
@@ -35,158 +35,145 @@
     return core, xbit, ybit
 
 
+def remote_copy(src, dst, send, recv, dev):
+    return pltpu.make_async_remote_copy(
+        src_ref=src, dst_ref=dst, send_sem=send, recv_sem=recv, device_id=dev, device_id_type=MESH
+    )
+
+
+def greet(peers):
+    barrier = pltpu.get_barrier_semaphore()
+    for peer in peers:
+        pl.semaphore_signal(barrier, inc=1, device_id=peer, device_id_type=MESH)
+    pl.semaphore_wait(barrier, len(peers))
+
+
+def other_quarters(d, z, nt):
+    return [(d, lax.rem(z + k, nt)) for k in range(1, nt)]
+
+
+def cube_peers(d):
+    core, xbit, ybit = dp_bits(d)
+    return d + 1 - 2 * core, d + 2 - 4 * xbit, d + 4 - 8 * ybit
+
+
+class CubeGather:
+    def __init__(self, items, via_y, send, recv, d, z):
+        self.items, self.via_y, self.send, self.recv = items, via_y, send, recv
+        self.d, self.z = d, z
+        self.d_core, self.d_x, self.d_y = cube_peers(d)
+        self.d_xy = self.d_x + self.d_y - d
+        self.sent = []
+
+    def push(self, i, j, src, dst, peer):
+        copy = remote_copy(src, dst, self.send.at[i, j], self.recv.at[i, j], (peer, self.z))
+        copy.start()
+        self.sent.append(copy)
+
+    def landed(self, i, j, slot):
+        at = self.items[i][1]
+        remote_copy(
+            at(slot), at(slot), self.send.at[i, j], self.recv.at[i, j], (self.d_core, self.z)
+        ).wait_recv()
+
+    def start(self, i):
+        src, at = self.items[i]
+        for j, peer in enumerate((self.d_x, self.d_y, self.d_core)):
+            self.push(i, j, src, at(self.d), peer)
+
+    def near(self, i):
+        at = self.items[i][1]
+        d_x, d_y, d_core = self.d_x, self.d_y, self.d_core
+        self.landed(i, 0, d_x)
+        if i in self.via_y:
+            self.push(i, 3, at(d_x), at(d_x), d_y)
+        self.push(i, 4, at(d_x), at(d_x), d_core)
+        self.landed(i, 1, d_y)
+        if i not in self.via_y:
+            self.push(i, 3, at(d_y), at(d_y), d_x)
+        self.push(i, 5, at(d_y), at(d_y), d_core)
+
+    def far(self, i):
+        at = self.items[i][1]
+        self.landed(i, 3, self.d_xy)
+        self.push(i, 6, at(self.d_xy), at(self.d_xy), self.d_core)
+
+    def finish(self):
+        for i in range(len(self.items)):
+            self.landed(i, 2, self.d_core)
+            for j in (4, 5, 6):
+                self.landed(i, j, self.d_core)
+        for copy in self.sent:
+            copy.wait_send()
+
+
 def gather_kernel(nt, *refs):
-    (tok, que, att, inn, mam, sha, sma) = refs[:7]
-    (tok_f, que_f, att_f, inn_f, mam_f, sha_f, sma_f) = refs[7:14]
-    (lsem, zs_send, zs_recv, t_send, t_recv, d_send, d_recv) = refs[14:]
+    (tok, que, att, inn, mam, hid, dwn, sha, sma) = refs[:9]
+    (tok_f, que_f, att_f, inn_f, mam_f, hid_f, dwn_f, sha_f, sma_f) = refs[9:18]
+    (lsem, zs_send, zs_recv, t_send, t_recv, d_send, d_recv) = refs[18:]
     d = lax.axis_index("dp")
     z = lax.axis_index("tensor")
-    core, xbit, ybit = dp_bits(d)
-    d_core = d + 1 - 2 * core
-    d_x = d + 2 - 4 * xbit
-    d_y = d + 4 - 8 * ybit
-    d_xy = d_x + 4 - 8 * ybit
-
-    barrier = pltpu.get_barrier_semaphore()
-    for peer in (d_core, d_x, d_y):
-        pl.semaphore_signal(barrier, inc=1, device_id=(peer, z), device_id_type=MESH)
-    for k in range(1, nt):
-        pl.semaphore_signal(
-            barrier, inc=1, device_id=(d, lax.rem(z + k, nt)), device_id_type=MESH
-        )
-    pl.semaphore_wait(barrier, 3 + nt - 1)
-
-    def remote(src, dst, send, recv, dev):
-        return pltpu.make_async_remote_copy(
-            src_ref=src, dst_ref=dst, send_sem=send, recv_sem=recv,
-            device_id=dev, device_id_type=MESH,
-        )
+    greet([(p, z) for p in cube_peers(d)] + other_quarters(d, z, nt))
 
     small = []
     for i, (src, dst) in enumerate(((sha, sha_f), (sma, sma_f))):
-        for k in range(1, nt):
-            copy = remote(
-                src, dst.at[d, z], zs_send.at[i, k], zs_recv.at[i, k],
-                (d, lax.rem(z + k, nt)),
-            )
-            copy.start()
-            small.append(copy)
+        for k, peer in enumerate(other_quarters(d, z, nt)):
+            small.append(remote_copy(src, dst.at[d, z], zs_send.at[i, k], zs_recv.at[i, k], peer))
+            small[-1].start()
     q_rows = que.shape[0]
     cols = att.shape[1]
     i_rows = inn.shape[1]
-    items = (
+    items = [
         (inn, lambda s: inn_f.at[:, pl.ds(s * i_rows, i_rows)]),
         (que, lambda s: que_f.at[pl.ds(s * q_rows, q_rows)]),
         (att, lambda s: att_f.at[:, pl.ds(pl.multiple_of(s * cols, cols), cols)]),
         (mam, lambda s: mam_f.at[:, pl.ds(pl.multiple_of(s * cols, cols), cols)]),
-    )
+        (hid, lambda s: hid_f.at[s, z]),
+        (dwn, lambda s: dwn_f.at[s, z]),
+        (sha_f.at[d], lambda s: sha_f.at[s]),
+        (sma_f.at[d], lambda s: sma_f.at[s]),
+    ]
+    cube = CubeGather(items, (0, 5, 7), d_send, d_recv, d, z)
     locals_ = []
     for i, (src, dst) in enumerate(
-        [(tok, tok_f.at[z]), (sha, sha_f.at[d, z]), (sma, sma_f.at[d, z])]
-        + [(src, at(d)) for src, at in items]
+        [(sha, sha_f.at[d, z]), (sma, sma_f.at[d, z]), (tok, tok_f.at[z])]
+        + [(src, at(d)) for src, at in items[:6]]
     ):
         copy = pltpu.make_async_copy(src, dst, lsem.at[i])
         copy.start()
         locals_.append(copy)
-    sent = []
-
-    def stage_one(i, src, at):
-        for j, peer in enumerate((d_x, d_y, d_core)):
-            copy = remote(src, at(d), d_send.at[i, j], d_recv.at[i, j], (peer, z))
-            copy.start()
-            sent.append(copy)
-
-    for i, (src, at) in enumerate(items):
-        stage_one(i, src, at)
-
-    def tok_copy(slot, dirn, hop):
-        dev = z + 1 if dirn == 0 else z - 1
-        return remote(
-            tok_f.at[slot], tok_f.at[slot], t_send.at[dirn, hop], t_recv.at[dirn, hop], (d, dev)
-        )
-
-    def own_copy(dirn):
-        dev = z + 1 if dirn == 0 else z - 1
-        return remote(tok, tok_f.at[z], t_send.at[dirn, 0], t_recv.at[dirn, 0], (d, dev))
-
-    pl.when(z < nt - 1)(lambda: own_copy(0).start())
-    pl.when(z > 0)(lambda: own_copy(1).start())
-
+    for i in range(4):
+        cube.start(i)
+    chain = ChainGather(tok, tok_f, t_send, t_recv, d, z, nt)
+    chain.start()
+    locals_[0].wait()
     locals_[1].wait()
-    locals_[2].wait()
     for copy in small:
         copy.wait()
-    n = len(items)
-    shared_items = (
-        (sha_f.at[d], lambda s: sha_f.at[s]),
-        (sma_f.at[d], lambda s: sma_f.at[s]),
-    )
-    for i, (src, at) in enumerate(shared_items):
-        stage_one(n + i, src, at)
-
-    def wait_recv(i, j, at, slot):
-        remote(at(slot), at(slot), d_send.at[i, j], d_recv.at[i, j], (d_core, z)).wait_recv()
-
-    def forward(i, j, at, slot, peer):
-        copy = remote(at(slot), at(slot), d_send.at[i, j], d_recv.at[i, j], (peer, z))
-        copy.start()
-        sent.append(copy)
-
-    everything = [at for _, at in items] + [at for _, at in shared_items]
-    via_y = (0, n + 1)
-
-    def diagonal(i, at):
-        wait_recv(i, 0, at, d_x)
-        if i in via_y:
-            forward(i, 3, at, d_x, d_y)
-        forward(i, 4, at, d_x, d_core)
-        wait_recv(i, 1, at, d_y)
-        if i not in via_y:
-            forward(i, 3, at, d_y, d_x)
-        forward(i, 5, at, d_y, d_core)
-
-    for i in range(n):
-        diagonal(i, everything[i])
-
-    def hop(dist):
-        def from_left():
-            tok_copy(z - dist, 0, dist - 1).wait_recv()
-
-        def from_right():
-            tok_copy(z + dist, 1, dist - 1).wait_recv()
-
-        pl.when(z >= dist)(from_left)
-        if dist < nt - 1:
-            pl.when((z >= dist) & (z < nt - 1))(lambda: tok_copy(z - dist, 0, dist).start())
-        pl.when(z + dist < nt)(from_right)
-        if dist < nt - 1:
-            pl.when((z + dist < nt) & (z > 0))(lambda: tok_copy(z + dist, 1, dist).start())
-
-    hop(1)
-    for i in range(n, n + 2):
-        diagonal(i, everything[i])
-    for i, at in enumerate(everything):
-        wait_recv(i, 3, at, d_xy)
-        forward(i, 6, at, d_xy, d_core)
-    for dist in range(2, nt):
-        hop(dist)
-    for i, at in enumerate(everything):
-        wait_recv(i, 2, at, d_core)
-        for j in (4, 5, 6):
-            wait_recv(i, j, at, d_core)
-    for i, copy in enumerate(locals_):
-        if i not in (1, 2):
-            copy.wait()
-    for copy in sent:
-        copy.wait_send()
-    pl.when(z < nt - 1)(lambda: own_copy(0).wait_send())
-    pl.when(z > 0)(lambda: own_copy(1).wait_send())
-    for dist in range(1, nt - 1):
-        pl.when((z >= dist) & (z < nt - 1))(lambda: tok_copy(z - dist, 0, dist).wait_send())
-        pl.when((z + dist < nt) & (z > 0))(lambda: tok_copy(z + dist, 1, dist).wait_send())
-
-
-def gather_start(tok, que, att, inn, mam, sha, sma, nd, nt):
+    cube.start(6)
+    cube.start(7)
+    cube.start(4)
+    cube.start(5)
+    for i in range(4):
+        cube.near(i)
+    chain.hop(1)
+    for i in (6, 7, 4, 5):
+        cube.near(i)
+    for i in (0, 1, 2, 3, 6, 7):
+        cube.far(i)
+    for dist in range(2, nt - 1):
+        chain.hop(dist)
+    cube.far(4)
+    cube.far(5)
+    if nt > 2:
+        chain.hop(nt - 1)
+    cube.finish()
+    for copy in locals_[2:]:
+        copy.wait()
+    chain.drain()
+
+
+def gather_start(tok, que, att, inn, mam, hid, dwn, sha, sma, nd, nt):
     if nd != 8:
         shared = lax.all_gather(sha, ("dp", "tensor"), axis=0)
         small = lax.all_gather(sma, ("dp", "tensor"), axis=0)
@@ -196,6 +183,8 @@
             lax.all_gather(att, "dp", axis=1, tiled=True),
             lax.all_gather(inn, "dp", axis=1, tiled=True),
             lax.all_gather(mam, "dp", axis=1, tiled=True),
+            None,
+            None,
             shared.reshape((nd, nt) + sha.shape),
             small.reshape((nd, nt) + sma.shape),
         )
@@ -206,6 +195,8 @@
         (att.shape[0], nd * att.shape[1]),
         (2, nd * inn.shape[1], inn.shape[2]),
         (mam.shape[0], nd * mam.shape[1]),
+        (nd, nt) + hid.shape,
+        (nd, nt) + dwn.shape,
         (nd, nt) + sha.shape,
         (nd, nt) + sma.shape,
     )
@@ -214,15 +205,15 @@
     return pl.pallas_call(
         partial(gather_kernel, nt),
         out_shape=[jax.ShapeDtypeStruct(s, bf) for s in outs],
-        in_specs=[anywhere] * 7,
-        out_specs=[anywhere] * 7,
+        in_specs=[anywhere] * 9,
+        out_specs=[anywhere] * 9,
         scratch_shapes=[
-            dma((7,)), dma((2, nt)), dma((2, nt)), dma((2, nt)), dma((2, nt)),
-            dma((6, 7)), dma((6, 7)),
+            dma((9,)), dma((2, nt)), dma((2, nt)), dma((2, nt)), dma((2, nt)),
+            dma((8, 7)), dma((8, 7)),
         ],
         compiler_params=pltpu.CompilerParams(collective_id=0, has_side_effects=True),
         name="gather_start",
-    )(tok, que, att, inn, mam, sha, sma)
+    )(tok, que, att, inn, mam, hid, dwn, sha, sma)
 
 
 def pick(values, index, axis=0):
@@ -251,26 +242,7 @@
 
 
 def cube_scatter(parts, nd, last=jnp.float32):
-    if nd != 8:
-        return lax.psum_scatter(parts, "dp", scatter_dimension=0, tiled=False).astype(last)
-    d = lax.axis_index("dp")
-    core, xbit, ybit = dp_bits(d)
-
-    def swap(values, bit):
-        return lax.ppermute(values, "dp", [(i, i ^ bit) for i in range(8)])
-
-    tail = parts.shape[1:]
-    cut = parts.reshape((4, 2) + tail)
-    held = add_low(pick(cut, core, 1), swap(pick(cut, 1 - core, 1), 1))
-    held = held.reshape((2, 2) + tail)
-    half = tail[0] // 2
-    one, two = held[:, :, :half], held[:, :, half:]
-    one_b = add_low(pick(one, xbit, 1), swap(pick(one, 1 - xbit, 1), 2))
-    two_b = add_low(pick(two, ybit, 0), swap(pick(two, 1 - ybit, 0), 4))
-    f32 = jnp.float32
-    one_c = pick(one_b, ybit).astype(f32) + swap(pick(one_b, 1 - ybit), 4).astype(f32)
-    two_c = pick(two_b, xbit).astype(f32) + swap(pick(two_b, 1 - xbit), 2).astype(f32)
-    return jnp.concatenate([one_c, two_c], axis=0).astype(last)
+    return lax.psum_scatter(parts, "dp", scatter_dimension=0, tiled=False).astype(last)
 
 
 F32, BF16 = jnp.float32, jnp.bfloat16
@@ -780,12 +752,25 @@
     return pl.BlockSpec(v.shape, lambda i: (0,) * v.ndim)
 
 
-def feed_kernel(
-    hid, gain, cot, whid, wdown, out_o, dh_o, dmix_o, gg_o, ghid_o, gdown_o, a2, a2t, acc, dacc
-):
+def feed_kernel(paired, hid, gain, cot, whid, wdown, out_o, dh_o, dmix_o, gg_o, piece_o, a2, a2t, acc, dacc, *pair):
     step = pl.program_id(0)
+    tiles = pl.num_programs(0)
     width = hid.shape[1]
     blocks = width // 128
+    units = whid.shape[4]
+    d = lax.axis_index("dp")
+    z = lax.axis_index("tensor")
+    core = lax.rem(d, 2)
+    if paired:
+        (sent, came, send, recv) = pair
+        sibling = d + 1 - 2 * core
+
+        def swap(tile):
+            return remote_copy(
+                sent.at[tile], came.at[tile], send.at[tile], recv.at[tile], (sibling, z)
+            )
+
+        pl.when(step == 0)(lambda: greet([(sibling, z)]))
 
     @pl.when(step == 0)
     def _():
@@ -797,7 +782,6 @@
         acc[...] = jnp.zeros(acc.shape, F32)
         dacc[...] = jnp.zeros(dacc.shape, F32)
 
-    units = whid.shape[4]
     w_gate = whid[:, 0, 0].reshape(width, units)
     w_up = whid[:, 0, 1].reshape(width, units)
     w_down = jnp.concatenate([wdown[k, 0] for k in range(blocks)], axis=1)
@@ -811,13 +795,54 @@
     du = (df * g * s).astype(BF16)
     dg = (df * u * s * (1.0 + g * (1.0 - s))).astype(BF16)
     dacc[...] += dot_nt(dg, w_gate) + dot_nt(du, w_up)
-    ghid_o[:, 0, 0] = dot_nn(a2t[...], dg).astype(BF16).reshape(blocks, 128, units)
-    ghid_o[:, 0, 1] = dot_nn(a2t[...], du).astype(BF16).reshape(blocks, 128, units)
+
+    per = units // 128
+    quarter_units = (piece_o.shape[2] // 3)
+    tiles_per = quarter_units // units
+
+    def places(tile):
+        part = lax.rem(tile, tiles_per)
+        rows = [(k * quarter_units + part * units + cb * 128, 128) for k in range(2) for cb in range(per)]
+        return tile // tiles_per, rows + [(2 * quarter_units + part * units, units)]
+
+    quarter, rows = places(step)
+    values = []
+    for grad in (dg, du):
+        full = dot_nn(a2t[...], grad).astype(BF16)
+        for cb in range(per):
+            values.append(full[:, 128 * cb : 128 * cb + 128].reshape(blocks, 128, 128))
     gd = dot_tn(f_low, c).astype(BF16)
-    for k in range(blocks):
-        gdown_o[k, 0] = gd[:, 128 * k : 128 * k + 128]
-
-    @pl.when(step == pl.num_programs(0) - 1)
+    values.append(jnp.stack([gd[:, 128 * k : 128 * k + 128] for k in range(blocks)]))
+    first = 0
+    for value, (row, n) in zip(values, rows):
+        at = pl.ds(pl.multiple_of(row, 128), n)
+        if paired:
+            value = value.reshape(blocks // 2, 2, n, 128)
+            even, odd = value[:, 0], value[:, 1]
+            piece_o[:, quarter, at, :] = jnp.where(core == 0, even, odd)
+            sent[step, :, first : first + n, :] = jnp.where(core == 0, odd, even)
+            first += n
+        else:
+            piece_o[:, quarter, at, :] = value
+
+    if paired:
+        swap(step).start()
+
+        def take(tile):
+            swap(tile).wait_recv()
+            quarter, rows = places(tile)
+            first = 0
+            for row, n in rows:
+                at = pl.ds(pl.multiple_of(row, 128), n)
+                piece_o[:, quarter, at, :] = (
+                    piece_o[:, quarter, at, :].astype(F32)
+                    + came[tile, :, first : first + n, :].astype(F32)
+                ).astype(BF16)
+                first += n
+
+        pl.when(step > 0)(lambda: take(step - 1))
+
+    @pl.when(step == tiles - 1)
     def _():
         v = hid[...]
         out_o[...] = (v + acc[...]).astype(BF16)
@@ -829,9 +854,17 @@
         dh = cot[...].astype(F32) + (f * gdy - v * lean)
         dh_o[...] = dh
         dmix_o[...] = dh.astype(BF16)
-
-
-def feed_forward(hid, gain, cot, whid, wdown):
+        if paired:
+            take(tiles - 1)
+
+            def sent_all(tile, carry):
+                swap(tile).wait_send()
+                return carry
+
+            lax.fori_loop(0, tiles, sent_all, 0)
+
+
+def feed_forward(paired, hid, gain, cot, whid, wdown):
     rows, width = hid.shape
     blocks, nt, _, depth, units = whid.shape
     tile = 256
@@ -839,21 +872,30 @@
     hid_spec = pl.BlockSpec((blocks, 1, 2, depth, tile), lambda i: (0, i // per, 0, 0, lax.rem(i, per)))
     down_spec = pl.BlockSpec((blocks, 1, tile, 128), lambda i: (0, i // per, lax.rem(i, per), 0))
     sds = jax.ShapeDtypeStruct
+    kept = blocks // 2 if paired else blocks
+    piece = (kept, nt, 3 * units, 128)
+    dma = pltpu.SemaphoreType.DMA
+    scratch = []
+    extra = {}
+    if paired:
+        box = pltpu.VMEM((nt * per, kept, 3 * tile, 128), BF16)
+        scratch = [box, box, dma((nt * per,)), dma((nt * per,))]
+        extra = dict(collective_id=4, has_side_effects=True)
 
     def fixed(*shape):
-        return pl.BlockSpec(shape, lambda i: (0, 0))
+        return pl.BlockSpec(shape, lambda i: (0,) * len(shape))
 
     return pl.pallas_call(
-        feed_kernel,
+        partial(feed_kernel, paired),
         grid=(nt * per,),
         in_specs=[fixed(rows, width), fixed(1, width), fixed(rows, width), hid_spec, down_spec],
-        out_specs=[fixed(rows, width), fixed(rows, width), fixed(rows, width), fixed(1, width), hid_spec,
-                   down_spec],
+        out_specs=[fixed(rows, width), fixed(rows, width), fixed(rows, width), fixed(1, width),
+                   fixed(*piece)],
         out_shape=[sds((rows, width), BF16), sds((rows, width), F32), sds((rows, width), BF16),
-                   sds((1, width), F32), sds(whid.shape, BF16), sds(wdown.shape, BF16)],
+                   sds((1, width), F32), sds(piece, BF16)],
         scratch_shapes=[pltpu.VMEM((rows, width), BF16), pltpu.VMEM((width, rows), BF16),
-                        pltpu.VMEM((rows, width), F32), pltpu.VMEM((rows, width), F32)],
-        compiler_params=pltpu.CompilerParams(vmem_limit_bytes=VMEM_LIMIT),
+                        pltpu.VMEM((rows, width), F32), pltpu.VMEM((rows, width), F32)] + scratch,
+        compiler_params=pltpu.CompilerParams(vmem_limit_bytes=VMEM_LIMIT, **extra),
         cost_estimate=pl.CostEstimate(flops=int(1e10), bytes_accessed=int(26e6), transcendentals=int(5e5)),
         name="feed_forward",
     )(hid, gain, cot, whid, wdown)
@@ -952,23 +994,6 @@
     )(a1, *args, dmix)
 
 
-def remote_copy(src, dst, send, recv, dev):
-    return pltpu.make_async_remote_copy(
-        src_ref=src, dst_ref=dst, send_sem=send, recv_sem=recv, device_id=dev, device_id_type=MESH
-    )
-
-
-def greet(peers):
-    barrier = pltpu.get_barrier_semaphore()
-    for peer in peers:
-        pl.semaphore_signal(barrier, inc=1, device_id=peer, device_id_type=MESH)
-    pl.semaphore_wait(barrier, len(peers))
-
-
-def other_quarters(d, z, nt):
-    return [(d, lax.rem(z + k, nt)) for k in range(1, nt)]
-
-
 class Exchange:
     def __init__(self, own, landed, send, recv, d, z, nt):
         self.own, self.landed, self.z, self.nt = own, landed, z, nt
@@ -1072,17 +1097,37 @@
     ]
 
 
-def mix_scatter_kernel(
-    channels, nt, o, y, z_in, sq, gain, watt, wmam, tok,
-    m_o, sq_o, hid_o,
-    sq_land, sq_send, sq_recv, parts, bufs, landed, c_send, c_recv,
-):
+def mix_scatter_kernel(channels, nt, feed, *refs):
+    (o, y, z_in, sq, gain, watt, wmam, tok), refs = refs[:8], refs[8:]
+    if feed:
+        refs = refs[2:]
+        turned, refs = refs[: 2 * (nt - 1)], refs[2 * (nt - 1) :]
+        (m_o, sq_o, hid_o, hid_f, dwn_f), refs = refs[:5], refs[5:]
+        (lsem, f_send, f_recv), refs = refs[:3], refs[3:]
+    else:
+        (m_o, sq_o, hid_o), refs = refs[:3], refs[3:]
+    (sq_land, sq_send, sq_recv, parts, bufs, landed, c_send, c_recv) = refs
     d = lax.axis_index("dp")
     z = lax.axis_index("tensor")
     rows = tok.shape[0]
-    greet(other_quarters(d, z, nt))
+    peers = [(p, z) for p in cube_peers(d)] if feed else []
+    greet(peers + other_quarters(d, z, nt))
     squares = Exchange(sq, sq_land, sq_send, sq_recv, d, z, nt)
     squares.start()
+    n = 2 * (nt - 1)
+    if feed:
+        items = []
+        for k in range(1, nt):
+            q = lax.rem(z - k + nt, nt)
+            items.append((turned[2 * k - 2], lambda s, q=q: hid_f.at[s, q]))
+            items.append((turned[2 * k - 1], lambda s, q=q: dwn_f.at[s, q]))
+        cube = CubeGather(items, (0, 3, 4), f_send, f_recv, d, z)
+        for i in range(n):
+            cube.start(i)
+        locals_ = []
+        for i, (src, dst) in enumerate([(src, at(d)) for src, at in items]):
+            locals_.append(pltpu.make_async_copy(src, dst, lsem.at[i]))
+            locals_[-1].start()
     chain = ChainScatter(parts, bufs, landed, c_send, c_recv, d, z, nt)
     squares.wait()
     sq_o[...] = squares.total()
@@ -1105,32 +1150,56 @@
         return carry
 
     lax.fori_loop(0, nt - 1, rest, 0)
+    if feed:
+        cube.near(0)
+        cube.near(1)
     for t in range(1, nt - 1):
         chain.step(t)
+        if feed:
+            cube.near(2 * t)
+            cube.near(2 * t + 1)
+            cube.far(2 * t - 2)
+            cube.far(2 * t - 1)
+    if feed:
+        cube.far(n - 2)
+        cube.far(n - 1)
     chain.finish(hid_o)
     hid_o[...] += tok[...].astype(F32)
     chain.drain()
-
-
-def mix_scatter(channels, nt, o, y, zr, sq, gain, watt, wmam, tok):
+    if feed:
+        cube.finish()
+        for copy in locals_:
+            copy.wait()
+
+
+def mix_scatter(channels, nt, o, y, zr, sq, gain, watt, wmam, tok, feed=()):
     total, inner = y.shape
     rows, width = tok.shape
     dma = pltpu.SemaphoreType.DMA
     sds = jax.ShapeDtypeStruct
     vmem = pl.BlockSpec(memory_space=pltpu.VMEM)
+    anywhere = pl.BlockSpec(memory_space=pl.ANY)
+    outs = [sds((total, inner), BF16), sds((8, total), F32), sds((rows, width), F32)]
+    scratch = []
+    n = 2 * (nt - 1)
+    if feed:
+        for v in feed[:2]:
+            outs.append(sds(v.shape, BF16))
+        scratch = [dma((n,)), dma((n, 7)), dma((n, 7))]
     return pl.pallas_call(
-        partial(mix_scatter_kernel, channels, nt),
-        in_specs=[vmem] * 8,
-        out_specs=[vmem] * 3,
-        out_shape=[sds((total, inner), BF16), sds((8, total), F32), sds((rows, width), F32)],
-        scratch_shapes=[pltpu.VMEM((nt - 1, 8, total), F32), dma((nt - 1,)), dma((nt - 1,)),
+        partial(mix_scatter_kernel, channels, nt, bool(feed)),
+        in_specs=[vmem] * 8 + [anywhere] * len(feed[:2]) + [vmem] * len(feed[2:]),
+        out_specs=[vmem] * 3 + [anywhere] * (len(outs) - 3),
+        out_shape=outs,
+        input_output_aliases={8: 3, 9: 4} if feed else {},
+        scratch_shapes=scratch + [pltpu.VMEM((nt - 1, 8, total), F32), dma((nt - 1,)), dma((nt - 1,)),
                         pltpu.VMEM((nt, rows, width), BF16)] + chain_scratch(nt, rows, width),
         compiler_params=pltpu.CompilerParams(
             vmem_limit_bytes=VMEM_LIMIT, collective_id=1, has_side_effects=True
         ),
         cost_estimate=pl.CostEstimate(flops=int(1e9), bytes_accessed=int(130e6), transcendentals=int(4e5)),
         name="mix_scatter",
-    )(o, y, zr, sq, gain, watt, wmam, tok)
+    )(o, y, zr, sq, gain, watt, wmam, tok, *feed)
 
 
 class ChainGather:
@@ -1174,17 +1243,32 @@
                 pl.when(self.has(way, dist) & self.goes_on(way))(self.copy(way, dist).wait_send)
 
 
-def unmix_gather_kernel(
-    nt, dmix, y, z_in, gain, watt, wmam,
-    g_o, do_o, dm_o, dot_o,
-    slots, g_send, g_recv, dot_own, dot_land, d_send, d_recv,
-):
+def unmix_gather_kernel(nt, feed, *refs):
+    (dmix, y, z_in, gain, watt, wmam), refs = refs[:6], refs[6:]
+    if feed:
+        pieces, refs = refs[0], refs[1:]
+        (g_o, do_o, dm_o, dot_o, own_o, sum_o), refs = refs[:6], refs[6:]
+        boxes, refs = refs[: 8 * (nt - 1)], refs[8 * (nt - 1) :]
+    else:
+        (g_o, do_o, dm_o, dot_o), refs = refs[:4], refs[4:]
+    (slots, g_send, g_recv, dot_own, dot_land, d_send, d_recv) = refs
     d = lax.axis_index("dp")
     z = lax.axis_index("tensor")
     rows = dmix.shape[0]
-    greet(other_quarters(d, z, nt))
+    bits = dp_bits(d)
+    peers = cube_peers(d)
+    greet(([(p, z) for p in peers[1:]] if feed else []) + other_quarters(d, z, nt))
     chain = ChainGather(dmix, slots, g_send, g_recv, d, z, nt)
     chain.start()
+    cubes = []
+    if feed:
+        for k in range(1, nt):
+            q = lax.rem(z + k, nt)
+            box = boxes[8 * k - 8 : 8 * k]
+            cubes.append(
+                SquareScatter(lambda i, j, q=q: (i, j, q), pieces, box[:6], box[6], box[7], peers, bits, z)
+            )
+            cubes[-1].start()
 
     def work(q, g):
         at = pl.ds(pl.multiple_of(q * rows, rows), rows)
@@ -1198,6 +1282,9 @@
         dot_own[:, at] = jnp.concatenate(turned, axis=1)
 
     work(z, dmix[...])
+    if feed:
+        own_o[...] = pieces[:, :, z]
+        cubes[0].middle()
     for dist in range(1, nt):
         chain.hop(dist)
 
@@ -1211,26 +1298,40 @@
             return carry
 
         lax.fori_loop(0, 2, side, 0)
+        if feed:
+            if dist < nt - 1:
+                cubes[dist].middle()
+            cubes[dist - 1].finish(sum_o.at[dist - 1])
     dots = Exchange(dot_own, dot_land, d_send, d_recv, d, z, nt)
     dots.start()
     chain.drain()
+    for cube in cubes:
+        cube.drain()
     dots.wait()
     dot_o[...] = dots.total()
 
 
-def unmix_gather(nt, dmix, y, zr, gain, watt, wmam):
+def unmix_gather(nt, dmix, y, zr, gain, watt, wmam, pieces=None):
     total, inner = y.shape
     rows, width = dmix.shape
     dma = pltpu.SemaphoreType.DMA
     sds = jax.ShapeDtypeStruct
     vmem = pl.BlockSpec(memory_space=pltpu.VMEM)
+    feed = [] if pieces is None else [pieces]
+    outs = [sds((total, width), BF16), sds((total, 128), BF16), sds((total, inner), F32),
+            sds((8, total), F32)]
+    scratch = []
+    if feed:
+        n, lanes = pieces.shape[3:]
+        outs += [sds((2, 2, n, lanes), BF16), sds((nt - 1, n, lanes), BF16)]
+        for _ in range(nt - 1):
+            scratch += square_scratch(n, lanes)
     return pl.pallas_call(
-        partial(unmix_gather_kernel, nt),
-        in_specs=[vmem] * 6,
-        out_specs=[vmem] * 4,
-        out_shape=[sds((total, width), BF16), sds((total, 128), BF16), sds((total, inner), F32),
-                   sds((8, total), F32)],
-        scratch_shapes=[pltpu.VMEM((nt, rows, width), BF16), dma((2, nt - 1)), dma((2, nt - 1)),
+        partial(unmix_gather_kernel, nt, bool(feed)),
+        in_specs=[vmem] * (6 + len(feed)),
+        out_specs=[vmem] * len(outs),
+        out_shape=outs,
+        scratch_shapes=scratch + [pltpu.VMEM((nt, rows, width), BF16), dma((2, nt - 1)), dma((2, nt - 1)),
                         pltpu.VMEM((8, total), F32), pltpu.VMEM((nt - 1, 8, total), F32),
                         dma((nt - 1,)), dma((nt - 1,))],
         compiler_params=pltpu.CompilerParams(
@@ -1238,80 +1339,119 @@
         ),
         cost_estimate=pl.CostEstimate(flops=int(1e9), bytes_accessed=int(130e6), transcendentals=int(4e5)),
         name="unmix_gather",
-    )(dmix, y, zr, gain, watt, wmam)
+    )(dmix, y, zr, gain, watt, wmam, *feed)
 
 
 def add_refs(left, right):
     return left.astype(F32) + right.astype(F32)
 
 
-class CubeScatter:
-    def __init__(self, pieces, bufs, send, recv, peers, bits, z):
-        (self.rc, self.held, self.r1, self.r2, self.ob, self.tb, self.r3, self.r4) = bufs
-        self.p = pieces
-        self.half = pieces.shape[3] // 2
-        self.core, self.x, self.y = bits
-        d_core, d_x, d_y = peers
-        half = self.half
-        n = pieces.shape[3]
-        core, x, y = bits
-        lo, hi = pl.ds(0, half), pl.ds(half, n - half)
-        mk = remote_copy
-        self.c0 = mk(pieces.at[:, :, 1 - core], self.rc, send.at[0], recv.at[0], (d_core, z))
-        self.c1 = mk(self.held.at[:, 1 - x, lo], self.r1, send.at[1], recv.at[1], (d_x, z))
-        self.c2 = mk(self.held.at[1 - y, :, hi], self.r2, send.at[2], recv.at[2], (d_y, z))
-        self.c3 = mk(self.ob.at[1 - y], self.r3, send.at[3], recv.at[3], (d_y, z))
-        self.c4 = mk(self.tb.at[1 - x], self.r4, send.at[4], recv.at[4], (d_x, z))
+class SquareScatter:
+    def __init__(self, place, held, bufs, send, recv, peers, bits, z):
+        (self.r1, self.r2, self.ob, self.tb, self.r3, self.r4) = bufs
+        self.place, self.held = place, held
+        n = held.shape[-2]
+        half = n // 2
+        self.lo, self.hi = pl.ds(0, half), pl.ds(half, n - half)
+        self.half = half
+        _, self.x, self.y = bits
+        x, y = self.x, self.y
+        _, d_x, d_y = peers
+        self.copies = []
+        for i in range(2):
+            self.copies.append(
+                remote_copy(held.at[place(i, 1 - x) + (self.lo,)], self.r1.at[i], send.at[i], recv.at[i],
+                            (d_x, z))
+            )
+        for j in range(2):
+            self.copies.append(
+                remote_copy(held.at[place(1 - y, j) + (self.hi,)], self.r2.at[j], send.at[2 + j],
+                            recv.at[2 + j], (d_y, z))
+            )
+        self.copies.append(remote_copy(self.ob.at[1 - y], self.r3, send.at[4], recv.at[4], (d_y, z)))
+        self.copies.append(remote_copy(self.tb.at[1 - x], self.r4, send.at[5], recv.at[5], (d_x, z)))
 
     def start(self):
-        self.c0.start()
+        for copy in self.copies[:4]:
+            copy.start()
 
     def middle(self):
-        self.c0.wait_recv()
         for i in range(2):
-            for j in range(2):
-                self.held[i, j] = add_refs(self.p[i, j, self.core], self.rc[i, j]).astype(BF16)
-        self.c1.start()
-        self.c2.start()
-
-    def last(self):
-        half = self.half
-        self.c1.wait_recv()
-        for i in range(2):
-            self.ob[i] = add_refs(self.held[i, self.x, 0:half], self.r1[i]).astype(BF16)
-        self.c3.start()
-        self.c2.wait_recv()
-        for i in range(2):
-            self.tb[i] = add_refs(self.held[self.y, i, half:], self.r2[i]).astype(BF16)
-        self.c4.start()
+            self.copies[i].wait_recv()
+            self.ob[i] = add_refs(self.held[self.place(i, self.x) + (self.lo,)], self.r1[i]).astype(BF16)
+        self.copies[4].start()
+        for j in range(2):
+            self.copies[2 + j].wait_recv()
+            self.tb[j] = add_refs(self.held[self.place(self.y, j) + (self.hi,)], self.r2[j]).astype(BF16)
+        self.copies[5].start()
 
     def finish(self, out):
-        half = self.half
-        self.c3.wait_recv()
-        out[0:half] = add_refs(self.ob[self.y], self.r3[...]).astype(out.dtype)
-        self.c4.wait_recv()
-        out[half:] = add_refs(self.tb[self.x], self.r4[...]).astype(out.dtype)
+        self.copies[4].wait_recv()
+        out[0 : self.half] = add_refs(self.ob[self.y], self.r3[...]).astype(out.dtype)
+        self.copies[5].wait_recv()
+        out[self.half :] = add_refs(self.tb[self.x], self.r4[...]).astype(out.dtype)
 
     def drain(self):
-        for copy in (self.c0, self.c1, self.c2, self.c3, self.c4):
+        for copy in self.copies:
             copy.wait_send()
 
 
-def cube_scratch(n, lanes):
+def square_scratch(n, lanes):
     dma = pltpu.SemaphoreType.DMA
     half = n // 2
     return [
-        pltpu.VMEM((2, 2, n, lanes), BF16),
-        pltpu.VMEM((2, 2, n, lanes), BF16),
         pltpu.VMEM((2, half, lanes), BF16),
         pltpu.VMEM((2, n - half, lanes), BF16),
         pltpu.VMEM((2, half, lanes), BF16),
         pltpu.VMEM((2, n - half, lanes), BF16),
         pltpu.VMEM((half, lanes), BF16),
         pltpu.VMEM((n - half, lanes), BF16),
-        dma((5,)),
-        dma((5,)),
+        dma((6,)),
+        dma((6,)),
     ]
+
+
+class CubeScatter:
+    def __init__(self, pieces, bufs, peers, bits, z):
+        (self.rc, self.held, send, recv) = bufs[:4]
+        self.p = pieces
+        self.core = bits[0]
+        self.first = remote_copy(
+            pieces.at[:, :, 1 - self.core], self.rc, send.at[0], recv.at[0], (peers[0], z)
+        )
+        self.square = SquareScatter(
+            lambda i, j: (i, j), self.held, bufs[4:10], bufs[10], bufs[11], peers, bits, z
+        )
+
+    def start(self):
+        self.first.start()
+
+    def middle(self):
+        self.first.wait_recv()
+        for i in range(2):
+            for j in range(2):
+                self.held[i, j] = add_refs(self.p[i, j, self.core], self.rc[i, j]).astype(BF16)
+        self.square.start()
+
+    def last(self):
+        self.square.middle()
+
+    def finish(self, out):
+        self.square.finish(out)
+
+    def drain(self):
+        self.first.wait_send()
+        self.square.drain()
+
+
+def cube_scratch(n, lanes):
+    dma = pltpu.SemaphoreType.DMA
+    return [
+        pltpu.VMEM((2, 2, n, lanes), BF16),
+        pltpu.VMEM((2, 2, n, lanes), BF16),
+        dma((1,)),
+        dma((1,)),
+    ] + square_scratch(n, lanes)
 
 
 class CubeTotal:
@@ -1345,25 +1485,28 @@
 
 
 def tail_kernel(
-    nt, n_all, parts, tok, gain, dh, pieces, shared, small,
-    gt_o, mix_o, sh_o, small_o, norm_o,
-    da, bufs, landed, c_send, c_recv, *rest,
+    nt, n_all, parts, tok, gain, dh, pieces, shared, small, feed_own, feed_rest,
+    gt_o, que_o, att_o, inn_o, mam_o, hid_o, dwn_o, sh_o, small_o, norm_o,
+    da, mixed, fed, bufs, landed, c_send, c_recv, *rest,
 ):
-    cube_a, rest = rest[:10], rest[10:]
-    cube_b, rest = rest[:10], rest[10:]
+    cube_a, rest = rest[:12], rest[12:]
+    cube_b, rest = rest[:12], rest[12:]
+    square_c, rest = rest[:8], rest[8:]
     (sh_sum, sh_land, sh_send, sh_recv) = rest[:4]
     (sm_held, sm_land, sm_send, sm_recv, all_own, all_land, all_send, all_recv) = rest[4:12]
     (ng_held, ng_land, ng_send, ng_recv, ngz_land, ngz_send, ngz_recv) = rest[12:]
     d = lax.axis_index("dp")
     z = lax.axis_index("tensor")
     bits = dp_bits(d)
-    core, x, y = bits
-    peers = (d + 1 - 2 * core, d + 2 - 4 * x, d + 4 - 8 * y)
+    peers = cube_peers(d)
     greet([(p, z) for p in peers] + other_quarters(d, z, nt))
     chain = ChainScatter(parts, bufs, landed, c_send, c_recv, d, z, nt)
     chain.step(0)
-    one = CubeScatter(pieces, cube_a[:8], cube_a[8], cube_a[9], peers, bits, z)
-    two = CubeScatter(shared, cube_b[:8], cube_b[8], cube_b[9], peers, bits, z)
+    one = CubeScatter(pieces, cube_a, peers, bits, z)
+    two = CubeScatter(shared, cube_b, peers, bits, z)
+    three = SquareScatter(
+        lambda i, j: (i, j), feed_own, square_c[:6], square_c[6], square_c[7], peers, bits, z
+    )
     sums = CubeTotal(sm_held, sm_land, sm_send, sm_recv, peers, z)
     sm_held[0] = small[...]
     sums.start(0)
@@ -1373,6 +1516,7 @@
     sums.start(1)
     two.middle()
     one.middle()
+    three.start()
     sums.take(1)
     sums.start(2)
     chain.step(1)
@@ -1392,9 +1536,32 @@
             remote_copy(sh_sum.at[rows], sh_land.at[k - 1], sh_send.at[k - 1], sh_recv.at[k - 1], (d, q))
         )
         copies[-1].start()
+    three.middle()
     for t in range(2, nt - 1):
         chain.step(t)
-    one.finish(mix_o)
+    one.finish(mixed)
+    block = que_o.shape[0]
+    inner = mam_o.shape[0]
+    first = 0
+    for j in range(que_o.shape[1] // 128):
+        que_o[:, 128 * j : 128 * j + 128] = mixed[first : first + block]
+        first += block
+    att_o[...] = mixed[first : first + att_o.shape[0]]
+    first += att_o.shape[0]
+    for i in range(2):
+        for j in range(inner // 128):
+            inn_o[i, :, 128 * j : 128 * j + 128] = mixed[first : first + block]
+            first += block
+    mam_o[...] = mixed[first : first + inner]
+    three.finish(fed)
+    for k in range(nt - 1):
+        fed[...] += feed_rest[k].astype(F32)
+    first = 0
+    for i in range(2):
+        for j in range(hid_o.shape[2] // 128):
+            hid_o[i, :, 128 * j : 128 * j + 128] = fed[first : first + block]
+            first += block
+    dwn_o[...] = fed[first:]
     small_o[...] = sm_held[3]
     over_all.wait()
     small_o[0:n_all, :] = over_all.total()
@@ -1419,11 +1586,11 @@
     last.start()
     last.wait()
     norm_o[...] = last.total()
-    for thing in (chain, one, two, sums, norms):
+    for thing in (chain, one, two, three, sums, norms):
         thing.drain()
 
 
-def tail(nt, n_all, parts, tok, gain, dh, pieces, shared, small):
+def tail(nt, n_all, parts, tok, gain, dh, pieces, shared, small, feed_own, feed_rest, shapes):
     rows, width = tok.shape
     n, lanes = pieces.shape[1:]
     s_rows, s_lanes = shared.shape[1:]
@@ -1435,12 +1602,13 @@
     shared = shared.reshape(2, 2, 2, s_rows, s_lanes)
     return pl.pallas_call(
         partial(tail_kernel, nt, n_all),
-        in_specs=[vmem] * 7,
-        out_specs=[vmem] * 5,
-        out_shape=[sds((rows, width), BF16), sds((n, lanes), F32), sds((s_rows // nt, s_lanes), F32),
-                   sds((m_rows, 128), F32), sds((8, 128), F32)],
-        scratch_shapes=[pltpu.VMEM((rows, width), F32)] + chain_scratch(nt, rows, width)
-        + cube_scratch(n, lanes) + cube_scratch(s_rows, s_lanes)
+        in_specs=[vmem] * 9,
+        out_specs=[vmem] * (4 + len(shapes)),
+        out_shape=[sds((rows, width), BF16)] + [sds(s, F32) for s in shapes]
+        + [sds((s_rows // nt, s_lanes), F32), sds((m_rows, 128), F32), sds((8, 128), F32)],
+        scratch_shapes=[pltpu.VMEM((rows, width), F32), pltpu.VMEM((n, lanes), F32),
+                        pltpu.VMEM(feed_own.shape[2:], F32)] + chain_scratch(nt, rows, width)
+        + cube_scratch(n, lanes) + cube_scratch(s_rows, s_lanes) + square_scratch(*feed_own.shape[2:])
         + [pltpu.VMEM((s_rows, s_lanes), BF16), pltpu.VMEM((nt - 1, s_rows // nt, s_lanes), BF16),
            dma((nt - 1,)), dma((nt - 1,)),
            pltpu.VMEM((4, m_rows, 128), F32), pltpu.VMEM((3, m_rows, 128), F32), dma((3,)), dma((3,)),
@@ -1453,7 +1621,7 @@
         ),
         cost_estimate=pl.CostEstimate(flops=int(1e7), bytes_accessed=int(150e6), transcendentals=0),
         name="tail",
-    )(parts, tok, gain, dh, pieces, shared, small)
+    )(parts, tok, gain, dh, pieces, shared, small, feed_own, feed_rest)
 
 
 def rope_wide(length):
@@ -1508,21 +1676,21 @@
     flat = jnp.concatenate([p.reshape(-1) for p in small_parts])
     small_len = -(-flat.shape[0] // 2048) * 2048
     small = jnp.pad(flat, (0, small_len - flat.shape[0])).reshape(-1, 128)
-    (tok_full, full_query, full_attend, full_inner, full_mamba, sha, sma) = gather_start(
-        tokens, query_proj, attend_out, inner_proj, mamba_out, shared_proj, small, nd, nt
+    (tok_full, full_query, full_attend, full_inner, full_mamba, hid_own, down_own, sha, sma) = gather_start(
+        tokens, query_proj, attend_out, inner_proj, mamba_out, hidden_proj, down_proj, shared_proj, small,
+        nd, nt,
     )
-    hid_in, down_in = hidden_proj, down_proj
+    feed = ()
     if nd == 8:
-        full_hidden = lax.all_gather(hid_in, ("dp", "tensor"), axis=0).reshape(
-            (nd, nt) + hidden_proj.shape
-        )
-        full_down = lax.all_gather(down_in, ("dp", "tensor"), axis=0).reshape(
-            (nd, nt) + down_proj.shape
-        )
+        hid_in, down_in, tok_full = lax.optimization_barrier((hidden_proj, down_proj, tok_full))
+        feed = [hid_own, down_own]
+        for k in range(1, nt):
+            ring = [(i, (i + k) % nt) for i in range(nt)]
+            feed += [lax.ppermute(hid_in, "tensor", ring), lax.ppermute(down_in, "tensor", ring)]
     else:
-        full_hidden = lax.all_gather(hid_in, "tensor", axis=2, tiled=True)
+        full_hidden = lax.all_gather(hidden_proj, "tensor", axis=2, tiled=True)
         full_hidden = to_blocks(lax.all_gather(full_hidden, "dp", axis=1, tiled=True), 1, nt)
-        full_down = lax.all_gather(down_in, "tensor", axis=0, tiled=True)
+        full_down = lax.all_gather(down_proj, "tensor", axis=0, tiled=True)
         full_down = to_blocks(lax.all_gather(full_down, "dp", axis=1, tiled=True), 0, nt)
 
     full_shared = sha.reshape(width, -1)
@@ -1559,22 +1727,33 @@
         heads, kv_head, tok_full.reshape(group_rows, width), gain_first, full_query, full_inner, step_rows,
         full_shared, cosine, sine, taps_x, taps_b, decay, bias, skip,
     )
-    m, squares, hidden = mix_scatter(
-        channels, nt, o, y, zr, squares, gain_mix, full_attend, full_mamba, tokens
+    mixed = mix_scatter(
+        channels, nt, o, y, zr, squares, gain_mix, full_attend, full_mamba, tokens, tuple(feed)
     )
-    layer_out, dh, dmix, grad_gain_two, hid_pieces, down_pieces = feed_forward(
-        hidden, gain_second, cotangent, full_hidden, full_down
+    m, squares, hidden = mixed[:3]
+    if nd == 8:
+        full_hidden, full_down = mixed[3:]
+    layer_out, dh, dmix, grad_gain_two, feed_pieces = feed_forward(
+        nd == 8, hidden, gain_second, cotangent, full_hidden, full_down
     )
-    grad_mix, do, dm, dots = unmix_gather(nt, dmix, y, zr, gain_mix, full_attend, full_mamba)
     if nd == 8:
-        hid_sum = cube_scatter(hid_pieces, nd, BF16)
-        down_sum = cube_scatter(down_pieces, nd, BF16)
-        gradient_hidden = chain_scatter(hid_sum, nt)
-        gradient_down = chain_scatter(down_sum, nt)
+        feed_pieces = feed_pieces.reshape((2, 2) + feed_pieces.shape[1:])
+        grad_mix, do, dm, dots, feed_own, feed_sums = unmix_gather(
+            nt, dmix, y, zr, gain_mix, full_attend, full_mamba, feed_pieces
+        )
+        feed_rest = jnp.stack(
+            [
+                lax.ppermute(feed_sums[k - 1], "tensor", [(i, (i + k) % nt) for i in range(nt)])
+                for k in range(1, nt)
+            ]
+        )
     else:
-        hid_full = hid_pieces.transpose(2, 0, 3, 1, 4).reshape(2, nd, width // nd, nt, units)
+        grad_mix, do, dm, dots = unmix_gather(nt, dmix, y, zr, gain_mix, full_attend, full_mamba)
+        hid_full = feed_pieces[:, :, : 2 * units].reshape(8, nt, 2, units // 128, width // 8, 128)
+        hid_full = hid_full.transpose(2, 0, 4, 1, 3, 5).reshape(2, nd, width // nd, nt, units)
         hid_sum = cube_scatter(hid_full.transpose(1, 3, 0, 2, 4), nd, BF16)
-        down_full = down_pieces.transpose(1, 2, 0, 3).reshape(nt, units, nd, width // nd)
+        down_full = feed_pieces[:, :, 2 * units :].transpose(1, 2, 0, 3)
+        down_full = down_full.reshape(nt, units, nd, width // nd)
         down_sum = cube_scatter(down_full.transpose(2, 0, 1, 3), nd, BF16)
         gradient_hidden = chain_scatter(hid_sum, nt)
         gradient_down = chain_scatter(down_sum, nt)
@@ -1618,19 +1797,26 @@
     small_sums = jnp.concatenate([rows_all, in_rows(over_dp)], axis=0)
     parts = part_one.reshape(nt, local_rows, width)
     if nd == 8:
-        gradient_tokens, mixer_sum, gradient_shared, small_sums, grad_gain_one = tail(
-            nt, n_all, parts, tokens, gain_first, dh, pieces, shared_pieces, small_sums
+        shapes = [
+            query_proj.shape, attend_out.shape, inner_proj.shape, mamba_out.shape, hidden_proj.shape,
+            down_proj.shape,
+        ]
+        (
+            gradient_tokens,
+            gradient_query,
+            gradient_attend,
+            gradient_inner,
+            gradient_mamba,
+            gradient_hidden,
+            gradient_down,
+            gradient_shared,
+            small_sums,
+            grad_gain_one,
+        ) = tail(
+            nt, n_all, parts, tokens, gain_first, dh, pieces, shared_pieces, small_sums, feed_own, feed_rest,
+            shapes,
         )
         grad_gain_one = grad_gain_one.reshape(1, width)
-        got = [mixer_sum[cuts[i] : cuts[i + 1]] for i in range(5)]
-
-        def back_rows(values):
-            return values.reshape(-1, 128, 128).transpose(1, 0, 2).reshape(128, -1)
-
-        gradient_query = back_rows(got[0])
-        gradient_attend = got[1]
-        gradient_inner = jnp.stack([back_rows(got[2]), back_rows(got[3])])
-        gradient_mamba = got[4]
     else:
         token_f32 = tokens.astype(F32)
         _, norm_one_back = jax.vjp(norm_apply, token_f32, gain_first[0])

time: 488 us -> 386 us (0.79); the launches traced: 478 us -> 385 us
  waiting for transfers between devices: 41.9 us -> 21.2 us
  Pallas kernels: 338 us -> 318 us
  starting transfers between devices: 30.6 us -> 11 us
  between operations: 15.2 us -> 1.13 us
  other arithmetic: 16 us -> 5.26 us
  local copies, waits for them, and re-layouts: 36.7 us -> 29 us
    ppermute x22 -> x9, starting transfers between devices: 30.5 us -> 11 us  [the longest x3 4.43 us: per_device(): lax.ppermute(hid_in, 'tensor', ring)]
    ppermute x22 -> x9, waiting for transfers between devices: 40.5 us -> 21.2 us  [the longest x3 21.2 us: per_device(): lax.ppermute(feed_sums[k - 1], 'tensor', [(i, (i + k) % nt) for i in rang...]
    pallas_call x1, Pallas kernels: 61.4 us -> 47.4 us  [gather_start(): pl.pallas_call(partial(gather_kernel, nt), out_shape=[jax.ShapeDtypeStruc...]
    convert_element_type x10 -> x0, other arithmetic: 9.66 us -> none  [add_low(): (left.astype(jnp.float32) + right.astype(jnp.float32)).astype(jnp.bfloat16)]
    squeeze x10 -> x1, local copies, waits for them, and re-layouts: 8.1 us -> 0.08 us  [per_device(): feed_sums[k - 1]]
    pallas_call x4, Pallas kernels: 203 us -> 197 us  [the longest x1 59.9 us: unmix_gather(): pl.pallas_call(partial(unmix_gather_kernel, nt, bool(feed)), in_specs=[vm...]
    unnamed x26 -> x56, local copies, waits for them, and re-layouts: 2.4 us -> 7.38 us
  transfers between devices with their start and end apart: 24 -> 9, of which waited for: 6 -> 3; matrix products, arithmetic and copies ran while one was open for 10% -> 2% of each run, Pallas kernels for 66% -> 8%
where the time goes in v4:
time: 386 us; the launch traced here: 385 us
  Pallas kernels  318 us (82%)
  local copies, waits for them, and re-layouts  29 us (8%)
  waiting for transfers between devices  21.2 us (5%)
  starting transfers between devices  11 us (3%)
  other arithmetic  5.26 us (1%)
    pallas_call x1, Pallas kernels, unmix_gather(): pl.pallas_call(partial(unmix_gather_kernel, nt, bool(feed)), in_specs=[vm...  59.9 us
    pallas_call x1, Pallas kernels, tail(): pl.pallas_call(partial(tail_kernel, nt, n_all), in_specs=[vmem] * 9, out_...  59.2 us
    pallas_call x1, Pallas kernels, mix_scatter(): pl.pallas_call(partial(mix_scatter_kernel, channels, nt, bool(feed)), in_...  52.3 us
    pallas_call x1, Pallas kernels, gather_start(): pl.pallas_call(partial(gather_kernel, nt), out_shape=[jax.ShapeDtypeStruc...  47.4 us
    pallas_call x1, Pallas kernels, feed_forward(): pl.pallas_call(partial(feed_kernel, paired), grid=(nt * per,), in_specs=[...  25.5 us
    pallas_call x1, Pallas kernels, scan_back(): pl.pallas_call(partial(scan_back_kernel, heads, channels), grid=(steps,),...  23.2 us
    pallas_call x1, Pallas kernels, mixers_forward(): pl.pallas_call(partial(forward_kernel, heads), grid=(total // rows,), in_...  23 us
    ppermute x3, waiting for transfers between devices, per_device(): lax.ppermute(feed_sums[k - 1], 'tensor', [(i, (i + k) % nt) for i in rang...  21.2 us
  transfers between devices with their start and end apart: 9, of which 3 were waited for; matrix products, arithmetic and copies ran while one was open for 2% of the time, Pallas kernels for 8%

profile of v4, /device:TPU:0, one launch (start us, length us, event | category | flops | bytes accessed | tf_op | source)
XLA Modules:
  0.0 385.4 jit_solution(15710014588958610134)
XLA Ops:
  0.7 0.8 reshape.173
  1.5 0.8 reshape.174
  2.3 0.7 reshape.175
  3.0 0.8 reshape.176
  3.8 0.8 concatenate.15
  4.5 0.6 pad_bitcast_fusion.1.refs_8_
  5.1 47.4 %gather_start.1 = (bf16[4,256,1024]{2,1,0:T(8,128)(2,1)}, bf16[1024,128]{1,0:T(8,128)(2,1)}, bf16[128,1024]{1,0:T(8,128)(2,1)}, bf16[2,1024,384]{2,1,0:T(8,128)(...) custom-call(bf16[256,1024]{1,0:T(8,128)(2,1)} %tok.1, ...), custom_call_target="tpu_custom_call" | custom-call | tf_op jit(solution)/shard_map/gather_start/pallas_call | solution.py:205
  52.5 1.6 collective-permute-start.5
  54.6 0.6 collective-permute-start.1
  55.2 3.3 collective-permute-start.4
  58.4 0.6 collective-permute-start.2
  59.0 0.9 reshape.180
  60.8 0.6 pad_convert_fusion.1.tapb
  61.8 0.7 broadcast_in_dim_reshape.3.skip
  62.4 0.7 slice.100.gain
  63.3 0.6 pad.42.stp
  63.9 0.6 pad_convert_fusion.tapx
  64.5 0.6 collective-permute-start
  65.1 0.7 pad.51.bias
  65.7 0.7 pad.48.decay
  66.4 23.0 %mixers_forward.1 = (bf16[1024,1024]{1,0:T(8,128)(2,1)}, bf16[1024,128]{1,0:T(8,128)(2,1)}, bf16[1024,128]{1,0:T(8,128)(2,1)}, bf16[1024,128]{1,0:T(8,128)(2,1)}...) custom-call(s32[1]{0:T(128)} %bitcast.kvh, ...), custom_call_target="tpu_custom_call" | custom-call | flops 5000000000 | bytes 15000000 | tf_op jit(solution)/shard_map/mixers_forward/pallas_call | solution.py:457
  89.6 0.7 slice.106.gain
  90.4 0.7 reshape.202.refs_4_.refs_3_.gain
  91.1 0.6 copy-done.12
  92.0 52.3 %mix_scatter.1 = (bf16[1024,384]{1,0:T(8,128)(2,1)}, f32[8,1024]{1,0:T(8,128)}, f32[256,1024]{1,0:T(8,128)}, bf16[8,4,2,128,512]{4,3,2,1,0:T(8,128)(2,1)}, bf16[8,4,512,128]{3,2,1,0:T(8,128)(2,1)}) custom-call(bf16[1024,128]{1,0:T(8,128)(2,1)} %get-tuple-element.87.refs_0_.o, ...), custom_call_target="tpu_custom_call", output_to_operand_aliasing={{3}: (8, {}), {4}: (9, {})} | custom-call | flops 1000000000 | bytes 130000000 | tf_op jit(solution)/shard_map/mix_scatter/pallas_call | solution.py:1189
  144.3 25.5 %feed_forward.1 = (bf16[256,1024]{1,0:T(8,128)(2,1)}, f32[256,1024]{1,0:T(8,128)}, bf16[256,1024]{1,0:T(8,128)(2,1)}, f32[1,1024]{1,0:T(1,128)}, bf16[4,4,1536,128]{3,2,1,0:T(8,128)(2,1)}) custom-call(f32[256,1024]{1,0:T(8,128)} %get-tuple-element.97.hid, f32[1,1024]{1,0:T(1,128)} %slice.106.gain, bf16[256,1024]{1,0:T(8,128)(2,1)} %cot.1, ...), custom_call_target="tpu_custom_call" | custom-call | flops 10000000000 | bytes 26000000 | tf_op jit(solution)/shard_map/feed_forward/pallas_call | solution.py:888
  169.8 59.9 %unmix_gather.1 = (bf16[1024,1024]{1,0:T(8,128)(2,1)}, bf16[1024,128]{1,0:T(8,128)(2,1)}, f32[1024,384]{1,0:T(8,128)}, f32[8,1024]{1,0:T(8,128)}, bf16[2,2,1536,...) custom-call(bf16[256,1024]{1,0:T(8,128)(2,1)} %get-tuple-element.105.refs_0_, ...), custom_call_target="tpu_custom_call" | custom-call | flops 1000000000 | bytes 130000000 | tf_op jit(solution)/shard_map/unmix_gather/pallas_call | solution.py:1329
  229.7 23.2 %scan_back.1 = (bf16[1024,384]{1,0:T(8,128)(2,1)}, bf16[1024,384]{1,0:T(8,128)(2,1)}, bf16[1024,256]{1,0:T(8,128)(2,1)}, f32[8,1024]{1,0:T(8,128)}, f32[8,384]{1...) custom-call(f32[1024,384]{1,0:T(8,128)} %get-tuple-element.109.dm, ...), custom_call_target="tpu_custom_call" | custom-call | flops 4000000000 | bytes 15000000 | tf_op jit(solution)/shard_map/scan_back/pallas_call | solution.py:729
  252.9 0.7 reshape.191
  253.6 0.7 reshape.193
  254.3 0.8 slice_reduce_fusion
  255.2 0.8 slice_reduce_fusion.2
  256.2 9.3 %attend_back.1 = (bf16[1024,128]{1,0:T(8,128)(2,1)}, bf16[1024,256]{1,0:T(8,128)(2,1)}) custom-call(s32[1]{0:T(128)} %bitcast.kvh, bf16[1024,128]{1,0:T(8,128)(2,1)} %get-tuple-element.101.q, bf16[1024,128]{1,0:T(8,128)(2,1)} %get-tuple-element.102.k2, bf16[1024,128]{1,0:T(8,128)(2,1)} %get-tuple-element.103.v2, f32[8,1024]{1,0:T(8,128)} %get-tuple-element.104.lse, ...), custom_call_target="tpu_custom_call" | custom-call | flops 2000000000 | bytes 3000000 | tf_op jit(solution)/shard_map/attend_back/pallas_call | solution.py:541
  265.5 9.8 %weight_pieces.1 = (bf16[8,1408,128]{2,1,0:T(8,128)(2,1)}, bf16[8,128,512]{2,1,0:T(8,128)(2,1)}, f32[8,1024]{1,0:T(8,128)}) custom-call(bf16[1024,1024]{1,0:T(8,128)(2,1)} %get-tuple-element.122.a1, bf16[1024,128]{1,0:T(8,128)(2,1)} %get-tuple-element.108.dq, bf16[1024,384]{1,0:T(8,128)(2,1)} %get-tuple-element.116.dz, ...), custom_call_target="tpu_custom_call" | custom-call | flops 4000000000 | bytes 12000000 | tf_op jit(solution)/shard_map/weight_pieces/pallas_call | solution.py:981
  275.3 0.8 reshape.194
  276.3 1.0 collective-permute-start.6
  277.2 2.9 collective-permute-start.8
  280.2 0.6 pad_maximum_fusion.1.small
  280.8 8.3 %down_parts.1 = bf16[1024,1024]{1,0:T(8,128)(2,1)} custom-call(bf16[1024,128]{1,0:T(8,128)(2,1)} %get-tuple-element.108.dq, bf16[1024,384]{1,0:T(8,128)(2,1)} %get-tuple-element.116.dz, bf16[1024,384]{1,0:T(8,128)(2,1)} %get-tuple-element.117.dx, bf16[1024,256]{1,0:T(8,128)(2,1)} %get-tuple-element.118.dkv, bf16[1024,256]{1,0:T(8,128)(2,1)} %get-tuple-element.119.db, ...), custom_call_target="tpu_custom_call" | custom-call | flops 3000000000 | bytes 8000000 | tf_op jit(solution)/shard_map/down_parts/pallas_call | solution.py:926
  289.1 1.1 collective-permute-done.6
  290.2 4.9 %collective-permute-done.8 = bf16[1536,128]{1,0:T(8,128)(2,1)S(1)} collective-permute-done((bf16[1536,128]{1,0:T(8,128)(2,1)S(1)}, bf16[1536,128]{1,0:T(8,128)(2,1)S(1)}, u32[]{:S(2)}, u32[]{:S(2)}) %collective-permute-start.8) | collective-permute-done | bytes 393248 | tf_op jit(solution)/shard_map/ppermute | solution.py:1746
  295.1 15.2 %collective-permute-done.7 = bf16[1536,128]{1,0:T(8,128)(2,1)S(1)} collective-permute-done((bf16[1536,128]{1,0:T(8,128)(2,1)S(1)}, bf16[1536,128]{1,0:T(8,128)(2,1)S(1)}, u32[]{:S(2)}, u32[]{:S(2)}) %collective-permute-start.7) | collective-permute-done | bytes 393248 | tf_op jit(solution)/shard_map/ppermute | solution.py:1746
  310.3 1.2 pad_maximum_fusion.feed_rest
  311.5 59.2 %tail.1 = (bf16[256,1024]{1,0:T(8,128)(2,1)}, f32[128,128]{1,0:T(8,128)}, f32[128,128]{1,0:T(8,128)}, f32[2,128,384]{2,1,0:T(8,128)}, f32[384,128]{1,0:T(8,128)}...) custom-call(bf16[4,256,1024]{2,1,0:T(8,128)(2,1)} %bitcast.72, ...), custom_call_target="tpu_custom_call" | custom-call | flops 10000000 | bytes 150000000 | tf_op jit(solution)/shard_map/tail/pallas_call | solution.py:1603
  370.7 0.8 slice.121
  371.5 0.7 slice.125
  372.2 0.7 slice.126
  372.9 0.7 slice.120
  373.6 0.8 slice_bitcast_fusion.3
  374.3 0.6 fusion.3
  375.1 0.7 constant_dynamic-slice_fusion.1
  375.8 0.7 constant_dynamic-slice_fusion.2
  376.5 0.7 constant_dynamic-slice_fusion
  377.1 0.6 dynamic-slice_bitcast_fusion
  377.7 1.3 fusion.1
  379.0 0.8 copy.84
  379.8 0.8 copy.85
  380.6 0.6 copy.86
  381.2 0.6 copy.87
  381.9 0.7 copy.88
  382.6 0.7 copy.89
  383.3 0.8 copy.90
  384.1 0.7 copy.91
  384.8 0.6 copy.92
  (92 shorter events, 2.9 us)
Async XLA Ops:
  0.7 59.6 %copy-start.19 = (bf16[6]{0:T(256)(128)(2,1)S(1)}, bf16[6]{0:T(256)(128)(2,1)}, u32[]{:S(2)}) copy-start(bf16[6]{0:T(256)(128)(2,1)} %param.29) | copy-start | bytes 40
  0.7 61.0 %copy-start.20 = (bf16[6]{0:T(256)(128)(2,1)S(1)}, bf16[6]{0:T(256)(128)(2,1)}, u32[]{:S(2)}) copy-start(bf16[6]{0:T(256)(128)(2,1)} %param.30) | copy-start | bytes 40
  0.7 61.0 %copy-start.18 = (bf16[6]{0:T(256)(128)(2,1)S(1)}, bf16[6]{0:T(256)(128)(2,1)}, u32[]{:S(2)}) copy-start(bf16[6]{0:T(256)(128)(2,1)} %param.31) | copy-start | bytes 40
  5.1 59.4 %copy-start.8 = (bf16[2,128,512]{2,1,0:T(8,128)(2,1)S(1)}, bf16[2,128,512]{2,1,0:T(8,128)(2,1)}, u32[]{:S(2)}) copy-start(bf16[2,128,512]{2,1,0:T(8,128)(2,1)} %refs_5_.1) | copy-start | bytes 786436
  52.5 12.0 %collective-permute-start.5 = (bf16[512,128]{1,0:T(8,128)(2,1)}, bf16[512,128]{1,0:T(8,128)(2,1)S(1)}, u32[]{:S(2)}, u32[]{:S(2)}) collective-permute-start(bf16[512,128]{1,0:T(8,128)(2,1)} %refs_6_.1), channel_id=1, source_target_pairs={{0,3},{1,0},{2,1},{3,2},{4,7},{5,4},{6,5},{7,6},{8,11},{9,8},{10,9... | collective-permute-start | bytes 393224 | tf_op jit(solution)/shard_map/ppermute | solution.py:1689
  54.1 37.0 %collective-permute-start.3 = (bf16[512,128]{1,0:T(8,128)(2,1)}, bf16[512,128]{1,0:T(8,128)(2,1)S(1)}, u32[]{:S(2)}, u32[]{:S(2)}) collective-permute-start(bf16[512,128]{1,0:T(8,128)(2,1)} %refs_6_.1), channel_id=1, source_target_pairs={{0,2},{1,3},{2,0},{3,1},{4,6},{5,7},{6,4},{7,5},{8,10},{9,11},{10,... | collective-permute-start | bytes 393224 | tf_op jit(solution)/shard_map/ppermute | solution.py:1689
  54.6 36.5 %collective-permute-start.1 = (bf16[512,128]{1,0:T(8,128)(2,1)}, bf16[512,128]{1,0:T(8,128)(2,1)S(1)}, u32[]{:S(2)}, u32[]{:S(2)}) collective-permute-start(bf16[512,128]{1,0:T(8,128)(2,1)} %refs_6_.1), channel_id=1, source_target_pairs={{0,1},{1,2},{2,3},{3,0},{4,5},{5,6},{6,7},{7,4},{8,9},{9,10},{10,1... | collective-permute-start | bytes 393224 | tf_op jit(solution)/shard_map/ppermute | solution.py:1689
  55.2 35.9 %collective-permute-start.4 = (bf16[2,128,512]{2,1,0:T(8,128)(2,1)}, bf16[2,128,512]{2,1,0:T(8,128)(2,1)S(1)}, u32[]{:S(2)}, u32[]{:S(2)}) collective-permute-start(bf16[2,128,512]{2,1,0:T(8,128)(2,1)} %refs_5_.1), channel_id=1, source_target_pairs={{0,3},{1,0},{2,1},{3,2},{4,7},{5,4},{6,5},{7,6},{8,11},{9,8},{10,9... | collective-permute-start | bytes 786440 | tf_op jit(solution)/shard_map/ppermute | solution.py:1689
  58.4 32.7 %collective-permute-start.2 = (bf16[2,128,512]{2,1,0:T(8,128)(2,1)}, bf16[2,128,512]{2,1,0:T(8,128)(2,1)S(1)}, u32[]{:S(2)}, u32[]{:S(2)}) collective-permute-start(bf16[2,128,512]{2,1,0:T(8,128)(2,1)} %refs_5_.1), channel_id=1, source_target_pairs={{0,2},{1,3},{2,0},{3,1},{4,6},{5,7},{6,4},{7,5},{8,10},{9,11},{10,... | collective-permute-start | bytes 786440 | tf_op jit(solution)/shard_map/ppermute | solution.py:1689
  64.5 24.9 %copy-start.11 = (bf16[512,128]{1,0:T(8,128)(2,1)}, bf16[512,128]{1,0:T(8,128)(2,1)S(1)}, u32[]{:S(2)}) copy-start(bf16[512,128]{1,0:T(8,128)(2,1)S(1)} %collective-permute-done.5.refs_15_) | copy-start | bytes 393220
  64.5 26.6 %collective-permute-start = (bf16[2,128,512]{2,1,0:T(8,128)(2,1)S(1)}, bf16[2,128,512]{2,1,0:T(8,128)(2,1)S(1)}, u32[]{:S(2)}, u32[]{:S(2)}) collective-permute-start(bf16[2,128,512]{2,1,0:T(8,128)(2,1)S(1)} %copy-done.8), channel_id=1, source_target_pairs={{0,1},{1,2},{2,3},{3,0},{4,5},{5,6},{6,7},{7,4},{8,9},{9,10},{10,1... | collective-permute-start | bytes 786440 | tf_op jit(solution)/shard_map/ppermute | solution.py:1689
  91.1 0.6 copy-start.12
  91.1 0.7 copy-start.13
  91.1 0.8 copy-start.5
  91.1 0.8 copy-start.6
  91.1 0.9 copy-start.7
  265.5 10.7 %copy-start = (bf16[3,1536,128]{2,1,0:T(8,128)(2,1)S(1)}, bf16[3,1536,128]{2,1,0:T(8,128)(2,1)}, u32[]{:S(2)}) copy-start(bf16[3,1536,128]{2,1,0:T(8,128)(2,1)} %get-tuple-element.134) | copy-start | bytes 3538948
  275.3 4.9 %copy-start.17 = (f32[1,1024]{1,0:T(1,128)S(1)}, f32[1,1024]{1,0:T(1,128)}, u32[]{:S(2)}) copy-start(f32[1,1024]{1,0:T(1,128)} %get-tuple-element.127) | copy-start | bytes 12292
  276.3 13.9 %collective-permute-start.6 = (bf16[1536,128]{1,0:T(8,128)(2,1)S(1)}, bf16[1536,128]{1,0:T(8,128)(2,1)S(1)}, u32[]{:S(2)}, u32[]{:S(2)}) collective-permute-start(bf16[1536,128]{1,0:T(8,128)(2,1)S(1)} %get-tuple-element.149), channel_id=1, source_target_pairs={{0,1},{1,2},{2,3},{3,0},{4,5},{5,6},{6,7},{7,4},{8,9},{9,10},{10,1... | collective-permute-start | bytes 1179656 | tf_op jit(solution)/shard_map/ppermute | solution.py:1746
  277.2 17.9 %collective-permute-start.8 = (bf16[1536,128]{1,0:T(8,128)(2,1)S(1)}, bf16[1536,128]{1,0:T(8,128)(2,1)S(1)}, u32[]{:S(2)}, u32[]{:S(2)}) collective-permute-start(bf16[1536,128]{1,0:T(8,128)(2,1)S(1)} %get-tuple-element.150), channel_id=1, source_target_pairs={{0,3},{1,0},{2,1},{3,2},{4,7},{5,4},{6,5},{7,6},{8,11},{9,8},{10,9... | collective-permute-start | bytes 1179656 | tf_op jit(solution)/shard_map/ppermute | solution.py:1746
  280.1 30.2 %collective-permute-start.7 = (bf16[1536,128]{1,0:T(8,128)(2,1)S(1)}, bf16[1536,128]{1,0:T(8,128)(2,1)S(1)}, u32[]{:S(2)}, u32[]{:S(2)}) collective-permute-start(bf16[1536,128]{1,0:T(8,128)(2,1)S(1)} %get-tuple-element.151), channel_id=1, source_target_pairs={{0,2},{1,3},{2,0},{3,1},{4,6},{5,7},{6,4},{7,5},{8,10},{9,11},{10,... | collective-permute-start | bytes 1179656 | tf_op jit(solution)/shard_map/ppermute | solution.py:1746
  311.5 67.5 %copy-start.1 = (bf16[256,1024]{1,0:T(8,128)(2,1)S(1)}, bf16[256,1024]{1,0:T(8,128)(2,1)}, u32[]{:S(2)}) copy-start(bf16[256,1024]{1,0:T(8,128)(2,1)} %get-tuple-element.174) | copy-start | bytes 1572868
  370.7 9.1 %copy-start.3 = (bf16[256,1024]{1,0:T(8,128)(2,1)S(1)}, bf16[256,1024]{1,0:T(8,128)(2,1)}, u32[]{:S(2)}) copy-start(bf16[256,1024]{1,0:T(8,128)(2,1)} %get-tuple-element.175) | copy-start | bytes 1572868
  370.7 9.9 %copy-start.16 = (f32[128,128]{1,0:T(8,128)S(1)}, f32[128,128]{1,0:T(8,128)}, u32[]{:S(2)}) copy-start(f32[128,128]{1,0:T(8,128)} %get-tuple-element.176) | copy-start | bytes 196612
  370.7 10.6 %copy-start.15 = (f32[128,128]{1,0:T(8,128)S(1)}, f32[128,128]{1,0:T(8,128)}, u32[]{:S(2)}) copy-start(f32[128,128]{1,0:T(8,128)} %get-tuple-element.177) | copy-start | bytes 196612
  370.7 11.2 %copy-start.4 = (f32[2,128,384]{2,1,0:T(8,128)S(1)}, f32[2,128,384]{2,1,0:T(8,128)}, u32[]{:S(2)}) copy-start(f32[2,128,384]{2,1,0:T(8,128)} %get-tuple-element.178) | copy-start | bytes 1179652
  379.0 3.6 copy-start.10
  379.0 4.3 %copy-start.2 = (f32[2,128,512]{2,1,0:T(8,128)S(1)}, f32[2,128,512]{2,1,0:T(8,128)}, u32[]{:S(2)}) copy-start(f32[2,128,512]{2,1,0:T(8,128)} %get-tuple-element.181) | copy-start | bytes 1572868
  379.8 4.3 %copy-start.9 = (f32[512,128]{1,0:T(8,128)S(1)}, f32[512,128]{1,0:T(8,128)}, u32[]{:S(2)}) copy-start(f32[512,128]{1,0:T(8,128)} %get-tuple-element.182) | copy-start | bytes 786436
  380.6 4.2 %copy-start.14 = (f32[32,512]{1,0:T(8,128)S(1)}, f32[32,512]{1,0:T(8,128)}, u32[]{:S(2)}) copy-start(f32[32,512]{1,0:T(8,128)} %get-tuple-element.188) | copy-start | bytes 196612
